TPU v7x, 256 devices: a whole 4x4x8 slice. The times are simulated.
256 devices in a mesh: grp: 2 (over y_lo), gx: 32 (over z, x), gy: 4 (over y_hi, core).
Axes of the slice: x: 4, y: 4 (y_hi: 2, y_lo: 2; y = y_hi * 2 + y_lo), z: 8, core: 2. Of those that a mesh axis runs over, the one named last changes fastest.
Arguments:
- scalars: float32 [2, 32, 256, 128], P('grp', None, ('gx', 'gy')), may hold values from -9 to 9
- velocity: float32 [3, 32, 256, 128], P(None, None, ('gx', 'gy')), may hold values from -0.15 to 0.15
- w_lift: bfloat16 [64, 54], replicated, may hold values from -0.875 to 0.875
- b_lift: float32 [64], replicated, may hold values from -3 to 3
- w_mix: bfloat16 [64, 1728], replicated, may hold values from -0.15625 to 0.15625
- b_mix: float32 [64], replicated, may hold values from -3 to 3
- w_out: bfloat16 [2, 64], replicated, may hold values from -0.75 to 0.75
- b_out: float32 [2], replicated, may hold values from -3 to 3
Outputs:
- advanced: float32 [2, 32, 256, 128], P('grp', None, ('gx', 'gy'))
- lift_grad: float32 [64, 54], replicated
- liftbias_grad: float32 [64], replicated
- mix_grad: float32 [64, 1728], replicated
- mixbias_grad: float32 [64], replicated
- out_grad: float32 [2, 64], replicated
- outbias_grad: float32 [2], replicated
All inputs are finite; a program needn't handle non-finite values.
Results may differ from a plain program's by a relative error of at most 0.0003.
Values may be sent and summed in bfloat16 or wider, within the bound.
A program may use at most 64 MiB of HBM per device.

v0:
```python
import math

import jax
import jax.numpy as jnp
from jax import lax
from jax.sharding import PartitionSpec as P


def extended(value, sides, width):
    for axis, dim in sides:
        size, length = (lax.axis_size(axis), value.shape[dim])
        up = [(i, (i + 1) % size) for i in range(size - 1)]
        down = [(j, i) for i, j in up]
        last = lax.slice_in_dim(value, length - width, length, axis=dim)
        leading = lax.slice_in_dim(value, 0, width, axis=dim)
        before = lax.ppermute(last, axis, up)
        after = lax.ppermute(leading, axis, down)
        value = jnp.concatenate([before, value, after], axis=dim)
    return value


def stencil(padded, velocity, diffusivity):
    centre = padded[:, 1:-1, 1:-1, 1:-1]
    plus_x = padded[:, 2:, 1:-1, 1:-1]
    minus_x = padded[:, :-2, 1:-1, 1:-1]
    plus_y = padded[:, 1:-1, 2:, 1:-1]
    minus_y = padded[:, 1:-1, :-2, 1:-1]
    plus_z = padded[:, 1:-1, 1:-1, 2:]
    minus_z = padded[:, 1:-1, 1:-1, :-2]
    laplace = plus_x + minus_x + plus_y + minus_y + plus_z + minus_z - 6.0 * centre
    advect = (
        velocity[0] * (plus_x - minus_x)
        + velocity[1] * (plus_y - minus_y)
        + velocity[2] * (plus_z - minus_z)
    )
    return centre + diffusivity * laplace - 0.5 * advect


def advance(tracer, velocity, diffusivity):
    widened = extended(tracer, ((("gx", "gy"), 2),), 1)
    padded = jnp.pad(widened, ((0, 0), (1, 1), (0, 0), (1, 1)))
    return stencil(padded, velocity, diffusivity)


def convolve(padded, kernel):
    result = lax.conv_general_dilated(
        padded[None],
        kernel,
        (1, 1, 1),
        ((0, 0), (0, 0), (1, 1)),
        dimension_numbers=("NCDHW", "OIDHW", "NCDHW"),
        preferred_element_type=jnp.float32,
    )
    return result[0]


def kernel_grad(padded, cotangent):
    deepened = jnp.pad(padded, ((0, 0), (0, 0), (0, 0), (1, 1)))
    size_x, size_y, size_z = (cotangent.shape[1], cotangent.shape[2], cotangent.shape[3])
    cot_rows = cotangent.reshape(cotangent.shape[0], -1)
    pieces = []
    for offset_x in range(3):
        for offset_y in range(3):
            for offset_z in range(3):
                window = deepened[
                    :,
                    offset_x : offset_x + size_x,
                    offset_y : offset_y + size_y,
                    offset_z : offset_z + size_z,
                ]
                window = window.reshape(deepened.shape[0], -1)
                pieces.append(
                    lax.dot_general(
                        cot_rows,
                        window,
                        (((1,), (1,)), ((), ())),
                        preferred_element_type=jnp.float32,
                    )
                )
    stacked = jnp.stack(pieces, axis=-1)
    return stacked.reshape(stacked.shape[0], -1)


def gelu_back(before, cotangent):
    return jax.vjp(jax.nn.gelu, before)[1](cotangent)[0]


def slab_rim(values):
    return extended(values, (("grp", 1), (("gx", "gy"), 2)), 1)


def learn(inputs, targets, w_lift, b_lift, w_mix, b_mix, w_out, b_out, loss_scale, add_rim):
    hidden = w_mix.shape[0]
    lift_kernel = w_lift.reshape(hidden, 2, 3, 3, 3)
    mix_kernel = w_mix.reshape(hidden, hidden, 3, 3, 3)
    net_input = inputs.astype(jnp.bfloat16)
    input_rim = add_rim(net_input)
    lift_pre = convolve(input_rim, lift_kernel) + b_lift[:, None, None, None]
    lifted = jax.nn.gelu(lift_pre).astype(jnp.bfloat16)
    lifted_rim = add_rim(lifted)
    mix_pre = convolve(lifted_rim, mix_kernel) + b_mix[:, None, None, None]
    mixed = jax.nn.gelu(mix_pre).astype(jnp.bfloat16)
    predicted = (
        jnp.einsum("kc,cxyz->kxyz", w_out, mixed, preferred_element_type=jnp.float32)
        + b_out[:, None, None, None]
    )
    error_cot = (loss_scale * (predicted - targets)).astype(jnp.bfloat16)
    out_grad = jnp.einsum("kxyz,cxyz->kc", error_cot, mixed, preferred_element_type=jnp.float32)
    outbias_grad = jnp.sum(error_cot, axis=(1, 2, 3), dtype=jnp.float32)
    mixed_cot = jnp.einsum("kc,kxyz->cxyz", w_out, error_cot, preferred_element_type=jnp.float32)
    mixpre_cot = gelu_back(mix_pre, mixed_cot).astype(jnp.bfloat16)
    mix_grad = kernel_grad(lifted_rim, mixpre_cot)
    mixbias_grad = jnp.sum(mixpre_cot, axis=(1, 2, 3), dtype=jnp.float32)
    flipped = jnp.flip(mix_kernel, (2, 3, 4)).transpose(1, 0, 2, 3, 4)
    lifted_cot = convolve(add_rim(mixpre_cot), flipped)
    liftpre_cot = gelu_back(lift_pre, lifted_cot).astype(jnp.bfloat16)
    lift_grad = kernel_grad(input_rim, liftpre_cot)
    liftbias_grad = jnp.sum(liftpre_cot, axis=(1, 2, 3), dtype=jnp.float32)
    return (lift_grad, liftbias_grad, mix_grad, mixbias_grad, out_grad, outbias_grad)


def on_device(scalars, velocity, w_lift, b_lift, w_mix, b_mix, w_out, b_out):
    diffusivity = jnp.where(lax.axis_index("grp") == 0, jnp.float32(0.08), jnp.float32(0.12))
    stepped = advance(scalars, velocity, diffusivity)
    advanced = advance(stepped, velocity, diffusivity)
    increment = advanced - stepped
    total_cells = scalars.size * lax.axis_size("gx") * lax.axis_size("gy")
    loss_scale = 2.0 / math.sqrt(total_cells)
    inputs, targets = (
        lax.all_to_all(stepped, "grp", split_axis=1, concat_axis=0, tiled=True),
        lax.all_to_all(increment, "grp", split_axis=1, concat_axis=0, tiled=True),
    )
    results = learn(
        inputs, targets, w_lift, b_lift, w_mix, b_mix, w_out, b_out, loss_scale, slab_rim
    )
    lift_grad, liftbias_grad, mix_grad, mixbias_grad, out_grad, outbias_grad = results
    summed = lax.psum(
        (lift_grad, liftbias_grad, mix_grad, mixbias_grad, out_grad, outbias_grad),
        ("grp", "gx", "gy"),
    )
    return (advanced, summed[0], summed[1], summed[2], summed[3], summed[4], summed[5])


def solution(mesh):
    in_specs = (
        P("grp", None, ("gx", "gy"), None),
        P(None, None, ("gx", "gy"), None),
        P(),
        P(),
        P(),
        P(),
        P(),
        P(),
    )
    out_specs = (P("grp", None, ("gx", "gy"), None), P(), P(), P(), P(), P(), P())
    return jax.shard_map(
        on_device, mesh=mesh, in_specs=in_specs, out_specs=out_specs, check_vma=False
    )
```

profile of v0, /device:TPU:1, one launch (start us, length us, event | category | flops | bytes accessed | tf_op | source)
XLA Modules:
  0.0 536.2 jit_solution(6048677606083950281)
XLA Ops:
  8.0 5.1 collective-permute-start.1
  13.2 3.0 collective-permute-start
  19.2 5.2 all_to_all.21
  24.4 1.8 collective-permute-start.4
  27.6 2.9 collective-permute-done.5
  30.5 3.6 collective-permute-start.7
  34.2 7.0 %collective-permute-start.6 = (bf16[2,18,1,128]{3,0,2,1:T(2,128)(2,1)S(1)}, bf16[2,18,1,128]{3,0,2,1:T(2,128)(2,1)S(1)}, u32[]{:S(2)}, u32[]{:S(2)}) collective-permute-start(bf16[2,18,1,128]{3,0,2,1:T(2,128)(2,1)S(1)} %get-tuple-element.53), channel_id=1, source_target_pairs={{0,1},{1,2},{2,3},{3,4},{4,5},{5,6},{6,7},{7,8},{8,9},{9,10},{10,1... | collective-permute-start | bytes 27656 | tf_op jit(solution)/shard_map/ppermute | solution.py:16
  46.5 3.7 convolution_select_fusion
  54.7 4.0 collective-permute-start.8
  58.7 1.9 collective-permute-start.3
  60.6 5.1 collective-permute-start.2
  65.9 1.9 collective-permute-start.11
  67.9 5.1 collective-permute-start.10
  74.2 3.3 all-to-all-start.1
  77.5 2.5 collective-permute-done.10
  80.2 3.6 copy.218
  83.8 2.9 pad.21.clone
  87.7 8.8 %fusion.26 = f32[16,2,8,17,64]{4,2,3,1,0:T(8,128)S(1)} fusion(bf16[64,64,3,3,3]{1,0,4,3,2:T(8,128)(2,1)S(1)} %copy-done.9, bf16[64,18,4,1,7,2]{0,4,5,2,1,3:T(8,128)(2,1)S(1)} %slice.418, bf16[64,18,4,1,8,17]{0,4,5,2,1,3:T(8,128)(2,1)S(1)} %copy.129, pred[8,17]{0,1:T(8,128)(4,1)S(1)} %copy-done.31), kind=kOutput, calls=%fused_computation.44 | convolution fusion | flops 967073792 | bytes 2717832 | tf_op jit(solution)/shard_map/conv_general_dilated | solution.py:46
  98.6 2.5 copy.215
  104.3 2.3 convert_reduce_fusion
  107.8 4.0 collective-permute-start.12
  137.7 1.9 collective-permute-start.15
  139.7 6.5 %collective-permute-start.14 = (bf16[64,18,1,128]{3,0,2,1:T(8,128)(2,1)}, bf16[64,18,1,128]{3,0,2,1:T(8,128)(2,1)S(1)}, u32[]{:S(2)}, u32[]{:S(2)}) collective-permute-start(bf16[64,18,1,128]{3,0,2,1:T(8,128)(2,1)} %get-tuple-element.41), channel_id=1, source_target_pairs={{0,1},{1,2},{2,3},{3,4},{4,5},{5,6},{6,7},{7,8},{8,9},{9,10},{10,1... | collective-permute-start | bytes 884744 | tf_op jit(solution)/shard_map/ppermute | solution.py:16
  147.1 2.1 copy.148
  150.4 1.9 convolution_bitcast_fusion.28
  152.3 268.0 %all-reduce.7.cloned.1.call-done = f32[64,1728]{0,1:T(8,128)} async-done(((f32[64,1728]{0,1:T(8,128)}), f32[64,1728]{0,1:T(8,128)}) %all-reduce.7.cloned.1.call-update) | async-done | bytes 442384 | tf_op jit(solution)/shard_map/psum | solution.py:137
  420.3 2.2 copy.150
  423.8 4.4 copy.219
  431.1 6.6 %fusion.22 = (bf16[16,2,8,17,64]{4,2,3,1,0:T(8,128)(2,1)}, f32[16,2,8,17,64]{4,2,3,1,0:T(8,128)S(1)}) fusion(f32[16,2,8,17,64]{4,2,3,1,0:T(8,128)S(1)} %copy-done.4, f32[64]{0:T(128)S(1)} %copy-done.26, bf16[64,64,3,3,3]{1,0,4,3,2:T(8,128)(2,1)S(1)} %copy-done.10, bf16[64,18,4,1,7,2]{0,4,5,2,1,3:T(8,128)(2,1)S(1)} %slice.424, ...), kind=kOutput, calls=%fused_computation.42 | convolution fusion | flops 972922880 | bytes 4389256 | tf_op jit(solution)/shard_map/conv_general_dilated | solution.py:46
  438.5 2.0 copy.216
  440.5 2.2 convert_reduce_fusion.1
  452.4 76.8 %all-reduce.4 = (f32[64,54]{0,1:T(8,128)}, f32[64]{0:T(128)}, f32[64]{0:T(128)}, f32[2,64]{1,0:T(2,128)}, f32[2]{0:T(128)}) all-reduce(f32[64,54]{0,1:T(8,128)S(1)} %reshape.29, f32[64]{0:T(128)S(1)} %get-tuple-element.33, f32[64]{0:T(128)S(1)} %copy-done.29, ...), channel_id=1, replica_groups=mesh['grp'=2,'gx'=32,'gy'=4] {'grp','gx','gy'}, use_global_device_ids=true, to_apply=%region_0.1 | all-reduce | flops 3714 | bytes 29712 | tf_op jit(solution)/shard_map/psum | solution.py:137
  (198 shorter events, 66.4 us)
Async XLA Ops:
  7.2 95.6 %copy-start = (bf16[2,64]{1,0:T(2,128)(2,1)S(1)}, bf16[2,64]{1,0:T(2,128)(2,1)}, u32[]{:S(2)}) copy-start(bf16[2,64]{1,0:T(2,128)(2,1)} %param.14) | copy-start | bytes 772
  8.0 8.2 %collective-permute-start.1 = (f32[1,32,1,128]{3,2,0,1:T(1,128)S(1)}, f32[1,32,1,128]{3,2,0,1:T(1,128)S(1)}, u32[]{:S(2)}, u32[]{:S(2)}) collective-permute-start(f32[1,32,1,128]{3,2,0,1:T(1,128)S(1)} %get-tuple-element.52), channel_id=1, source_target_pairs={{1,0},{2,1},{3,2},{4,3},{5,4},{6,5},{7,6},{8,7},{9,8},{10,9},{11,1... | collective-permute-start | bytes 49160 | tf_op jit(solution)/shard_map/ppermute | solution.py:17
  13.2 3.8 collective-permute-start
  24.4 17.5 %copy-start.14 = (bf16[1,32,2,128]{3,1,2,0:T(8,128)(2,1)}, bf16[1,32,2,128]{3,1,2,0:T(8,128)(2,1)S(1)}, u32[]{:S(2)}) copy-start(bf16[1,32,2,128]{3,1,2,0:T(8,128)(2,1)S(1)} %copy.227) | copy-start | bytes 49156
  24.4 17.5 %copy-start.12 = (bf16[2,16,2,128]{3,0,2,1:T(2,128)(2,1)}, bf16[2,16,2,128]{3,0,2,1:T(2,128)(2,1)S(1)}, u32[]{:S(2)}) copy-start(bf16[2,16,2,128]{3,0,2,1:T(2,128)(2,1)S(1)} %copy.118) | copy-start | bytes 49156
  24.4 3.1 collective-permute-start.4
  26.2 4.3 collective-permute-start.5
  27.5 14.4 %copy-start.23 = (bf16[2,1,2,128]{3,0,2,1:T(2,128)(2,1)}, bf16[2,1,2,128]{3,0,2,1:T(2,128)(2,1)S(1)}, u32[]{:S(2)}) copy-start(bf16[2,1,2,128]{3,0,2,1:T(2,128)(2,1)S(1)} %collective-permute-done.4) | copy-start | bytes 3076
  27.5 19.0 %copy-start.30 = (pred[8,17]{0,1:T(8,128)(4,1)S(1)}, pred[8,17]{0,1:T(8,128)(4,1)}, u32[]{:S(2)}) copy-start(pred[8,17]{0,1:T(8,128)(4,1)} %constant.57) | copy-start | bytes 412
  30.5 11.4 %copy-start.21 = (bf16[2,1,2,128]{3,0,2,1:T(2,128)(2,1)}, bf16[2,1,2,128]{3,0,2,1:T(2,128)(2,1)S(1)}, u32[]{:S(2)}) copy-start(bf16[2,1,2,128]{3,0,2,1:T(2,128)(2,1)S(1)} %collective-permute-done.5) | copy-start | bytes 3076
  30.5 19.8 %copy-start.7 = (bf16[2,18,2,128]{3,0,2,1:T(2,128)(2,1)}, bf16[2,18,2,128]{3,0,2,1:T(2,128)(2,1)S(1)}, u32[]{:S(2)}) copy-start(bf16[2,18,2,128]{3,0,2,1:T(2,128)(2,1)S(1)} %constant_dynamic-update-slice_fusion) | copy-start | bytes 55300
  30.5 14.2 %collective-permute-start.7 = (bf16[2,18,1,128]{3,0,2,1:T(2,128)(2,1)S(1)}, bf16[2,18,1,128]{3,0,2,1:T(2,128)(2,1)S(1)}, u32[]{:S(2)}, u32[]{:S(2)}) collective-permute-start(bf16[2,18,1,128]{3,0,2,1:T(2,128)(2,1)S(1)} %get-tuple-element.54), channel_id=1, source_target_pairs={{1,0},{2,1},{3,2},{4,3},{5,4},{6,5},{7,6},{8,7},{9,8},{10,9},{11,1... | collective-permute-start | bytes 27656 | tf_op jit(solution)/shard_map/ppermute | solution.py:17
  34.2 10.6 %collective-permute-start.6 = (bf16[2,18,1,128]{3,0,2,1:T(2,128)(2,1)S(1)}, bf16[2,18,1,128]{3,0,2,1:T(2,128)(2,1)S(1)}, u32[]{:S(2)}, u32[]{:S(2)}) collective-permute-start(bf16[2,18,1,128]{3,0,2,1:T(2,128)(2,1)S(1)} %get-tuple-element.53), channel_id=1, source_target_pairs={{0,1},{1,2},{2,3},{3,4},{4,5},{5,6},{6,7},{7,8},{8,9},{9,10},{10,1... | collective-permute-start | bytes 27656 | tf_op jit(solution)/shard_map/ppermute | solution.py:16
  44.8 5.5 %copy-start.18 = (bf16[2,18,1,128]{3,0,2,1:T(2,128)(2,1)}, bf16[2,18,1,128]{3,0,2,1:T(2,128)(2,1)S(1)}, u32[]{:S(2)}) copy-start(bf16[2,18,1,128]{3,0,2,1:T(2,128)(2,1)S(1)} %collective-permute-done.6) | copy-start | bytes 27652
  52.9 20.4 %copy-start.11 = (f32[3,32,2,128]{3,2,1,0:T(2,128)S(1)}, f32[3,32,2,128]{3,2,1,0:T(2,128)}, u32[]{:S(2)}) copy-start(f32[3,32,2,128]{3,2,1,0:T(2,128)} %param.9) | copy-start | bytes 294916
  53.4 12.4 %collective-permute-start.9 = (bf16[64,1,2,128]{3,0,2,1:T(8,128)(2,1)S(1)}, bf16[64,1,2,128]{3,0,2,1:T(8,128)(2,1)S(1)}, u32[]{:S(2)}, u32[]{:S(2)}) collective-permute-start(bf16[64,1,2,128]{3,0,2,1:T(8,128)(2,1)S(1)} %get-tuple-element.48), channel_id=1, source_target_pairs={{128,0},{129,1},{130,2},{131,3},{132,4},{133,5},{134,6},{135,7},{1... | collective-permute-start | bytes 98312 | tf_op jit(solution)/shard_map/ppermute | solution.py:17
  54.7 11.1 %collective-permute-start.8 = (bf16[64,1,2,128]{3,0,2,1:T(8,128)(2,1)S(1)}, bf16[64,1,2,128]{3,0,2,1:T(8,128)(2,1)S(1)}, u32[]{:S(2)}, u32[]{:S(2)}) collective-permute-start(bf16[64,1,2,128]{3,0,2,1:T(8,128)(2,1)S(1)} %get-tuple-element.47), channel_id=1, source_target_pairs={{0,128},{1,129},{2,130},{3,131},{4,132},{5,133},{6,134},{7,135},{8... | collective-permute-start | bytes 98312 | tf_op jit(solution)/shard_map/ppermute | solution.py:16
  58.7 14.3 %collective-permute-start.3 = (f32[1,32,1,128]{3,2,0,1:T(1,128)S(1)}, f32[1,32,1,128]{3,2,0,1:T(1,128)S(1)}, u32[]{:S(2)}, u32[]{:S(2)}) collective-permute-start(f32[1,32,1,128]{3,2,0,1:T(1,128)S(1)} %get-tuple-element.50), channel_id=1, source_target_pairs={{1,0},{2,1},{3,2},{4,3},{5,4},{6,5},{7,6},{8,7},{9,8},{10,9},{11,1... | collective-permute-start | bytes 49160 | tf_op jit(solution)/shard_map/ppermute | solution.py:17
  60.6 12.4 %collective-permute-start.2 = (f32[1,32,1,128]{3,2,0,1:T(1,128)S(1)}, f32[1,32,1,128]{3,2,0,1:T(1,128)S(1)}, u32[]{:S(2)}, u32[]{:S(2)}) collective-permute-start(f32[1,32,1,128]{3,2,0,1:T(1,128)S(1)} %get-tuple-element.49), channel_id=1, source_target_pairs={{0,1},{1,2},{2,3},{3,4},{4,5},{5,6},{6,7},{7,8},{8,9},{9,10},{10,1... | collective-permute-start | bytes 49160 | tf_op jit(solution)/shard_map/ppermute | solution.py:16
  65.9 11.6 %collective-permute-start.11 = (bf16[64,18,1,128]{3,0,2,1:T(8,128)(2,1)S(1)}, bf16[64,18,1,128]{3,0,2,1:T(8,128)(2,1)S(1)}, u32[]{:S(2)}, u32[]{:S(2)}) collective-permute-start(bf16[64,18,1,128]{3,0,2,1:T(8,128)(2,1)S(1)} %get-tuple-element.44), channel_id=1, source_target_pairs={{1,0},{2,1},{3,2},{4,3},{5,4},{6,5},{7,6},{8,7},{9,8},{10,9},{11,1... | collective-permute-start | bytes 884744 | tf_op jit(solution)/shard_map/ppermute | solution.py:17
  67.9 12.1 %collective-permute-start.10 = (bf16[64,18,1,128]{3,0,2,1:T(8,128)(2,1)S(1)}, bf16[64,18,1,128]{3,0,2,1:T(8,128)(2,1)S(1)}, u32[]{:S(2)}, u32[]{:S(2)}) collective-permute-start(bf16[64,18,1,128]{3,0,2,1:T(8,128)(2,1)S(1)} %get-tuple-element.43), channel_id=1, source_target_pairs={{0,1},{1,2},{2,3},{3,4},{4,5},{5,6},{6,7},{7,8},{8,9},{9,10},{10,1... | collective-permute-start | bytes 884744 | tf_op jit(solution)/shard_map/ppermute | solution.py:16
  74.2 28.6 %all-to-all-start.1 = ((f32[1,32,2,128]{3,2,0,1:T(2,128)}), f32[1,32,2,128]{3,2,0,1:T(2,128)S(1)}, u32[]{:S(2)}, u32[]{:S(2)}) async-start(f32[1,32,2,128]{3,2,0,1:T(2,128)} %get-tuple-element.35), calls=%async_computation.1 | async-start | bytes 65536 | tf_op jit(solution)/shard_map/all_to_all | solution.py:131
  77.4 342.9 %all-reduce.7.cloned.1.call-start = ((), (), s32[]{:S(2)}) async-start(), calls=%async_computation.2 | async-start | bytes 1769472 | tf_op jit(solution)/shard_map/psum | solution.py:137
  80.0 3.7 copy-start.1
  104.3 7.6 %copy-start.2 = (bf16[64,18,1,128]{3,0,2,1:T(8,128)(2,1)S(1)}, bf16[64,18,1,128]{3,0,2,1:T(8,128)(2,1)}, u32[]{:S(2)}) copy-start(bf16[64,18,1,128]{3,0,2,1:T(8,128)(2,1)} %copy-done.1) | copy-start | bytes 884740
  106.5 30.2 %collective-permute-start.13 = (bf16[64,1,2,128]{3,0,2,1:T(8,128)(2,1)S(1)}, bf16[64,1,2,128]{3,0,2,1:T(8,128)(2,1)S(1)}, u32[]{:S(2)}, u32[]{:S(2)}) collective-permute-start(bf16[64,1,2,128]{3,0,2,1:T(8,128)(2,1)S(1)} %get-tuple-element.46), channel_id=1, source_target_pairs={{128,0},{129,1},{130,2},{131,3},{132,4},{133,5},{134,6},{135,7},{1... | collective-permute-start | bytes 98312 | tf_op jit(solution)/shard_map/ppermute | solution.py:17
  107.8 28.9 %collective-permute-start.12 = (bf16[64,1,2,128]{3,0,2,1:T(8,128)(2,1)S(1)}, bf16[64,1,2,128]{3,0,2,1:T(8,128)(2,1)S(1)}, u32[]{:S(2)}, u32[]{:S(2)}) collective-permute-start(bf16[64,1,2,128]{3,0,2,1:T(8,128)(2,1)S(1)} %get-tuple-element.45), channel_id=1, source_target_pairs={{0,128},{1,129},{2,130},{3,131},{4,132},{5,133},{6,134},{7,135},{8... | collective-permute-start | bytes 98312 | tf_op jit(solution)/shard_map/ppermute | solution.py:16
  136.8 9.4 %copy-start.16 = (bf16[64,1,2,128]{3,0,2,1:T(8,128)(2,1)}, bf16[64,1,2,128]{3,0,2,1:T(8,128)(2,1)S(1)}, u32[]{:S(2)}) copy-start(bf16[64,1,2,128]{3,0,2,1:T(8,128)(2,1)S(1)} %collective-permute-done.12) | copy-start | bytes 98308
  137.7 284.8 %collective-permute-start.15 = (bf16[64,18,1,128]{3,0,2,1:T(8,128)(2,1)}, bf16[64,18,1,128]{3,0,2,1:T(8,128)(2,1)S(1)}, u32[]{:S(2)}, u32[]{:S(2)}) collective-permute-start(bf16[64,18,1,128]{3,0,2,1:T(8,128)(2,1)} %get-tuple-element.42), channel_id=1, source_target_pairs={{1,0},{2,1},{3,2},{4,3},{5,4},{6,5},{7,6},{8,7},{9,8},{10,9},{11,1... | collective-permute-start | bytes 884744 | tf_op jit(solution)/shard_map/ppermute | solution.py:17
  139.7 282.9 %collective-permute-start.14 = (bf16[64,18,1,128]{3,0,2,1:T(8,128)(2,1)}, bf16[64,18,1,128]{3,0,2,1:T(8,128)(2,1)S(1)}, u32[]{:S(2)}, u32[]{:S(2)}) collective-permute-start(bf16[64,18,1,128]{3,0,2,1:T(8,128)(2,1)} %get-tuple-element.41), channel_id=1, source_target_pairs={{0,1},{1,2},{2,3},{3,4},{4,5},{5,6},{6,7},{7,8},{8,9},{9,10},{10,1... | collective-permute-start | bytes 884744 | tf_op jit(solution)/shard_map/ppermute | solution.py:16
  149.3 273.3 %copy-start.17 = (bf16[64,1,2,128]{3,0,2,1:T(8,128)(2,1)S(1)}, bf16[64,1,2,128]{3,0,2,1:T(8,128)(2,1)}, u32[]{:S(2)}) copy-start(bf16[64,1,2,128]{3,0,2,1:T(8,128)(2,1)} %copy-done.16) | copy-start | bytes 98308
  440.5 3.4 copy-start.24
  (21 other events, 43.8 us)
Sparse Core Ops, SparseCore 0:
  150.4 269.8 all-reduce.6
where the time goes:
time: 545 us; the launch traced here: 536 us
  waiting for transfers between devices  274 us (50%)
  blocking collectives  82 us (15%)
  matrix products  58.2 us (11%)
  starting transfers between devices  58.1 us (11%)
  local copies, waits for them, and re-layouts  39 us (7%)
  between operations  15.1 us (3%)
  other arithmetic  9.44 us (2%)
    psum x1, waiting for transfers between devices, on_device(): lax.psum((lift_grad, liftbias_grad, mix_grad, mixbias_grad, out_grad, out...  268 us
    psum x1, blocking collectives, on_device(): lax.psum((lift_grad, liftbias_grad, mix_grad, mixbias_grad, out_grad, out...  76.8 us
    ppermute x8, starting transfers between devices, extended(): before = lax.ppermute(last, axis, up)  36.4 us
    dot_general x54, matrix products, kernel_grad(): lax.dot_general(cot_rows, window, (((1,), (1,)), ((), ())), preferred_ele...  33.5 us
    unnamed x80, local copies, waits for them, and re-layouts  20.6 us
    conv_general_dilated x3, matrix products, convolve(): lax.conv_general_dilated(padded[None], kernel, (1, 1, 1), ((0, 0), (0, 0)...  19.1 us
    ppermute x8, starting transfers between devices, extended(): after = lax.ppermute(leading, axis, down)  18.4 us
  transfers between devices with their start and end apart: 18, of which 4 were waited for; matrix products, arithmetic and copies ran while one was open for 11% of the time, Pallas kernels for 0%

commit v1 on v0

--- a/solution.py
+++ b/solution.py
@@ -3,7 +3,177 @@
 import jax
 import jax.numpy as jnp
 from jax import lax
+from jax.experimental import pallas as pl
+from jax.experimental.pallas import tpu as pltpu
 from jax.sharding import PartitionSpec as P
+
+
+MESH = pl.DeviceIdType.MESH
+
+
+def total_kernel(buf, out, from_core, mine, from_plane, from_z, s1, r1, s2, r2, s3, r3, s4, r4, s5, r5):
+    y_lo = lax.axis_index("grp")
+    gx = lax.axis_index("gx")
+    gy = lax.axis_index("gy")
+    z, x = gx // 4, gx % 4
+    y_hi, core = gy // 2, gy % 2
+    place = x * 4 + y_hi * 2 + y_lo
+    sibling = (y_lo, gx, y_hi * 2 + 1 - core)
+
+    def in_plane(other):
+        return (other % 2, z * 4 + other // 4, ((other // 2) % 2) * 2 + core)
+
+    def in_z(other):
+        return (y_lo, other * 4 + x, gy)
+
+    barrier = pltpu.get_barrier_semaphore()
+    pl.semaphore_signal(barrier, inc=1, device_id=sibling, device_id_type=MESH)
+
+    def greet_plane(j, _):
+        pl.semaphore_signal(barrier, inc=1, device_id=in_plane((place + j) % 16), device_id_type=MESH)
+        return 0
+
+    def greet_z(j, _):
+        pl.semaphore_signal(barrier, inc=1, device_id=in_z((z + j) % 8), device_id_type=MESH)
+        return 0
+
+    lax.fori_loop(1, 16, greet_plane, 0)
+    lax.fori_loop(1, 8, greet_z, 0)
+    pl.semaphore_wait(barrier, 23)
+
+    theirs = pl.multiple_of((1 - core) * 16, 16)
+    ours = pl.multiple_of(core * 16, 16)
+    swap = pltpu.make_async_remote_copy(
+        buf.at[pl.ds(theirs, 16)], from_core, s1, r1, device_id=sibling, device_id_type=MESH
+    )
+    swap.start()
+    swap.wait()
+
+    def add_core(j, _):
+        mine[j] = buf[ours + j] + from_core[j]
+        return 0
+
+    lax.fori_loop(0, 16, add_core, 0)
+
+    def to_plane(j):
+        other = (place + j) % 16
+        return pltpu.make_async_remote_copy(
+            mine.at[other], from_plane.at[place], s2.at[other], r2.at[place],
+            device_id=in_plane(other), device_id_type=MESH,
+        )
+
+    def of_plane(j):
+        other = (place + j) % 16
+        return pltpu.make_async_remote_copy(
+            mine.at[other], from_plane.at[other], s2.at[other], r2.at[other],
+            device_id=in_plane(other), device_id_type=MESH,
+        )
+
+    lax.fori_loop(1, 16, lambda j, _: (to_plane(j).start(), 0)[1], 0)
+    from_plane[place] = mine[place]
+
+    def wait_plane(j, _):
+        of_plane(j).wait()
+        return 0
+
+    lax.fori_loop(1, 16, wait_plane, 0)
+    total = from_plane[0]
+    for j in range(1, 16):
+        total = total + from_plane[j]
+    from_z[z] = total
+
+    def to_z(j):
+        other = (z + j) % 8
+        return pltpu.make_async_remote_copy(
+            from_z.at[z], from_z.at[z], s3.at[other], r3.at[z], device_id=in_z(other), device_id_type=MESH
+        )
+
+    def of_z(j):
+        other = (z + j) % 8
+        return pltpu.make_async_remote_copy(
+            from_z.at[other], from_z.at[other], s3.at[other], r3.at[other], device_id=in_z(other), device_id_type=MESH
+        )
+
+    lax.fori_loop(1, 8, lambda j, _: (to_z(j).start(), 0)[1], 0)
+
+    def wait_z(j, _):
+        of_z(j).wait()
+        return 0
+
+    lax.fori_loop(1, 8, wait_z, 0)
+    total = from_z[0]
+    for j in range(1, 8):
+        total = total + from_z[j]
+    out[ours + place] = total
+
+    def gather(j):
+        other = (place + j) % 16
+        return pltpu.make_async_remote_copy(
+            out.at[ours + place], out.at[ours + place], s4.at[other], r4.at[place],
+            device_id=in_plane(other), device_id_type=MESH,
+        )
+
+    def gathered(j):
+        other = (place + j) % 16
+        return pltpu.make_async_remote_copy(
+            out.at[ours + other], out.at[ours + other], s4.at[other], r4.at[other],
+            device_id=in_plane(other), device_id_type=MESH,
+        )
+
+    def hand(j):
+        other = (place + j) % 16
+        return pltpu.make_async_remote_copy(
+            out.at[ours + other], out.at[ours + other], s5.at[other], r5.at[other],
+            device_id=sibling, device_id_type=MESH,
+        )
+
+    def handed(j):
+        other = (place + j) % 16
+        return pltpu.make_async_remote_copy(
+            out.at[theirs + other], out.at[theirs + other], s5.at[other], r5.at[other],
+            device_id=sibling, device_id_type=MESH,
+        )
+
+    lax.fori_loop(1, 16, lambda j, _: (gather(j).start(), 0)[1], 0)
+    hand(0).start()
+
+    def pass_on(j, _):
+        gathered(j).wait_recv()
+        hand(j).start()
+        return 0
+
+    lax.fori_loop(1, 16, pass_on, 0)
+
+    def finish(j, _):
+        handed(j).wait_recv()
+        hand(j).wait_send()
+        return 0
+
+    lax.fori_loop(0, 16, finish, 0)
+    lax.fori_loop(1, 16, lambda j, _: (gather(j).wait_send(), 0)[1], 0)
+
+
+def all_total(buf):
+    rows = buf.shape[1]
+    chunk = (rows, 128)
+    dma = pltpu.SemaphoreType.DMA
+    vmem = pl.BlockSpec(memory_space=pltpu.VMEM)
+    return pl.pallas_call(
+        total_kernel,
+        out_shape=jax.ShapeDtypeStruct(buf.shape, jnp.float32),
+        in_specs=[vmem],
+        out_specs=vmem,
+        scratch_shapes=[
+            pltpu.VMEM((16,) + chunk, jnp.float32),
+            pltpu.VMEM((16,) + chunk, jnp.float32),
+            pltpu.VMEM((16,) + chunk, jnp.float32),
+            pltpu.VMEM((8,) + chunk, jnp.float32),
+            dma, dma, dma((16,)), dma((16,)), dma((8,)), dma((8,)),
+            dma((16,)), dma((16,)), dma((16,)), dma((16,)),
+        ],
+        compiler_params=pltpu.CompilerParams(collective_id=0, has_side_effects=True, vmem_limit_bytes=40 * 2**20),
+        name="total",
+    )(buf)
 
 
 def extended(value, sides, width):
@@ -134,10 +304,15 @@
         inputs, targets, w_lift, b_lift, w_mix, b_mix, w_out, b_out, loss_scale, slab_rim
     )
     lift_grad, liftbias_grad, mix_grad, mixbias_grad, out_grad, outbias_grad = results
-    summed = lax.psum(
-        (lift_grad, liftbias_grad, mix_grad, mixbias_grad, out_grad, outbias_grad),
-        ("grp", "gx", "gy"),
-    )
+    parts = (lift_grad, liftbias_grad, mix_grad, mixbias_grad, out_grad, outbias_grad)
+    flat = jnp.concatenate([part.reshape(-1) for part in parts])
+    rows = -(-flat.size // (32 * 128))
+    flat = jnp.pad(flat, (0, rows * 32 * 128 - flat.size))
+    flat = all_total(flat.reshape(32, rows, 128)).reshape(-1)
+    summed, at = [], 0
+    for part in parts:
+        summed.append(flat[at : at + part.size].reshape(part.shape))
+        at += part.size
     return (advanced, summed[0], summed[1], summed[2], summed[3], summed[4], summed[5])
 
 

time: 545 us -> 323 us (0.59)
  waiting for transfers between devices: 274 us -> 11 us
  blocking collectives: 82 us -> 5.05 us
  matrix products: 58.2 us -> 131 us
  Pallas kernels: 0 us -> 47.1 us
  local copies, waits for them, and re-layouts: 39 us -> 54.5 us
  between operations: 15.1 us -> 1.8 us
  other arithmetic: 9.44 us -> 17.3 us
  starting transfers between devices: 58.1 us -> 51.7 us
    psum x1 -> x0, waiting for transfers between devices: 268 us -> none  [on_device(): lax.psum((lift_grad, liftbias_grad, mix_grad, mixbias_grad, out_grad, out...]
    psum x1 -> x0, blocking collectives: 76.8 us -> none  [on_device(): lax.psum((lift_grad, liftbias_grad, mix_grad, mixbias_grad, out_grad, out...]
    conv_general_dilated x3, matrix products: 19.1 us -> 86.1 us  [convolve(): lax.conv_general_dilated(padded[None], kernel, (1, 1, 1), ((0, 0), (0, 0)...]
    pallas_call x0 -> x1, Pallas kernels: none -> 47.1 us  [all_total(): pl.pallas_call(total_kernel, out_shape=jax.ShapeDtypeStruct(buf.shape, jn...]
    unnamed x80, local copies, waits for them, and re-layouts: 20.6 us -> 2.89 us
    broadcast_in_dim x3, local copies, waits for them, and re-layouts: 4.3 us -> 21.5 us  [convolve(): padded[None]]
    dot_general x54, matrix products: 33.5 us -> 42.3 us  [kernel_grad(): lax.dot_general(cot_rows, window, (((1,), (1,)), ((), ())), preferred_ele...]
    ppermute x8, waiting for transfers between devices: 2.96 us -> 11 us  [extended(): after = lax.ppermute(leading, axis, down)]
  transfers between devices with their start and end apart: 18 -> 17, of which waited for: 4 -> 3; matrix products, arithmetic and copies ran while one was open for 11% -> 44% of each run, Pallas kernels for 0% -> 0%
where the time goes in v1:
time: 323 us; the launch traced here: 319 us
  matrix products  131 us (41%)
  local copies, waits for them, and re-layouts  54.5 us (17%)
  starting transfers between devices  51.7 us (16%)
  Pallas kernels  47.1 us (15%)
  other arithmetic  17.3 us (5%)
  waiting for transfers between devices  11 us (3%)
  blocking collectives  5.05 us (2%)
    conv_general_dilated x3, matrix products, convolve(): lax.conv_general_dilated(padded[None], kernel, (1, 1, 1), ((0, 0), (0, 0)...  86.1 us
    pallas_call x1, Pallas kernels, all_total(): pl.pallas_call(total_kernel, out_shape=jax.ShapeDtypeStruct(buf.shape, jn...  47.1 us
    dot_general x54, matrix products, kernel_grad(): lax.dot_general(cot_rows, window, (((1,), (1,)), ((), ())), preferred_ele...  42.3 us
    ppermute x8, starting transfers between devices, extended(): before = lax.ppermute(last, axis, up)  34.4 us
    broadcast_in_dim x3, local copies, waits for them, and re-layouts, convolve(): padded[None]  21.5 us
    ppermute x8, starting transfers between devices, extended(): after = lax.ppermute(leading, axis, down)  13.5 us
    ppermute x8, waiting for transfers between devices, extended(): after = lax.ppermute(leading, axis, down)  11 us
    conv_general_dilated x3, local copies, waits for them, and re-layouts, convolve(): lax.conv_general_dilated(padded[None], kernel, (1, 1, 1), ((0, 0), (0, 0)...  6.91 us
  transfers between devices with their start and end apart: 17, of which 3 were waited for; matrix products, arithmetic and copies ran while one was open for 44% of the time, Pallas kernels for 0%

profile of v1, /device:TPU:1, one launch (start us, length us, event | category | flops | bytes accessed | tf_op | source)
XLA Modules:
  0.0 319.4 jit_solution(11573381403504963761)
XLA Ops:
  1.5 6.2 %collective-permute-start = (f32[1,32,1,128]{3,2,0,1:T(1,128)S(1)}, f32[1,32,1,128]{3,2,0,1:T(1,128)S(1)}, u32[]{:S(2)}, u32[]{:S(2)}) collective-permute-start(f32[1,32,1,128]{3,2,0,1:T(1,128)S(1)} %get-tuple-element.76), channel_id=1, source_target_pairs={{0,1},{1,2},{2,3},{3,4},{4,5},{5,6},{6,7},{7,8},{8,9},{9,10},{10,1... | collective-permute-start | bytes 49160 | tf_op jit(solution)/shard_map/ppermute | solution.py:186
  7.7 1.9 collective-permute-start.1
  9.7 4.6 %collective-permute-done.1 = f32[1,32,1,128]{3,2,0,1:T(1,128)S(1)} collective-permute-done((f32[1,32,1,128]{3,2,0,1:T(1,128)S(1)}, f32[1,32,1,128]{3,2,0,1:T(1,128)S(1)}, u32[]{:S(2)}, u32[]{:S(2)}) %collective-permute-start.1) | collective-permute-done | bytes 16416 | tf_op jit(solution)/shard_map/ppermute | solution.py:187
  16.4 5.1 %all_to_all.21 = bf16[1,32,2,128]{3,2,0,1:T(2,128)(2,1)S(1)} all-to-all(bf16[1,32,2,128]{3,2,0,1:T(2,128)(2,1)S(1)} %get-tuple-element.34), channel_id=1, replica_groups=mesh['grp'=2,'gx'=32,'gy'=4] {'grp'}, dimensions={1} | all-to-all | bytes 32768 | tf_op jit(solution)/shard_map/all_to_all | solution.py:300
  21.5 1.9 collective-permute-start.4
  28.4 3.0 collective-permute-done.5
  31.4 4.2 %collective-permute-start.6 = (bf16[2,18,1,128]{3,0,2,1:T(2,128)(2,1)S(1)}, bf16[2,18,1,128]{3,0,2,1:T(2,128)(2,1)S(1)}, u32[]{:S(2)}, u32[]{:S(2)}) collective-permute-start(bf16[2,18,1,128]{3,0,2,1:T(2,128)(2,1)S(1)} %get-tuple-element.78), channel_id=1, source_target_pairs={{0,1},{1,2},{2,3},{3,4},{4,5},{5,6},{6,7},{7,8},{8,9},{9,10},{10,1... | collective-permute-start | bytes 27656 | tf_op jit(solution)/shard_map/ppermute | solution.py:186
  35.6 1.9 collective-permute-start.7
  37.6 5.1 %collective-permute-start.2 = (f32[1,32,1,128]{3,2,0,1:T(1,128)S(1)}, f32[1,32,1,128]{3,2,0,1:T(1,128)S(1)}, u32[]{:S(2)}, u32[]{:S(2)}) collective-permute-start(f32[1,32,1,128]{3,2,0,1:T(1,128)S(1)} %get-tuple-element.74), channel_id=1, source_target_pairs={{0,1},{1,2},{2,3},{3,4},{4,5},{5,6},{6,7},{7,8},{8,9},{9,10},{10,1... | collective-permute-start | bytes 49160 | tf_op jit(solution)/shard_map/ppermute | solution.py:186
  42.7 1.9 collective-permute-start.3
  44.8 8.0 %copy.386 = bf16[1,2,18,4,128]{1,0,4,3,2:T(2,128)(2,1)} copy(bf16[1,2,18,4,128]{4,1,3,2,0:T(2,128)(2,1)S(1)} %fusion.287) | data formatting | bytes 73728 | tf_op jit(solution)/shard_map/broadcast_in_dim | solution.py:217
  52.8 17.2 %fusion.157 = f32[1,64,16,2,128]{1,0,4,3,2:T(1,128)S(1)} fusion(bf16[1,2,18,4,128]{1,0,4,3,2:T(2,128)(2,1)} %copy.386, bf16[64,2,3,3,3]{0,4,3,2,1:T(4,128)(2,1)S(1)} %reshape.35), kind=kOutput, calls=%fused_computation.287 | convolution fusion | flops 28164096 | bytes 1092352 | tf_op jit(solution)/shard_map/conv_general_dilated | solution.py:216
  75.0 3.4 %collective-permute-done.9 = bf16[64,1,2,128]{3,1,2,0:T(2,128)(2,1)S(1)} collective-permute-done((bf16[64,1,2,128]{3,1,2,0:T(2,128)(2,1)S(1)}, bf16[64,1,2,128]{3,1,2,0:T(2,128)(2,1)S(1)}, u32[]{:S(2)}, u32[]{:S(2)}) %collective-permute-start.9) | collective-permute-done | bytes 32800 | tf_op jit(solution)/shard_map/ppermute | solution.py:187
  79.0 1.9 collective-permute-start.11
  81.0 6.9 %collective-permute-start.10 = (bf16[64,18,1,128]{3,0,2,1:T(8,128)(2,1)S(1)}, bf16[64,18,1,128]{3,0,2,1:T(8,128)(2,1)S(1)}, u32[]{:S(2)}, u32[]{:S(2)}) collective-permute-start(bf16[64,18,1,128]{3,0,2,1:T(8,128)(2,1)S(1)} %copy.389), channel_id=1, source_target_pairs={{0,1},{1,2},{2,3},{3,4},{4,5},{5,6},{6,7},{7,8},{8,9},{9,10},{10,1... | collective-permute-start | bytes 884744 | tf_op jit(solution)/shard_map/ppermute | solution.py:186
  88.8 3.9 %all-to-all-start.1 = ((f32[1,32,2,128]{3,2,0,1:T(2,128)}), f32[1,32,2,128]{3,2,0,1:T(2,128)}, u32[]{:S(2)}, u32[]{:S(2)}) async-start(f32[1,32,2,128]{3,2,0,1:T(2,128)} %get-tuple-element.32), calls=%async_computation.1 | async-start | bytes 65536 | tf_op jit(solution)/shard_map/all_to_all | solution.py:301
  97.6 6.7 %copy.394 = bf16[1,64,18,4,128]{1,0,4,3,2:T(2,128)(2,1)} copy(bf16[1,64,18,4,128]{4,2,3,1,0:T(8,128)(2,1)S(1)} %fusion.286) | data formatting | bytes 2359296 | tf_op jit(solution)/shard_map/broadcast_in_dim | solution.py:217
  104.3 47.8 %fusion.277 = f32[1,64,16,2,128]{1,0,4,3,2:T(1,128)} fusion(bf16[1,64,18,4,128]{1,0,4,3,2:T(2,128)(2,1)} %copy.394, bf16[64,64,3,3,3]{1,0,4,3,2:T(8,128)(2,1)} %copy.395), kind=kOutput, calls=%fused_computation.403 | convolution fusion | flops 901251072 | bytes 2449408 | tf_op jit(solution)/shard_map/conv_general_dilated | solution.py:216
  152.1 2.8 copy.396
  156.1 1.8 convert_reduce_fusion.2
  158.2 2.6 convert_reduce_fusion
  160.9 3.3 %collective-permute-start.12 = (bf16[64,1,2,128]{3,1,2,0:T(2,128)(2,1)S(1)}, bf16[64,1,2,128]{3,1,2,0:T(2,128)(2,1)S(1)}, u32[]{:S(2)}, u32[]{:S(2)}) collective-permute-start(bf16[64,1,2,128]{3,1,2,0:T(2,128)(2,1)S(1)} %get-tuple-element.68), channel_id=1, source_target_pairs={{0,128},{1,129},{2,130},{3,131},{4,132},{5,133},{6,134},{7,135},{8... | collective-permute-start | bytes 98312 | tf_op jit(solution)/shard_map/ppermute | solution.py:186
  166.2 3.6 %pad_slice_fusion = (bf16[64,16,2,128]{3,1,2,0:T(8,128)(2,1)}, bf16[64,16,2,128]{3,1,2,0:T(8,128)(2,1)S(1)}, bf16[64,16,2,128]{3,1,2,0:T(8,128)(2,1)S(1)}, bf16[...) fusion(bf16[64,18,4,128]{3,1,2,0:T(8,128)(2,1)S(1)} %pad_maximu, ...), kind=kLoop, calls=%fused_computation | loop fusion | bytes 10616832 | tf_op jit(solution)/shard_map/slice | solution.py:235
  206.6 1.9 collective-permute-start.15
  208.5 5.1 %collective-permute-start.14 = (bf16[64,18,1,128]{3,0,2,1:T(8,128)(2,1)}, bf16[64,18,1,128]{3,0,2,1:T(8,128)(2,1)}, u32[]{:S(2)}, u32[]{:S(2)}) collective-permute-start(bf16[64,18,1,128]{3,0,2,1:T(8,128)(2,1)} %copy.401), channel_id=1, source_target_pairs={{0,1},{1,2},{2,3},{3,4},{4,5},{5,6},{6,7},{7,8},{8,9},{9,10},{10,1... | collective-permute-start | bytes 884744 | tf_op jit(solution)/shard_map/ppermute | solution.py:186
  215.8 1.8 copy.498
  217.7 2.6 reshape_reshape.7
  224.3 6.8 %copy.405 = bf16[1,64,18,4,128]{1,0,4,3,2:T(2,128)(2,1)} copy(bf16[1,64,18,4,128]{4,2,3,1,0:T(8,128)(2,1)S(1)} %maximum_bitcast_fusion) | data formatting | bytes 2359296 | tf_op jit(solution)/shard_map/broadcast_in_dim | solution.py:217
  231.1 21.1 %fusion.278 = f32[1,64,16,2,128]{1,0,4,3,2:T(1,128)} fusion(bf16[1,64,18,4,128]{1,0,4,3,2:T(2,128)(2,1)} %copy.405, bf16[64,64,3,3,3]{1,0,4,3,2:T(8,128)(2,1)S(1)} %copy-done.14), kind=kOutput, calls=%fused_computation.404 | convolution fusion | flops 901251072 | bytes 2449408 | tf_op jit(solution)/shard_map/conv_general_dilated | solution.py:216
  252.2 2.8 copy.407
  265.7 2.4 concatenate.91
  268.1 47.1 %total.1 = f32[32,28,128]{2,1,0:T(8,128)S(1)} custom-call(f32[32,28,128]{2,1,0:T(8,128)S(1)} %reshape.38.buf), custom_call_target="tpu_custom_call" | custom-call | tf_op jit(solution)/shard_map/total/pallas_call | solution.py:161
  (209 shorter events, 79.9 us)
Async XLA Ops:
  0.6 155.4 %copy-start = (bf16[2,64]{1,0:T(2,128)(2,1)S(1)}, bf16[2,64]{1,0:T(2,128)(2,1)}, u32[]{:S(2)}) copy-start(bf16[2,64]{1,0:T(2,128)(2,1)} %param.14) | copy-start | bytes 772
  1.5 8.2 %collective-permute-start = (f32[1,32,1,128]{3,2,0,1:T(1,128)S(1)}, f32[1,32,1,128]{3,2,0,1:T(1,128)S(1)}, u32[]{:S(2)}, u32[]{:S(2)}) collective-permute-start(f32[1,32,1,128]{3,2,0,1:T(1,128)S(1)} %get-tuple-element.76), channel_id=1, source_target_pairs={{0,1},{1,2},{2,3},{3,4},{4,5},{5,6},{6,7},{7,8},{8,9},{9,10},{10,1... | collective-permute-start | bytes 49160 | tf_op jit(solution)/shard_map/ppermute | solution.py:186
  7.7 6.6 %collective-permute-start.1 = (f32[1,32,1,128]{3,2,0,1:T(1,128)S(1)}, f32[1,32,1,128]{3,2,0,1:T(1,128)S(1)}, u32[]{:S(2)}, u32[]{:S(2)}) collective-permute-start(f32[1,32,1,128]{3,2,0,1:T(1,128)S(1)} %get-tuple-element.77), channel_id=1, source_target_pairs={{1,0},{2,1},{3,2},{4,3},{5,4},{6,5},{7,6},{8,7},{9,8},{10,9},{11,1... | collective-permute-start | bytes 49160 | tf_op jit(solution)/shard_map/ppermute | solution.py:187
  21.5 31.4 %copy-start.22 = (bf16[1,32,2,128]{3,1,2,0:T(8,128)(2,1)}, bf16[1,32,2,128]{3,1,2,0:T(8,128)(2,1)S(1)}, u32[]{:S(2)}) copy-start(bf16[1,32,2,128]{3,1,2,0:T(8,128)(2,1)S(1)} %copy.739) | copy-start | bytes 49156
  21.5 6.8 %collective-permute-start.4 = (bf16[2,1,2,128]{3,0,2,1:T(2,128)(2,1)S(1)}, bf16[2,1,2,128]{3,0,2,1:T(2,128)(2,1)S(1)}, u32[]{:S(2)}, u32[]{:S(2)}) collective-permute-start(bf16[2,1,2,128]{3,0,2,1:T(2,128)(2,1)S(1)} %get-tuple-element.81), channel_id=1, source_target_pairs={{0,128},{1,129},{2,130},{3,131},{4,132},{5,133},{6,134},{7,135},{8... | collective-permute-start | bytes 3080 | tf_op jit(solution)/shard_map/ppermute | solution.py:186
  27.0 4.3 %collective-permute-start.5 = (bf16[2,1,2,128]{3,0,2,1:T(2,128)(2,1)S(1)}, bf16[2,1,2,128]{3,0,2,1:T(2,128)(2,1)S(1)}, u32[]{:S(2)}, u32[]{:S(2)}) collective-permute-start(bf16[2,1,2,128]{3,0,2,1:T(2,128)(2,1)S(1)} %get-tuple-element.80), channel_id=1, source_target_pairs={{128,0},{129,1},{130,2},{131,3},{132,4},{133,5},{134,6},{135,7},{1... | collective-permute-start | bytes 3080 | tf_op jit(solution)/shard_map/ppermute | solution.py:187
  28.3 9.2 %copy-start.34 = (bf16[2,1,2,128]{3,0,2,1:T(2,128)(2,1)}, bf16[2,1,2,128]{3,0,2,1:T(2,128)(2,1)S(1)}, u32[]{:S(2)}) copy-start(bf16[2,1,2,128]{3,0,2,1:T(2,128)(2,1)S(1)} %collective-permute-done.4) | copy-start | bytes 3076
  31.3 61.3 %copy-start.20 = (bf16[2,18,2,128]{3,0,2,1:T(2,128)(2,1)}, bf16[2,18,2,128]{3,0,2,1:T(2,128)(2,1)S(1)}, u32[]{:S(2)}) copy-start(bf16[2,18,2,128]{3,0,2,1:T(2,128)(2,1)S(1)} %constant_dynamic-update-slice_fusion) | copy-start | bytes 55300
  31.4 13.3 %collective-permute-start.6 = (bf16[2,18,1,128]{3,0,2,1:T(2,128)(2,1)S(1)}, bf16[2,18,1,128]{3,0,2,1:T(2,128)(2,1)S(1)}, u32[]{:S(2)}, u32[]{:S(2)}) collective-permute-start(bf16[2,18,1,128]{3,0,2,1:T(2,128)(2,1)S(1)} %get-tuple-element.78), channel_id=1, source_target_pairs={{0,1},{1,2},{2,3},{3,4},{4,5},{5,6},{6,7},{7,8},{8,9},{9,10},{10,1... | collective-permute-start | bytes 27656 | tf_op jit(solution)/shard_map/ppermute | solution.py:186
  35.6 9.1 %collective-permute-start.7 = (bf16[2,18,1,128]{3,0,2,1:T(2,128)(2,1)S(1)}, bf16[2,18,1,128]{3,0,2,1:T(2,128)(2,1)S(1)}, u32[]{:S(2)}, u32[]{:S(2)}) collective-permute-start(bf16[2,18,1,128]{3,0,2,1:T(2,128)(2,1)S(1)} %get-tuple-element.79), channel_id=1, source_target_pairs={{1,0},{2,1},{3,2},{4,3},{5,4},{6,5},{7,6},{8,7},{9,8},{10,9},{11,1... | collective-permute-start | bytes 27656 | tf_op jit(solution)/shard_map/ppermute | solution.py:187
  37.6 37.1 %collective-permute-start.2 = (f32[1,32,1,128]{3,2,0,1:T(1,128)S(1)}, f32[1,32,1,128]{3,2,0,1:T(1,128)S(1)}, u32[]{:S(2)}, u32[]{:S(2)}) collective-permute-start(f32[1,32,1,128]{3,2,0,1:T(1,128)S(1)} %get-tuple-element.74), channel_id=1, source_target_pairs={{0,1},{1,2},{2,3},{3,4},{4,5},{5,6},{6,7},{7,8},{8,9},{9,10},{10,1... | collective-permute-start | bytes 49160 | tf_op jit(solution)/shard_map/ppermute | solution.py:186
  42.7 31.9 %collective-permute-start.3 = (f32[1,32,1,128]{3,2,0,1:T(1,128)S(1)}, f32[1,32,1,128]{3,2,0,1:T(1,128)S(1)}, u32[]{:S(2)}, u32[]{:S(2)}) collective-permute-start(f32[1,32,1,128]{3,2,0,1:T(1,128)S(1)} %get-tuple-element.75), channel_id=1, source_target_pairs={{1,0},{2,1},{3,2},{4,3},{5,4},{6,5},{7,6},{8,7},{9,8},{10,9},{11,1... | collective-permute-start | bytes 49160 | tf_op jit(solution)/shard_map/ppermute | solution.py:187
  44.7 48.0 %copy-start.24 = (bf16[2,18,1,128]{3,0,2,1:T(2,128)(2,1)}, bf16[2,18,1,128]{3,0,2,1:T(2,128)(2,1)S(1)}, u32[]{:S(2)}) copy-start(bf16[2,18,1,128]{3,0,2,1:T(2,128)(2,1)S(1)} %collective-permute-done.6) | copy-start | bytes 27652
  71.9 16.0 %copy-start.15 = (f32[3,32,2,128]{3,2,1,0:T(2,128)S(1)}, f32[3,32,2,128]{3,2,1,0:T(2,128)}, u32[]{:S(2)}) copy-start(f32[3,32,2,128]{3,2,1,0:T(2,128)} %param.9) | copy-start | bytes 294916
  71.9 3.0 collective-permute-start.8
  73.3 5.0 %collective-permute-start.9 = (bf16[64,1,2,128]{3,1,2,0:T(2,128)(2,1)S(1)}, bf16[64,1,2,128]{3,1,2,0:T(2,128)(2,1)S(1)}, u32[]{:S(2)}, u32[]{:S(2)}) collective-permute-start(bf16[64,1,2,128]{3,1,2,0:T(2,128)(2,1)S(1)} %get-tuple-element.71), channel_id=1, source_target_pairs={{128,0},{129,1},{130,2},{131,3},{132,4},{133,5},{134,6},{135,7},{1... | collective-permute-start | bytes 98312 | tf_op jit(solution)/shard_map/ppermute | solution.py:187
  75.0 18.4 %copy-start.5 = (bf16[64,1,2,128]{3,1,2,0:T(2,128)(2,1)}, bf16[64,1,2,128]{3,1,2,0:T(2,128)(2,1)S(1)}, u32[]{:S(2)}) copy-start(bf16[64,1,2,128]{3,1,2,0:T(2,128)(2,1)S(1)} %collective-permute-done.8) | copy-start | bytes 98308
  78.4 15.0 %copy-start.7 = (bf16[64,1,2,128]{3,1,2,0:T(2,128)(2,1)}, bf16[64,1,2,128]{3,1,2,0:T(2,128)(2,1)S(1)}, u32[]{:S(2)}) copy-start(bf16[64,1,2,128]{3,1,2,0:T(2,128)(2,1)S(1)} %collective-permute-done.9) | copy-start | bytes 98308
  79.0 15.9 %collective-permute-start.11 = (bf16[64,18,1,128]{3,0,2,1:T(8,128)(2,1)S(1)}, bf16[64,18,1,128]{3,0,2,1:T(8,128)(2,1)S(1)}, u32[]{:S(2)}, u32[]{:S(2)}) collective-permute-start(bf16[64,18,1,128]{3,0,2,1:T(8,128)(2,1)S(1)} %copy.390), channel_id=1, source_target_pairs={{1,0},{2,1},{3,2},{4,3},{5,4},{6,5},{7,6},{8,7},{9,8},{10,9},{11,1... | collective-permute-start | bytes 884744 | tf_op jit(solution)/shard_map/ppermute | solution.py:187
  81.0 14.2 %collective-permute-start.10 = (bf16[64,18,1,128]{3,0,2,1:T(8,128)(2,1)S(1)}, bf16[64,18,1,128]{3,0,2,1:T(8,128)(2,1)S(1)}, u32[]{:S(2)}, u32[]{:S(2)}) collective-permute-start(bf16[64,18,1,128]{3,0,2,1:T(8,128)(2,1)S(1)} %copy.389), channel_id=1, source_target_pairs={{0,1},{1,2},{2,3},{3,4},{4,5},{5,6},{6,7},{7,8},{8,9},{9,10},{10,1... | collective-permute-start | bytes 884744 | tf_op jit(solution)/shard_map/ppermute | solution.py:186
  88.8 67.3 %all-to-all-start.1 = ((f32[1,32,2,128]{3,2,0,1:T(2,128)}), f32[1,32,2,128]{3,2,0,1:T(2,128)}, u32[]{:S(2)}, u32[]{:S(2)}) async-start(f32[1,32,2,128]{3,2,0,1:T(2,128)} %get-tuple-element.32), calls=%async_computation.1 | async-start | bytes 65536 | tf_op jit(solution)/shard_map/all_to_all | solution.py:301
  156.1 9.5 %copy-start.2 = (bf16[64,18,1,128]{3,1,2,0:T(8,128)(2,1)S(1)}, bf16[64,18,1,128]{3,1,2,0:T(8,128)(2,1)}, u32[]{:S(2)}) copy-start(bf16[64,18,1,128]{3,1,2,0:T(8,128)(2,1)} %copy-done.1) | copy-start | bytes 884740
  156.1 9.5 %copy-start.6 = (bf16[64,1,2,128]{3,1,2,0:T(2,128)(2,1)S(1)}, bf16[64,1,2,128]{3,1,2,0:T(2,128)(2,1)}, u32[]{:S(2)}) copy-start(bf16[64,1,2,128]{3,1,2,0:T(2,128)(2,1)} %copy-done.5) | copy-start | bytes 98308
  156.1 9.5 %copy-start.8 = (bf16[64,1,2,128]{3,1,2,0:T(2,128)(2,1)S(1)}, bf16[64,1,2,128]{3,1,2,0:T(2,128)(2,1)}, u32[]{:S(2)}) copy-start(bf16[64,1,2,128]{3,1,2,0:T(2,128)(2,1)} %copy-done.7) | copy-start | bytes 98308
  160.8 53.7 %copy-start.3 = (bf16[64,16,2,128]{3,1,2,0:T(8,128)(2,1)}, bf16[64,16,2,128]{3,1,2,0:T(8,128)(2,1)S(1)}, u32[]{:S(2)}) copy-start(bf16[64,16,2,128]{3,1,2,0:T(8,128)(2,1)S(1)} %get-tuple-element.29) | copy-start | bytes 1572868
  160.9 43.5 %collective-permute-start.12 = (bf16[64,1,2,128]{3,1,2,0:T(2,128)(2,1)S(1)}, bf16[64,1,2,128]{3,1,2,0:T(2,128)(2,1)S(1)}, u32[]{:S(2)}, u32[]{:S(2)}) collective-permute-start(bf16[64,1,2,128]{3,1,2,0:T(2,128)(2,1)S(1)} %get-tuple-element.68), channel_id=1, source_target_pairs={{0,128},{1,129},{2,130},{3,131},{4,132},{5,133},{6,134},{7,135},{8... | collective-permute-start | bytes 98312 | tf_op jit(solution)/shard_map/ppermute | solution.py:186
  164.3 40.2 %collective-permute-start.13 = (bf16[64,1,2,128]{3,1,2,0:T(2,128)(2,1)S(1)}, bf16[64,1,2,128]{3,1,2,0:T(2,128)(2,1)S(1)}, u32[]{:S(2)}, u32[]{:S(2)}) collective-permute-start(bf16[64,1,2,128]{3,1,2,0:T(2,128)(2,1)S(1)} %get-tuple-element.69), channel_id=1, source_target_pairs={{128,0},{129,1},{130,2},{131,3},{132,4},{133,5},{134,6},{135,7},{1... | collective-permute-start | bytes 98312 | tf_op jit(solution)/shard_map/ppermute | solution.py:187
  204.5 10.1 %copy-start.13 = (bf16[64,16,2,128]{3,1,2,0:T(8,128)(2,1)S(1)}, bf16[64,16,2,128]{3,1,2,0:T(8,128)(2,1)}, u32[]{:S(2)}) copy-start(bf16[64,16,2,128]{3,1,2,0:T(8,128)(2,1)} %get-tuple-element.36) | copy-start | bytes 1572868
  204.5 9.5 %copy-start.16 = (bf16[64,1,2,128]{3,1,2,0:T(2,128)(2,1)}, bf16[64,1,2,128]{3,1,2,0:T(2,128)(2,1)S(1)}, u32[]{:S(2)}) copy-start(bf16[64,1,2,128]{3,1,2,0:T(2,128)(2,1)S(1)} %collective-permute-done.12) | copy-start | bytes 98308
  204.5 9.5 %copy-start.18 = (bf16[64,1,2,128]{3,1,2,0:T(2,128)(2,1)}, bf16[64,1,2,128]{3,1,2,0:T(2,128)(2,1)S(1)}, u32[]{:S(2)}) copy-start(bf16[64,1,2,128]{3,1,2,0:T(2,128)(2,1)S(1)} %collective-permute-done.13) | copy-start | bytes 98308
  206.6 13.7 %collective-permute-start.15 = (bf16[64,18,1,128]{3,0,2,1:T(8,128)(2,1)}, bf16[64,18,1,128]{3,0,2,1:T(8,128)(2,1)}, u32[]{:S(2)}, u32[]{:S(2)}) collective-permute-start(bf16[64,18,1,128]{3,0,2,1:T(8,128)(2,1)} %copy.402), channel_id=1, source_target_pairs={{1,0},{2,1},{3,2},{4,3},{5,4},{6,5},{7,6},{8,7},{9,8},{10,9},{11,1... | collective-permute-start | bytes 884744 | tf_op jit(solution)/shard_map/ppermute | solution.py:187
  208.5 12.9 %collective-permute-start.14 = (bf16[64,18,1,128]{3,0,2,1:T(8,128)(2,1)}, bf16[64,18,1,128]{3,0,2,1:T(8,128)(2,1)}, u32[]{:S(2)}, u32[]{:S(2)}) collective-permute-start(bf16[64,18,1,128]{3,0,2,1:T(8,128)(2,1)} %copy.401), channel_id=1, source_target_pairs={{0,1},{1,2},{2,3},{3,4},{4,5},{5,6},{6,7},{7,8},{8,9},{9,10},{10,1... | collective-permute-start | bytes 884744 | tf_op jit(solution)/shard_map/ppermute | solution.py:186
  (23 other events, 72.6 us)

commit v2 on v1

v2 whole, which is shorter than its diff:
```python
import functools
import math

import jax
import jax.numpy as jnp
import numpy as np
from jax import lax
from jax.experimental import pallas as pl
from jax.experimental.pallas import tpu as pltpu
from jax.sharding import PartitionSpec as P

MESH = pl.DeviceIdType.MESH
F32 = jnp.float32
BF16 = jnp.bfloat16
VMEM = pl.BlockSpec(memory_space=pltpu.VMEM)
VMEM_BYTES = 48 * 2**20


def place():
    return lax.axis_index("grp"), lax.axis_index("gx") * 4 + lax.axis_index("gy")


def roll_z(value, step):
    lane = lax.broadcasted_iota(jnp.int32, value.shape, value.ndim - 1)
    edge = 0 if step > 0 else 127
    return jnp.where(lane % 128 == edge, 0.0, pltpu.roll(value, step % 128, value.ndim - 1))


def solver_kernel(
    sc, vel, adv, net, tgt,
    halo, held, wide, seen, inc, gains,
    a_send, a_recv, b_send, b_recv, n_send, n_recv, c_send, c_recv,
):
    g, s = place()
    diffusivity = jnp.where(g == 0, jnp.float32(0.08), jnp.float32(0.12))

    def device(step, field):
        other = lax.rem(s + step + 128, 128)
        return (field, other // 4, lax.rem(other, 4))

    partners = [(d, f) for d in (-2, -1, 0, 1, 2) for f in (0, 1) if (d, f) != (0, 0)]
    def partner(d, f):
        return device(d, g if f == 0 else 1 - g)

    barrier = pltpu.get_barrier_semaphore()
    for d, f in partners:
        pl.semaphore_signal(barrier, inc=1, device_id=partner(d, f), device_id_type=MESH)
    pl.semaphore_wait(barrier, len(partners))

    def send(src, dst, ssem, rsem, d, f):
        return pltpu.make_async_remote_copy(
            src, dst, ssem, rsem, device_id=partner(d, f), device_id_type=MESH
        )

    first = [
        send(sc, halo.at[0], a_send.at[0], a_recv.at[0], 1, 0),
        send(sc, halo.at[1], a_send.at[1], a_recv.at[1], -1, 0),
    ]
    for copy in first:
        copy.start()

    speed = [[vel[pl.ds(64 * d + y, 32, stride=2), :] for y in range(2)] for d in range(3)]
    row = lax.broadcasted_iota(jnp.int32, (32, 128), 0)

    def step(centre, below, above, y):
        plus_x = jnp.where(row == 31, 0.0, pltpu.roll(centre, 31, 0))
        minus_x = jnp.where(row == 0, 0.0, pltpu.roll(centre, 1, 0))
        plus_z = roll_z(centre, -1)
        minus_z = roll_z(centre, 1)
        laplace = plus_x + minus_x + above + below + plus_z + minus_z - 6.0 * centre
        advect = (
            speed[0][y] * (plus_x - minus_x)
            + speed[1][y] * (above - below)
            + speed[2][y] * (plus_z - minus_z)
        )
        return centre + diffusivity * laplace - 0.5 * advect

    own = [sc[pl.ds(y, 32, stride=2), :] for y in range(2)]
    for copy in first:
        copy.wait_recv()
    below = jnp.where(s == 0, 0.0, halo[0, pl.ds(1, 32, stride=2), :])
    above = jnp.where(s == 127, 0.0, halo[1, pl.ds(0, 32, stride=2), :])
    stepped = [step(own[0], below, own[1], 0), step(own[1], own[0], above, 1)]
    for y in range(2):
        held[y] = stepped[y]
        wide[y] = stepped[y].astype(BF16)

    second = [
        send(held.at[1], gains.at[0], b_send.at[0], b_recv.at[0], 1, 0),
        send(held.at[0], gains.at[1], b_send.at[1], b_recv.at[1], -1, 0),
    ]
    third = []
    for index, (d, f) in enumerate(partners):
        field = g
        if abs(d) == 2:
            y = 1 if d > 0 else 0
            src, dst = wide.at[y], seen.at[2 - d, field, y]
        else:
            src, dst = wide, seen.at[2 - d, field]
        third.append(send(src, dst, n_send.at[index], n_recv.at[index], d, f))
    arrivals = []
    for index, (d, f) in enumerate(partners):
        field = g if f == 0 else 1 - g
        if abs(d) == 2:
            y = 1 if d > 0 else 0
            src, dst = wide.at[y], seen.at[2 - d, field, y]
        else:
            src, dst = wide, seen.at[2 - d, field]
        arrivals.append(send(src, dst, n_send.at[index], n_recv.at[index], d, f))
    for copy in second:
        copy.start()
    for copy in third:
        copy.start()
    for y in range(2):
        seen[2, g, y] = wide[y]
    net[pl.ds(0, 48), :] = jnp.zeros((48, 128), F32)
    net[pl.ds(35 * 16, 48), :] = jnp.zeros((48, 128), F32)
    tgt[pl.ds(0, 8), :] = jnp.zeros((8, 128), F32)
    tgt[pl.ds(33 * 8, 8), :] = jnp.zeros((8, 128), F32)

    for copy in second:
        copy.wait_recv()
    below = jnp.where(s == 0, 0.0, gains[0])
    above = jnp.where(s == 127, 0.0, gains[1])
    advanced = [
        step(stepped[0], below, stepped[1], 0),
        step(stepped[1], stepped[0], above, 1),
    ]
    for y in range(2):
        adv[pl.ds(y, 32, stride=2), :] = advanced[y]
        inc[g, 1 + y] = advanced[y] - stepped[y]
    fourth, landings = [], []
    for index, (d, f) in enumerate([(0, 1), (1, 0), (1, 1), (-1, 0), (-1, 1)]):
        def ends(field):
            if d == 0:
                return inc.at[g, pl.ds(1, 2)], inc.at[field, pl.ds(1, 2)]
            if d == 1:
                return inc.at[g, 2], inc.at[field, 0]
            return inc.at[g, 1], inc.at[field, 3]
        fourth.append(send(*ends(g), c_send.at[index], c_recv.at[index], d, f))
        landings.append(
            send(*ends(g if f == 0 else 1 - g), c_send.at[index], c_recv.at[index], d, f)
        )
    for copy in fourth:
        copy.start()

    for copy in arrivals:
        copy.wait_recv()
    for field in range(2):
        for yy in range(8):
            slab, y = (yy + 1) // 2, (yy + 1) % 2
            y_at = 2 * s - 3 + yy
            inside = (y_at >= 0) & (y_at < 256)
            value = jnp.where(inside, seen[slab, field, y].astype(F32), 0.0)
            net[pl.ds(48 + field * 8 + yy, 32, stride=16), :] = value
    for copy in landings:
        copy.wait_recv()
    for field in range(2):
        for yy in range(4):
            tgt[pl.ds(8 + yy * 2 + field, 32, stride=8), :] = inc[field, yy]
    for copy in first + second + third + fourth:
        copy.wait_send()


def solve(scalars, velocity):
    dma = pltpu.SemaphoreType.DMA
    return pl.pallas_call(
        solver_kernel,
        out_shape=(
            jax.ShapeDtypeStruct((64, 128), F32),
            jax.ShapeDtypeStruct((38 * 16, 128), F32),
            jax.ShapeDtypeStruct((34 * 8, 128), F32),
        ),
        in_specs=[VMEM, VMEM],
        out_specs=(VMEM, VMEM, VMEM),
        scratch_shapes=[
            pltpu.VMEM((2, 64, 128), F32),
            pltpu.VMEM((2, 32, 128), F32),
            pltpu.VMEM((2, 32, 128), BF16),
            pltpu.VMEM((5, 2, 2, 32, 128), BF16),
            pltpu.VMEM((2, 4, 32, 128), F32),
            pltpu.VMEM((2, 32, 128), F32),
            dma((2,)), dma((2,)), dma((2,)), dma((2,)),
            dma((9,)), dma((9,)), dma((5,)), dma((5,)),
        ],
        compiler_params=pltpu.CompilerParams(
            collective_id=0, has_side_effects=True, vmem_limit_bytes=VMEM_BYTES
        ),
        name="solver",
    )(scalars, velocity)


def gelu_parts(v):
    c = math.sqrt(2.0 / math.pi)
    square = v * v
    t = jnp.tanh(v * (c + (c * 0.044715) * square))
    half = 0.5 + 0.5 * t
    value = v * half
    slope = half + (0.5 * v) * (1.0 - t * t) * (c + (3.0 * c * 0.044715) * square)
    return value, slope


def rows_dot(a, b):
    return lax.dot_general(a, b, (((1,), (1,)), ((), ())), preferred_element_type=F32)


def net_kernel(
    loss_scale,
    net, tgt, w_lift, b_lift, w_mix, w_back, b_mix, w_out, w_outt, b_out, pick,
    packed,
    v3, lifted, slope1, cot, total, total_lift, total_out, sums,
):
    g, s = place()
    x0 = g * 16

    def fill(x, _):
        rows = net[pl.ds(pl.multiple_of((x0 + x) * 16, 16), 16), :]
        v3[x, pl.ds(0, 16), :] = roll_z(rows, 1).astype(BF16)
        v3[x, pl.ds(16, 16), :] = rows.astype(BF16)
        v3[x, pl.ds(32, 16), :] = roll_z(rows, -1).astype(BF16)
        return 0

    lax.fori_loop(0, 22, fill, 0)

    bias1 = jnp.broadcast_to(b_lift[...], (64, 128))
    bias1 = jnp.concatenate([bias1] * 6, axis=0)

    def lift(x, _):
        seen = jnp.concatenate(
            [v3[pl.ds(2 * x, 3)].reshape(144, 128), v3[pl.ds(2 * x + 1, 3)].reshape(144, 128)], axis=1
        )
        pre = jnp.dot(w_lift[...], seen, preferred_element_type=F32)
        for half in range(2):
            value, slope = gelu_parts(pre[:, half * 128 : half * 128 + 128] + bias1)
            lifted[2 * x + half] = value.astype(BF16)
            slope1[2 * x + half] = slope[128:256]
        return 0

    lax.fori_loop(0, 10, lift, 0)

    def clear(ref, first_x, last_x, first_y, last_y):
        @pl.when(g == 0)
        def _():
            for x in first_x:
                ref[x] = jnp.zeros(ref.shape[1:], BF16)

        @pl.when(g == 1)
        def _():
            for x in last_x:
                ref[x] = jnp.zeros(ref.shape[1:], BF16)

        def wipe(rows):
            def body(x, _):
                ref[x, rows, :] = jnp.zeros((rows.size, 128), BF16)
                return 0
            lax.fori_loop(0, ref.shape[0], body, 0)

        @pl.when(s == 0)
        def _():
            wipe(first_y)

        @pl.when(s == 127)
        def _():
            wipe(last_y)

    clear(lifted, (0, 1), (18, 19), pl.ds(0, 128), pl.ds(256, 128))

    bias2 = jnp.broadcast_to(b_mix[...], (64, 128))
    bias_out = jnp.broadcast_to(b_out[...], (16, 128))
    total[...] = jnp.zeros_like(total)
    total_lift[...] = jnp.zeros_like(total_lift)
    total_out[...] = jnp.zeros_like(total_out)
    sums[...] = jnp.zeros_like(sums)

    def gathered(parts):
        return parts[:64] , parts[64:128], parts[128:]

    def summed_z(u):
        before, here, after = gathered(u)
        return roll_z(before, 1) + here + roll_z(after, -1)

    def mix(x, _):
        pieces = [lifted[x + ox] for ox in range(3)]
        seen = jnp.concatenate(
            [
                jnp.concatenate([piece[64 * y : 64 * y + 192] for piece in pieces], axis=0)
                for y in range(4)
            ],
            axis=1,
        )
        u = jnp.dot(w_mix[...], seen, preferred_element_type=F32)
        values, slopes = [], []
        for y in range(4):
            value, slope = gelu_parts(summed_z(u[:, 128 * y : 128 * y + 128]) + bias2)
            values.append(value.astype(BF16))
            slopes.append(slope)
        mixed = jnp.concatenate(values, axis=0)
        slope = jnp.concatenate(slopes, axis=0)
        predicted = jnp.dot(w_out[...], mixed, preferred_element_type=F32) + bias_out
        goal = tgt[pl.ds(pl.multiple_of((x0 + x) * 8, 8), 8), :]
        goal = jnp.concatenate([goal, jnp.zeros((8, 128), F32)], axis=0)
        error = (loss_scale * (predicted - goal)).astype(BF16)
        back = jnp.dot(w_outt[...], error, preferred_element_type=F32)
        cot[x] = (back * slope).astype(BF16)
        own = (x >= 1) & (x <= 16)
        error = jnp.where(own, error.astype(F32), 0.0)
        sums[pl.ds(0, 16), :] += error
        total_out[...] += rows_dot(mixed[64:192], error.astype(BF16))
        return 0

    lax.fori_loop(0, 18, mix, 0)
    clear(cot, (0,), (17,), pl.ds(0, 64), pl.ds(192, 64))

    def grads(x, _):
        near = [lifted[x + 1 + ox] for ox in range(3)]
        mine = cot[x + 1, pl.ds(64, 128), :].astype(F32)
        sums[pl.ds(16, 128), :] += mine
        before = roll_z(mine, -1).astype(BF16)
        after = roll_z(mine, 1).astype(BF16)
        here = cot[x + 1, pl.ds(64, 128), :]
        seen = jnp.concatenate(
            [
                jnp.concatenate([piece[64 * y + 64 : 64 * y + 256] for piece in near], axis=0)
                for y in range(2)
            ],
            axis=1,
        )
        theirs = jnp.concatenate(
            [
                jnp.concatenate([part[64 * y : 64 * y + 64] for part in (before, here, after)], axis=0)
                for y in range(2)
            ],
            axis=1,
        )
        total[...] += rows_dot(seen, theirs)
        pieces = [cot[x + ox] for ox in range(3)]
        seen = jnp.concatenate(
            [
                jnp.concatenate([piece[64 * y : 64 * y + 192] for piece in pieces], axis=0)
                for y in range(2)
            ],
            axis=1,
        )
        u = jnp.dot(w_back[...], seen, preferred_element_type=F32)
        back = jnp.concatenate([summed_z(u[:, :128]), summed_z(u[:, 128:])], axis=0)
        down = (back * slope1[x + 2]).astype(BF16)
        sums[pl.ds(144, 128), :] += down.astype(F32)
        total_lift[...] += rows_dot(down, v3[pl.ds(x + 2, 3)].reshape(144, 128))
        return 0

    lax.fori_loop(0, 16, grads, 0)

    packed[pl.ds(0, 576), :] = total[:, 0:128]
    packed[pl.ds(576, 288), :] = jnp.concatenate(
        [total[pl.ds(0, 288), 128:192], total[pl.ds(288, 288), 128:192]], axis=1
    )
    lift_grad = jnp.zeros((64, 128), F32)
    for y in range(2):
        lift_grad += jnp.dot(
            total_lift[pl.ds(64 * y, 64), :], pick[y],
            preferred_element_type=F32, precision=lax.Precision.HIGHEST,
        )
    def row_sum(first):
        both = sums[pl.ds(first, 64), :] + sums[pl.ds(first + 64, 64), :]
        return jnp.sum(both, axis=1, keepdims=True)

    lane = lax.broadcasted_iota(jnp.int32, (64, 128), 1)
    small = lift_grad
    small = jnp.where(lane == 54, row_sum(144), small)
    small = jnp.where(lane == 55, row_sum(16), small)
    for k in range(2):
        piece = total_out[pl.ds(0, 64), 2 + k : 3 + k] + total_out[pl.ds(64, 64), 4 + k : 5 + k]
        small = jnp.where(lane == 56 + k, piece, small)
    per_row = jnp.sum(sums[pl.ds(0, 8), :], axis=1, keepdims=True)
    pair = per_row[2:4] + per_row[4:6]
    row = lax.broadcasted_iota(jnp.int32, (64, 128), 0)
    for k in range(2):
        small = jnp.where((lane == 58) & (row == k), pair[k : k + 1], small)
    packed[pl.ds(864, 32), :] = jnp.concatenate([small[:32, :64], small[32:, :64]], axis=1)


def local_grads(loss_scale, net, tgt, weights):
    return pl.pallas_call(
        functools.partial(net_kernel, loss_scale),
        out_shape=jax.ShapeDtypeStruct((896, 128), F32),
        in_specs=[VMEM] * (2 + len(weights)),
        out_specs=VMEM,
        scratch_shapes=[
            pltpu.VMEM((22, 48, 128), BF16),
            pltpu.VMEM((20, 384, 128), BF16),
            pltpu.VMEM((20, 128, 128), F32),
            pltpu.VMEM((18, 256, 128), BF16),
            pltpu.VMEM((576, 192), F32),
            pltpu.VMEM((128, 144), F32),
            pltpu.VMEM((128, 16), F32),
            pltpu.VMEM((272, 128), F32),
        ],
        compiler_params=pltpu.CompilerParams(vmem_limit_bytes=VMEM_BYTES),
        name="network",
    )(net, tgt, *weights)


def picks():
    grad = np.zeros((2, 144, 128), np.float32)
    ahead = np.zeros((6, 54, 144), np.float32)
    for ox in range(3):
        for oz in range(3):
            for ch in range(2):
                for oy in range(3):
                    tap = 27 * ch + 9 * ox + 3 * oy + oz
                    for y in range(2):
                        grad[y, ((ox * 3 + oz) * 2 + ch) * 8 + 2 + y + oy, tap] = 1
                    for y in range(6):
                        ahead[y, tap, ((ox * 3 + oz) * 2 + ch) * 8 + y + oy] = 1
    return grad, ahead


def layouts(w_lift, b_lift, w_mix, b_mix, w_out, b_out):
    grad, ahead = picks()
    lift = jnp.einsum("oj,yjc->yoc", w_lift, jnp.asarray(ahead, BF16)).reshape(384, 144)
    taps = w_mix.reshape(64, 64, 9, 3)
    mix = taps.transpose(3, 0, 2, 1).reshape(192, 576)
    back = taps[:, :, ::-1, ::-1].transpose(3, 1, 2, 0).reshape(192, 576)
    out = jnp.zeros((16, 256), BF16)
    for y in range(4):
        out = lax.dynamic_update_slice(out, w_out, (2 * y, 64 * y))
    bias = jnp.tile(b_out, 8)[:, None]
    return (
        lift, b_lift[:, None], mix, back, b_mix[:, None], out, out.T, bias, jnp.asarray(grad),
    )


def total_kernel(buf, out, from_core, mine, from_plane, from_z, s1, r1, s2, r2, s3, r3, s4, r4, s5, r5):
    y_lo = lax.axis_index("grp")
    gx = lax.axis_index("gx")
    gy = lax.axis_index("gy")
    z, x = gx // 4, gx % 4
    y_hi, core = gy // 2, gy % 2
    place = x * 4 + y_hi * 2 + y_lo
    sibling = (y_lo, gx, y_hi * 2 + 1 - core)

    def in_plane(other):
        return (other % 2, z * 4 + other // 4, ((other // 2) % 2) * 2 + core)

    def in_z(other):
        return (y_lo, other * 4 + x, gy)

    barrier = pltpu.get_barrier_semaphore()
    pl.semaphore_signal(barrier, inc=1, device_id=sibling, device_id_type=MESH)

    def greet_plane(j, _):
        pl.semaphore_signal(barrier, inc=1, device_id=in_plane((place + j) % 16), device_id_type=MESH)
        return 0

    def greet_z(j, _):
        pl.semaphore_signal(barrier, inc=1, device_id=in_z((z + j) % 8), device_id_type=MESH)
        return 0

    lax.fori_loop(1, 16, greet_plane, 0)
    lax.fori_loop(1, 8, greet_z, 0)
    pl.semaphore_wait(barrier, 23)

    theirs = pl.multiple_of((1 - core) * 16, 16)
    ours = pl.multiple_of(core * 16, 16)
    swap = pltpu.make_async_remote_copy(
        buf.at[pl.ds(theirs, 16)], from_core, s1, r1, device_id=sibling, device_id_type=MESH
    )
    swap.start()
    swap.wait()

    def add_core(j, _):
        mine[j] = buf[ours + j] + from_core[j]
        return 0

    lax.fori_loop(0, 16, add_core, 0)

    def to_plane(j):
        other = (place + j) % 16
        return pltpu.make_async_remote_copy(
            mine.at[other], from_plane.at[place], s2.at[other], r2.at[place],
            device_id=in_plane(other), device_id_type=MESH,
        )

    def of_plane(j):
        other = (place + j) % 16
        return pltpu.make_async_remote_copy(
            mine.at[other], from_plane.at[other], s2.at[other], r2.at[other],
            device_id=in_plane(other), device_id_type=MESH,
        )

    lax.fori_loop(1, 16, lambda j, _: (to_plane(j).start(), 0)[1], 0)
    from_plane[place] = mine[place]

    def wait_plane(j, _):
        of_plane(j).wait()
        return 0

    lax.fori_loop(1, 16, wait_plane, 0)
    total = from_plane[0]
    for j in range(1, 16):
        total = total + from_plane[j]
    from_z[z] = total

    def to_z(j):
        other = (z + j) % 8
        return pltpu.make_async_remote_copy(
            from_z.at[z], from_z.at[z], s3.at[other], r3.at[z], device_id=in_z(other), device_id_type=MESH
        )

    def of_z(j):
        other = (z + j) % 8
        return pltpu.make_async_remote_copy(
            from_z.at[other], from_z.at[other], s3.at[other], r3.at[other], device_id=in_z(other), device_id_type=MESH
        )

    lax.fori_loop(1, 8, lambda j, _: (to_z(j).start(), 0)[1], 0)

    def wait_z(j, _):
        of_z(j).wait()
        return 0

    lax.fori_loop(1, 8, wait_z, 0)
    total = from_z[0]
    for j in range(1, 8):
        total = total + from_z[j]
    out[ours + place] = total

    def gather(j):
        other = (place + j) % 16
        return pltpu.make_async_remote_copy(
            out.at[ours + place], out.at[ours + place], s4.at[other], r4.at[place],
            device_id=in_plane(other), device_id_type=MESH,
        )

    def gathered(j):
        other = (place + j) % 16
        return pltpu.make_async_remote_copy(
            out.at[ours + other], out.at[ours + other], s4.at[other], r4.at[other],
            device_id=in_plane(other), device_id_type=MESH,
        )

    def hand(j):
        other = (place + j) % 16
        return pltpu.make_async_remote_copy(
            out.at[ours + other], out.at[ours + other], s5.at[other], r5.at[other],
            device_id=sibling, device_id_type=MESH,
        )

    def handed(j):
        other = (place + j) % 16
        return pltpu.make_async_remote_copy(
            out.at[theirs + other], out.at[theirs + other], s5.at[other], r5.at[other],
            device_id=sibling, device_id_type=MESH,
        )

    lax.fori_loop(1, 16, lambda j, _: (gather(j).start(), 0)[1], 0)
    hand(0).start()

    def pass_on(j, _):
        gathered(j).wait_recv()
        hand(j).start()
        return 0

    lax.fori_loop(1, 16, pass_on, 0)

    def finish(j, _):
        handed(j).wait_recv()
        hand(j).wait_send()
        return 0

    lax.fori_loop(0, 16, finish, 0)
    lax.fori_loop(1, 16, lambda j, _: (gather(j).wait_send(), 0)[1], 0)


def all_total(buf):
    chunk = buf.shape[1:]
    dma = pltpu.SemaphoreType.DMA
    vmem = pl.BlockSpec(memory_space=pltpu.VMEM)
    return pl.pallas_call(
        total_kernel,
        out_shape=jax.ShapeDtypeStruct(buf.shape, jnp.float32),
        in_specs=[vmem],
        out_specs=vmem,
        scratch_shapes=[
            pltpu.VMEM((16,) + chunk, jnp.float32),
            pltpu.VMEM((16,) + chunk, jnp.float32),
            pltpu.VMEM((16,) + chunk, jnp.float32),
            pltpu.VMEM((8,) + chunk, jnp.float32),
            dma, dma, dma((16,)), dma((16,)), dma((8,)), dma((8,)),
            dma((16,)), dma((16,)), dma((16,)), dma((16,)),
        ],
        compiler_params=pltpu.CompilerParams(collective_id=1, has_side_effects=True, vmem_limit_bytes=40 * 2**20),
        name="total",
    )(buf)


def on_device(scalars, velocity, w_lift, b_lift, w_mix, b_mix, w_out, b_out):
    total_cells = scalars.size * lax.axis_size("gx") * lax.axis_size("gy")
    loss_scale = 2.0 / math.sqrt(total_cells)
    advanced, net, target = solve(scalars.reshape(64, 128), velocity.reshape(192, 128))
    weights = layouts(w_lift, b_lift, w_mix, b_mix, w_out, b_out)
    packed = local_grads(loss_scale, net, target, weights)
    summed = all_total(packed.reshape(32, 7, 4, 128)).reshape(896, 128)
    first = summed[:576].reshape(9, 64, 2, 64)
    last = summed[576:864].reshape(288, 2, 64).transpose(1, 0, 2).reshape(9, 64, 1, 64)
    mix_grad = jnp.concatenate([first, last], axis=2).transpose(3, 1, 0, 2).reshape(64, 1728)
    small = summed[864:].reshape(32, 2, 64).transpose(1, 0, 2).reshape(64, 64)
    return (
        advanced.reshape(scalars.shape),
        small[:, :54],
        small[:, 54],
        mix_grad,
        small[:, 55],
        small[:, 56:58].T,
        small[:2, 58],
    )


def solution(mesh):
    cells = P("grp", None, ("gx", "gy"), None)
    in_specs = (cells, P(None, None, ("gx", "gy"), None)) + (P(),) * 6
    out_specs = (cells,) + (P(),) * 6
    return jax.shard_map(
        on_device, mesh=mesh, in_specs=in_specs, out_specs=out_specs, check_vma=False
    )
```

time: 323 us -> 98.7 us (0.31); the launches traced: 319 us -> 98.5 us
  matrix products: 131 us -> 1.17 us
  starting transfers between devices: 51.7 us -> 0 us
  local copies, waits for them, and re-layouts: 54.5 us -> 16.4 us
  Pallas kernels: 47.1 us -> 79.4 us
  other arithmetic: 17.3 us -> 0.66 us
  waiting for transfers between devices: 11 us -> 0 us
  blocking collectives: 5.05 us -> 0 us
    conv_general_dilated x3 -> x0, matrix products: 86.1 us -> none  [convolve(): lax.conv_general_dilated(padded[None], kernel, (1, 1, 1), ((0, 0), (0, 0)...]
    pallas_call x0 -> x2, Pallas kernels: none -> 53.7 us  [the longest x1 28.3 us: local_grads(): pl.pallas_call(functools.partial(net_kernel, loss_scale), out_shape=jax.S...]
    ppermute x16 -> x0, starting transfers between devices: 47.8 us -> none  [the longest x8 34.4 us: extended(): before = lax.ppermute(last, axis, up)]
    dot_general x57 -> x1, matrix products: 44.8 us -> 1.17 us  [layouts(): jnp.einsum('oj,yjc->yoc', w_lift, jnp.asarray(ahead, BF16))]
    pallas_call x1, Pallas kernels: 47.1 us -> 25.7 us  [all_total(): pl.pallas_call(total_kernel, out_shape=jax.ShapeDtypeStruct(buf.shape, jn...]
    broadcast_in_dim x3 -> x2, local copies, waits for them, and re-layouts: 21.5 us -> 0.84 us  [the longest x1 0.75 us: layouts(): b_lift[:, None]]
    ppermute x16 -> x0, waiting for transfers between devices: 11 us -> none  [the longest x8 11 us: extended(): after = lax.ppermute(leading, axis, down)]
    slice x20 -> x5, local copies, waits for them, and re-layouts: 9.14 us -> 1.42 us  [the longest x1 0.7 us: on_device(): small[:, 55]]
  transfers between devices with their start and end apart: 17 -> 0, of which waited for: 3 -> 0; matrix products, arithmetic and copies ran while one was open for 44% -> 0% of each run, Pallas kernels for 0% -> 0%
where the time goes in v2:
time: 98.7 us; the launch traced here: 98.5 us
  Pallas kernels  79.4 us (80%)
  local copies, waits for them, and re-layouts  16.4 us (17%)
  matrix products  1.17 us (1%)
    pallas_call x1, Pallas kernels, local_grads(): pl.pallas_call(functools.partial(net_kernel, loss_scale), out_shape=jax.S...  28.3 us
    pallas_call x1, Pallas kernels, all_total(): pl.pallas_call(total_kernel, out_shape=jax.ShapeDtypeStruct(buf.shape, jn...  25.7 us
    pallas_call x1, Pallas kernels, solve(): pl.pallas_call(solver_kernel, out_shape=(jax.ShapeDtypeStruct((64, 128),...  25.4 us
    unnamed x21, local copies, waits for them, and re-layouts  6.18 us
    dynamic_update_slice x5, local copies, waits for them, and re-layouts, layouts(): out = lax.dynamic_update_slice(out, w_out, (2 * y, 64 * y))  2.37 us

profile of v2, /device:TPU:1, one launch (start us, length us, event | category | flops | bytes accessed | tf_op | source)
XLA Modules:
  0.0 98.5 jit_solution(16842157971481289429)
XLA Ops:
  0.7 0.9 copy-done.2
  1.5 0.8 copy-done.3
  2.3 25.4 %solver.1 = (f32[64,128]{1,0:T(8,128)S(1)}, f32[608,128]{1,0:T(8,128)S(1)}, f32[272,128]{1,0:T(8,128)S(1)}) custom-call(f32[64,128]{1,0:T(8,128)S(1)} %bitcast.42, f32[192,128]{1,0:T(8,128)S(1)} %bitcast.40), custom_call_target="tpu_custom_call" | custom-call | tf_op jit(solution)/shard_map/solver/pallas_call | solution.py:167
  27.7 1.2 %fusion = bf16[6,144,64]{1,2,0:T(8,128)(2,1)S(1)} fusion(bf16[6,54,144]{2,1,0:T(8,128)(2,1)} %constant.8.clone, bf16[64,54]{0,1:T(8,128)(2,1)S(1)} %copy-done), kind=kOutput, calls=%fused_computation.4 | convolution fusion | flops 5971968 | bytes 210816 | tf_op jit(solution)/shard_map/oj,yjc->yoc/dot_general | solution.py:420
  28.9 0.7 copy.55.b_lift
  29.6 1.2 %copy.48 = bf16[64,1728]{0,1:T(8,128)(2,1)S(1)} copy(bf16[64,1728]{1,0:T(8,128)(2,1)} %param.14) | data formatting | bytes 442368 | tf_op args[4]
  30.9 0.3 reshape.64
  31.1 1.4 %copy.69 = bf16[3,64,9,64]{3,2,1,0:T(8,128)(2,1)S(1)} copy(bf16[3,64,9,64]{1,0,2,3:T(4,128)(2,1)S(1)} %bitcast.43) | data formatting | bytes 442368 | tf_op jit(solution)/shard_map/reshape | solution.py:422
  32.6 0.4 reshape.76.w_mix
  33.0 1.5 %rev.3 = bf16[64,64,9,3]{0,3,2,1:T(4,128)(2,1)S(1)} reverse(bf16[64,64,9,3]{0,3,2,1:T(4,128)(2,1)S(1)} %reshape.64), dimensions={2,3} | reverse | bytes 442368 | tf_op jit(solution)/shard_map/rev | solution.py:423
  34.6 0.1 copy.70
  34.7 0.4 reshape.77.w_back
  35.2 0.1 copy.58.b_mix
  35.3 0.1 copy.51
  35.4 0.8 dynamic_update_slice.13
  36.2 0.8 dynamic_update_slice.14
  37.0 0.7 dynamic_update_slice.15
  37.9 28.3 %network.1 = f32[896,128]{1,0:T(8,128)S(1)} custom-call(f32[608,128]{1,0:T(8,128)S(1)} %get-tuple-element.11.net, f32[272,128]{1,0:T(8,128)S(1)} %get-tuple-element.12.tgt, bf16[384,144]{1,0:T(8,128)(2,1)S(1)} %bitcast.38, f32[64,1]{1,0:T(8,128)S(1)} %copy.55.b_lift, bf16[192,576]{1,0:T(8,128)(2,1)S(1)} %reshape.76.w_mix, ...), custom_call_target="tpu_custom_call" | custom-call | tf_op jit(solution)/shard_map/network/pallas_call | solution.py:383
  66.2 25.7 %total.1 = f32[32,7,4,128]{3,2,1,0:T(4,128)S(1)} custom-call(f32[32,7,4,128]{3,2,1,0:T(4,128)S(1)} %bitcast.37), custom_call_target="tpu_custom_call" | custom-call | tf_op jit(solution)/shard_map/total/pallas_call | solution.py:579
  91.9 0.1 reshape.69
  92.0 0.7 copy.66
  92.7 0.7 slice_reduce_fusion
  93.4 0.1 copy.73
  93.5 0.2 copy.63
  93.7 0.4 reshape.71
  94.1 0.7 maximum_bitcast_fusion
  94.8 0.2 copy.65
  95.0 0.4 reshape.74
  95.4 1.1 %copy.67 = f32[64,1728]{1,0:T(8,128)} copy(f32[64,1728]{0,1:T(8,128)S(1)} %reshape.74) | data formatting | bytes 884736
  96.5 0.6 copy.68
  97.2 0.7 slice_reduce_fusion.2
  97.8 0.6 copy.78
  (21 shorter events, 0.4 us)
Async XLA Ops:
  0.6 27.1 %copy-start = (bf16[64,54]{0,1:T(8,128)(2,1)S(1)}, bf16[64,54]{0,1:T(8,128)(2,1)}, u32[]{:S(2)}) copy-start(bf16[64,54]{0,1:T(8,128)(2,1)} %param.12) | copy-start | bytes 20740
  0.6 0.9 copy-start.2
  1.5 0.8 copy-start.3
  34.5 0.7 copy-start.4
  34.5 0.7 copy-start.5
  34.5 3.3 %copy-start.6 = (f32[2]{0:T(128)S(1)}, f32[2]{0:T(128)}, u32[]{:S(2)}) copy-start(f32[2]{0:T(128)} %param.17) | copy-start | bytes 28
  34.5 3.3 %copy-start.1 = (f32[2,144,128]{2,1,0:T(8,128)S(1)}, f32[2,144,128]{2,1,0:T(8,128)}, u32[]{:S(2)}) copy-start(f32[2,144,128]{2,1,0:T(8,128)} %constant.20.clone.pick) | copy-start | bytes 442372

commit v3 on v2

v3 whole, which is shorter than its diff:
```python
import functools
import math

import jax
import jax.numpy as jnp
import numpy as np
from jax import lax
from jax.experimental import pallas as pl
from jax.experimental.pallas import tpu as pltpu
from jax.sharding import PartitionSpec as P

MESH = pl.DeviceIdType.MESH
F32 = jnp.float32
BF16 = jnp.bfloat16
VMEM = pl.BlockSpec(memory_space=pltpu.VMEM)
VMEM_BYTES = 62 * 2**20


def place():
    return lax.axis_index("grp"), lax.axis_index("gx") * 4 + lax.axis_index("gy")


def roll_z(value, step):
    lane = lax.broadcasted_iota(jnp.int32, value.shape, value.ndim - 1)
    edge = 0 if step > 0 else 127
    return jnp.where(lane % 128 == edge, 0.0, pltpu.roll(value, step % 128, value.ndim - 1))


def solver(
    ring, prepare_mix, prepare_lift, prepare_back,
    sc, vel, adv, net, tgt,
    halo, held, wide, seen, inc, gains,
    a_send, a_recv, b_send, b_recv, n_send, n_recv, c_send, c_recv,
):
    g, s = place()
    diffusivity = jnp.where(g == 0, jnp.float32(0.08), jnp.float32(0.12))

    def device(step, field):
        other = lax.rem(s + step + 128, 128)
        return (field, other // 4, lax.rem(other, 4))

    partners = [(d, f) for d in (-2, -1, 0, 1, 2) for f in (0, 1) if (d, f) != (0, 0)]
    def partner(d, f):
        return device(d, g if f == 0 else 1 - g)

    barrier = pltpu.get_barrier_semaphore()
    for d, f in partners:
        pl.semaphore_signal(barrier, inc=1, device_id=partner(d, f), device_id_type=MESH)
    ring.greet(barrier)
    prepare_mix()
    pl.semaphore_wait(barrier, len(partners) + 23)

    def send(src, dst, ssem, rsem, d, f):
        return pltpu.make_async_remote_copy(
            src, dst, ssem, rsem, device_id=partner(d, f), device_id_type=MESH
        )

    first = [
        send(sc, halo.at[0], a_send.at[0], a_recv.at[0], 1, 0),
        send(sc, halo.at[1], a_send.at[1], a_recv.at[1], -1, 0),
    ]
    for copy in first:
        copy.start()

    speed = [[vel[pl.ds(64 * d + y, 32, stride=2), :] for y in range(2)] for d in range(3)]
    row = lax.broadcasted_iota(jnp.int32, (32, 128), 0)

    def step(centre, below, above, y):
        plus_x = jnp.where(row == 31, 0.0, pltpu.roll(centre, 31, 0))
        minus_x = jnp.where(row == 0, 0.0, pltpu.roll(centre, 1, 0))
        plus_z = roll_z(centre, -1)
        minus_z = roll_z(centre, 1)
        laplace = plus_x + minus_x + above + below + plus_z + minus_z - 6.0 * centre
        advect = (
            speed[0][y] * (plus_x - minus_x)
            + speed[1][y] * (above - below)
            + speed[2][y] * (plus_z - minus_z)
        )
        return centre + diffusivity * laplace - 0.5 * advect

    prepare_lift()
    own = [sc[pl.ds(y, 32, stride=2), :] for y in range(2)]
    for copy in first:
        copy.wait_recv()
    below = jnp.where(s == 0, 0.0, halo[0, pl.ds(1, 32, stride=2), :])
    above = jnp.where(s == 127, 0.0, halo[1, pl.ds(0, 32, stride=2), :])
    stepped = [step(own[0], below, own[1], 0), step(own[1], own[0], above, 1)]
    for y in range(2):
        held[y] = stepped[y]
        wide[y] = stepped[y].astype(BF16)

    second = [
        send(held.at[1], gains.at[0], b_send.at[0], b_recv.at[0], 1, 0),
        send(held.at[0], gains.at[1], b_send.at[1], b_recv.at[1], -1, 0),
    ]
    third = []
    for index, (d, f) in enumerate(partners):
        field = g
        if abs(d) == 2:
            y = 1 if d > 0 else 0
            src, dst = wide.at[y], seen.at[2 - d, field, y]
        else:
            src, dst = wide, seen.at[2 - d, field]
        third.append(send(src, dst, n_send.at[index], n_recv.at[index], d, f))
    arrivals = []
    for index, (d, f) in enumerate(partners):
        field = g if f == 0 else 1 - g
        if abs(d) == 2:
            y = 1 if d > 0 else 0
            src, dst = wide.at[y], seen.at[2 - d, field, y]
        else:
            src, dst = wide, seen.at[2 - d, field]
        arrivals.append(send(src, dst, n_send.at[index], n_recv.at[index], d, f))
    for copy in second:
        copy.start()
    for copy in third:
        copy.start()
    for y in range(2):
        seen[2, g, y] = wide[y]
    net[pl.ds(0, 48), :] = jnp.zeros((48, 128), F32)
    net[pl.ds(35 * 16, 48), :] = jnp.zeros((48, 128), F32)
    tgt[pl.ds(0, 8), :] = jnp.zeros((8, 128), F32)
    tgt[pl.ds(33 * 8, 8), :] = jnp.zeros((8, 128), F32)

    prepare_back()
    for copy in second:
        copy.wait_recv()
    below = jnp.where(s == 0, 0.0, gains[0])
    above = jnp.where(s == 127, 0.0, gains[1])
    advanced = [
        step(stepped[0], below, stepped[1], 0),
        step(stepped[1], stepped[0], above, 1),
    ]
    for y in range(2):
        adv[pl.ds(y, 32, stride=2), :] = advanced[y]
        inc[g, 1 + y] = advanced[y] - stepped[y]
    fourth, landings = [], []
    for index, (d, f) in enumerate([(0, 1), (1, 0), (1, 1), (-1, 0), (-1, 1)]):
        def ends(field):
            if d == 0:
                return inc.at[g, pl.ds(1, 2)], inc.at[field, pl.ds(1, 2)]
            if d == 1:
                return inc.at[g, 2], inc.at[field, 0]
            return inc.at[g, 1], inc.at[field, 3]
        fourth.append(send(*ends(g), c_send.at[index], c_recv.at[index], d, f))
        landings.append(
            send(*ends(g if f == 0 else 1 - g), c_send.at[index], c_recv.at[index], d, f)
        )
    for copy in fourth:
        copy.start()

    for copy in arrivals:
        copy.wait_recv()
    for field in range(2):
        for yy in range(8):
            slab, y = (yy + 1) // 2, (yy + 1) % 2
            y_at = 2 * s - 3 + yy
            inside = (y_at >= 0) & (y_at < 256)
            value = jnp.where(inside, seen[slab, field, y].astype(F32), 0.0)
            net[pl.ds(48 + field * 8 + yy, 32, stride=16), :] = value
    for copy in landings:
        copy.wait_recv()
    for field in range(2):
        for yy in range(4):
            tgt[pl.ds(8 + yy * 2 + field, 32, stride=8), :] = inc[field, yy]
    return first + second + third + fourth


def gelu_parts(v):
    c = math.sqrt(2.0 / math.pi)
    square = v * v
    t = jnp.tanh(v * (c + (c * 0.044715) * square))
    half = 0.5 + 0.5 * t
    value = v * half
    slope = half + (0.5 * v) * (1.0 - t * t) * (c + (3.0 * c * 0.044715) * square)
    return value, slope


def rows_dot(a, b):
    return lax.dot_general(a, b, (((1,), (1,)), ((), ())), preferred_element_type=F32)


class Prepared:
    def __init__(self, w_lift, b_lift, w_mix, b_mix, w_out, b_out, ahead, spread, lift, mix, back, out, outt, bias):
        self.__dict__.update(locals())

    def mix_form(self):
        wide = jnp.concatenate([self.w_mix[...].astype(F32), jnp.zeros((64, 64), F32)], axis=1)
        turned = [wide] + [pltpu.roll(wide, 1792 - oz, 1) for oz in (1, 2)]
        turned = jnp.concatenate([t[:, :1728] for t in turned], axis=0).astype(BF16)
        self.mix[...] = jnp.dot(turned, self.spread[...], preferred_element_type=F32).astype(BF16)

    def lift_form(self):
        flat = self.w_lift[...].astype(F32).T.astype(BF16)
        for y in range(6):
            band = jnp.dot(flat, self.ahead[y], preferred_element_type=F32)
            self.lift[pl.ds(64 * y, 64), :] = band.astype(BF16)
        for index, ref in enumerate((self.b_lift, self.b_mix)):
            self.bias[index] = jnp.broadcast_to(ref[...], (128, 64)).T
        four = jnp.concatenate([self.w_out[...].astype(F32)] * 4, axis=1)
        row = lax.broadcasted_iota(jnp.int32, (16, 256), 0)
        lane = lax.broadcasted_iota(jnp.int32, (16, 256), 1)
        both = jnp.where(row % 2 == 0, four[0:1], four[1:2])
        both = jnp.where(row // 2 == lane // 64, both, 0.0)
        self.out[...] = both.astype(BF16)
        self.outt[...] = both.T.astype(BF16)

    def back_form(self):
        flat = self.mix[...].astype(F32).T
        for oz in range(3):
            tiles = [flat[64 * m : 64 * m + 64, 64 * oz : 64 * oz + 64] for m in range(8, -1, -1)]
            self.back[pl.ds(64 * (2 - oz), 64), :] = jnp.concatenate(tiles, axis=1).astype(BF16)

def network(loss_scale, net, tgt, prepared, unspread_ref, pick, v3, lifted, slope1, mixed, slope2, cot, down, errors, total, buf):
    g, s = place()
    x0 = g * 16

    def fill(x, _):
        rows = net[pl.ds(pl.multiple_of((x0 + x) * 16, 16), 16), :]
        v3[x, pl.ds(0, 16), :] = roll_z(rows, 1).astype(BF16)
        v3[x, pl.ds(16, 16), :] = rows.astype(BF16)
        v3[x, pl.ds(32, 16), :] = roll_z(rows, -1).astype(BF16)
        return 0

    lax.fori_loop(0, 22, fill, 0, unroll=11)

    def lift(x, _):
        seen = jnp.concatenate(
            [v3[pl.ds(2 * x, 3)].reshape(144, 128), v3[pl.ds(2 * x + 1, 3)].reshape(144, 128)], axis=1
        )
        pre = jnp.dot(prepared.lift[...], seen, preferred_element_type=F32)
        bias = jnp.concatenate([prepared.bias[0]] * 6, axis=0)
        for half in range(2):
            value, slope = gelu_parts(pre[:, half * 128 : half * 128 + 128] + bias)
            lifted[2 * x + half] = value.astype(BF16)
            slope1[2 * x + half] = slope[128:256]
        return 0

    lax.fori_loop(0, 10, lift, 0, unroll=5)

    def clear(ref, first_x, last_x, first_y, last_y):
        @pl.when(g == 0)
        def _():
            for x in first_x:
                ref[x] = jnp.zeros(ref.shape[1:], BF16)

        @pl.when(g == 1)
        def _():
            for x in last_x:
                ref[x] = jnp.zeros(ref.shape[1:], BF16)

        def wipe(rows):
            def body(x, _):
                ref[x, rows, :] = jnp.zeros((rows.size, 128), BF16)
                return 0
            lax.fori_loop(0, ref.shape[0], body, 0)

        @pl.when(s == 0)
        def _():
            wipe(first_y)

        @pl.when(s == 127)
        def _():
            wipe(last_y)

    clear(lifted, (0, 1), (18, 19), pl.ds(0, 128), pl.ds(256, 128))

    def summed_z(u):
        return roll_z(u[:64], 1) + u[64:128] + roll_z(u[128:], -1)

    def around(ref, x, first, rows):
        pieces = [ref[x + ox] for ox in range(3)]
        return jnp.concatenate(
            [
                jnp.concatenate([piece[64 * y : 64 * y + 192] for piece in pieces], axis=0)
                for y in range(first, first + rows)
            ],
            axis=1,
        )

    def mix(x, _):
        u = jnp.dot(prepared.mix[...], around(lifted, x, 0, 4), preferred_element_type=F32)
        for y in range(4):
            value, slope = gelu_parts(summed_z(u[:, 128 * y : 128 * y + 128]) + prepared.bias[1])
            mixed[x, pl.ds(64 * y, 64), :] = value.astype(BF16)
            slope2[x, pl.ds(64 * y, 64), :] = slope
        return 0

    lax.fori_loop(0, 18, mix, 0, unroll=3)

    def compare(batch, _):
        first = 6 * batch
        seen = jnp.concatenate([mixed[first + j] for j in range(6)], axis=1)
        row = lax.broadcasted_iota(jnp.int32, (16, 768), 0)
        bias = jnp.where(row % 2 == 0, prepared.b_out[:, 0:1], prepared.b_out[:, 1:2])
        predicted = jnp.dot(prepared.out[...], seen, preferred_element_type=F32) + bias
        goal = jnp.concatenate(
            [tgt[pl.ds(pl.multiple_of((x0 + first + j) * 8, 8), 8), :] for j in range(6)], axis=1
        )
        goal = jnp.concatenate([goal, jnp.zeros((8, 768), F32)], axis=0)
        error = (loss_scale * (predicted - goal)).astype(BF16)
        back = jnp.dot(prepared.outt[...], error, preferred_element_type=F32)
        for j in range(6):
            cot[first + j] = (back[:, 128 * j : 128 * j + 128] * slope2[first + j]).astype(BF16)
            errors[first + j] = error[:, 128 * j : 128 * j + 128]
        return 0

    lax.fori_loop(0, 3, compare, 0)
    clear(cot, (0,), (17,), pl.ds(0, 64), pl.ds(192, 64))
    total[...] = jnp.zeros_like(total)

    def mix_grad(x, mixbias):
        here = cot[x + 1, pl.ds(64, 128), :]
        mine = here.astype(F32)
        before = roll_z(mine, -1).astype(BF16)
        after = roll_z(mine, 1).astype(BF16)
        seen = around(lifted, x + 1, 1, 2)
        theirs = jnp.concatenate(
            [
                jnp.concatenate([part[64 * y : 64 * y + 64] for part in (before, here, after)], axis=0)
                for y in range(2)
            ],
            axis=1,
        )
        total[...] += rows_dot(seen, theirs)
        u = jnp.dot(prepared.back[...], around(cot, x, 0, 2), preferred_element_type=F32)
        back = jnp.concatenate([summed_z(u[:, :128]), summed_z(u[:, 128:])], axis=0)
        down[x] = (back * slope1[x + 2]).astype(BF16)
        return mixbias + mine[:64] + mine[64:]

    mixbias = lax.fori_loop(0, 16, mix_grad, jnp.zeros((64, 128), F32), unroll=4)

    liftbias = jnp.zeros((64, 128), F32)
    outbias = jnp.zeros((8, 128), F32)
    lift_total = jnp.zeros((128, 144), F32)
    out_total = jnp.zeros((128, 16), F32)
    for batch in range(4):
        xs = range(4 * batch, 4 * batch + 4)
        lows = [down[x] for x in xs]
        for low in lows:
            low = low.astype(F32)
            liftbias = liftbias + low[:64] + low[64:]
        ins = jnp.concatenate([v3[x + 2 : x + 5].reshape(144, 128) for x in xs], axis=1)
        lift_total += rows_dot(jnp.concatenate(lows, axis=1), ins)
        errs = [errors[x + 1] for x in xs]
        for err in errs:
            outbias = outbias + err.astype(F32)[:8]
        out_total += rows_dot(
            jnp.concatenate([mixed[x + 1, pl.ds(64, 128), :] for x in xs], axis=1),
            jnp.concatenate(errs, axis=1),
        )

    flat = total[...].T
    high = flat.astype(BF16)
    low = (flat - high.astype(F32)).astype(BF16)
    placed = jnp.dot(jnp.concatenate([high, low], axis=0), unspread_ref[...], preferred_element_type=F32)
    placed = placed[:192] + placed[192:]
    full = placed[:64] + pltpu.roll(placed[64:128], 1, 1) + pltpu.roll(placed[128:], 2, 1)

    small = jnp.zeros((64, 128), F32)
    for y in range(2):
        small += jnp.dot(
            lift_total[64 * y : 64 * y + 64], pick[y],
            preferred_element_type=F32, precision=lax.Precision.HIGHEST,
        )
    lane = lax.broadcasted_iota(jnp.int32, (64, 128), 1)
    row = lax.broadcasted_iota(jnp.int32, (64, 128), 0)
    small = jnp.where(lane == 118, jnp.sum(liftbias, axis=1, keepdims=True), small)
    small = jnp.where(lane == 119, jnp.sum(mixbias, axis=1, keepdims=True), small)
    for k in range(2):
        piece = out_total[:64, 2 + k : 3 + k] + out_total[64:, 4 + k : 5 + k]
        small = jnp.where(lane == 120 + k, piece, small)
    per_row = jnp.sum(outbias, axis=1, keepdims=True)
    pair = per_row[2:4] + per_row[4:6]
    for k in range(2):
        small = jnp.where((lane == 122) & (row == k), pair[k : k + 1], small)
    full = jnp.concatenate([full[:, :1664], full[:, 1664:] + small], axis=1)
    for c in range(32):
        at, half = 4 * (c // 2), 896 * (c % 2)
        buf[c] = full[at : at + 4, half : half + 896]

class Ring:
    def __init__(self):
        y_lo = lax.axis_index("grp")
        gx = lax.axis_index("gx")
        gy = lax.axis_index("gy")
        self.z, self.x = gx // 4, gx % 4
        self.y_hi, self.core = gy // 2, gy % 2
        self.y_lo, self.gx, self.gy = y_lo, gx, gy
        self.place = self.x * 4 + self.y_hi * 2 + y_lo
        self.sibling = (y_lo, gx, self.y_hi * 2 + 1 - self.core)

    def in_plane(self, other):
        return (other % 2, self.z * 4 + other // 4, ((other // 2) % 2) * 2 + self.core)

    def in_z(self, other):
        return (self.y_lo, other * 4 + self.x, self.gy)

    def greet(self, barrier):
        pl.semaphore_signal(barrier, inc=1, device_id=self.sibling, device_id_type=MESH)

        def greet_plane(j, _):
            other = self.in_plane((self.place + j) % 16)
            pl.semaphore_signal(barrier, inc=1, device_id=other, device_id_type=MESH)
            return 0

        def greet_z(j, _):
            other = self.in_z((self.z + j) % 8)
            pl.semaphore_signal(barrier, inc=1, device_id=other, device_id_type=MESH)
            return 0

        lax.fori_loop(1, 16, greet_plane, 0)
        lax.fori_loop(1, 8, greet_z, 0)


def all_sum(ring, buf, out, from_core, mine, from_plane, from_z, s1, r1, s2, r2, s3, r3, s4, r4, s5, r5):
    place, z, core, sibling = ring.place, ring.z, ring.core, ring.sibling
    in_plane, in_z = ring.in_plane, ring.in_z
    theirs = pl.multiple_of((1 - core) * 16, 16)
    ours = pl.multiple_of(core * 16, 16)
    swap = pltpu.make_async_remote_copy(
        buf.at[pl.ds(theirs, 16)], from_core, s1, r1, device_id=sibling, device_id_type=MESH
    )
    swap.start()
    swap.wait()

    def add_core(j, _):
        mine[j] = buf[ours + j] + from_core[j]
        return 0

    lax.fori_loop(0, 16, add_core, 0)

    def to_plane(j):
        other = (place + j) % 16
        return pltpu.make_async_remote_copy(
            mine.at[other], from_plane.at[place], s2.at[other], r2.at[place],
            device_id=in_plane(other), device_id_type=MESH,
        )

    def of_plane(j):
        other = (place + j) % 16
        return pltpu.make_async_remote_copy(
            mine.at[other], from_plane.at[other], s2.at[other], r2.at[other],
            device_id=in_plane(other), device_id_type=MESH,
        )

    lax.fori_loop(1, 16, lambda j, _: (to_plane(j).start(), 0)[1], 0)
    from_plane[place] = mine[place]

    def wait_plane(j, _):
        of_plane(j).wait()
        return 0

    lax.fori_loop(1, 16, wait_plane, 0)
    total = from_plane[0]
    for j in range(1, 16):
        total = total + from_plane[j]
    from_z[z] = total

    def to_z(j):
        other = (z + j) % 8
        return pltpu.make_async_remote_copy(
            from_z.at[z], from_z.at[z], s3.at[other], r3.at[z], device_id=in_z(other), device_id_type=MESH
        )

    def of_z(j):
        other = (z + j) % 8
        return pltpu.make_async_remote_copy(
            from_z.at[other], from_z.at[other], s3.at[other], r3.at[other], device_id=in_z(other), device_id_type=MESH
        )

    lax.fori_loop(1, 8, lambda j, _: (to_z(j).start(), 0)[1], 0)

    def wait_z(j, _):
        of_z(j).wait()
        return 0

    lax.fori_loop(1, 8, wait_z, 0)
    total = from_z[0]
    for j in range(1, 8):
        total = total + from_z[j]
    out[ours + place] = total

    def gather(j):
        other = (place + j) % 16
        return pltpu.make_async_remote_copy(
            out.at[ours + place], out.at[ours + place], s4.at[other], r4.at[place],
            device_id=in_plane(other), device_id_type=MESH,
        )

    def gathered(j):
        other = (place + j) % 16
        return pltpu.make_async_remote_copy(
            out.at[ours + other], out.at[ours + other], s4.at[other], r4.at[other],
            device_id=in_plane(other), device_id_type=MESH,
        )

    def hand(j):
        other = (place + j) % 16
        return pltpu.make_async_remote_copy(
            out.at[ours + other], out.at[ours + other], s5.at[other], r5.at[other],
            device_id=sibling, device_id_type=MESH,
        )

    def handed(j):
        other = (place + j) % 16
        return pltpu.make_async_remote_copy(
            out.at[theirs + other], out.at[theirs + other], s5.at[other], r5.at[other],
            device_id=sibling, device_id_type=MESH,
        )

    lax.fori_loop(1, 16, lambda j, _: (gather(j).start(), 0)[1], 0)
    hand(0).start()

    def pass_on(j, _):
        gathered(j).wait_recv()
        hand(j).start()
        return 0

    lax.fori_loop(1, 16, pass_on, 0)

    def finish(j, _):
        handed(j).wait_recv()
        hand(j).wait_send()
        return 0

    lax.fori_loop(0, 16, finish, 0)
    lax.fori_loop(1, 16, lambda j, _: (gather(j).wait_send(), 0)[1], 0)


def picks():
    grad = np.zeros((2, 144, 128), np.float32)
    ahead = np.zeros((6, 54, 144), np.float32)
    for ox in range(3):
        for oz in range(3):
            for ch in range(2):
                for oy in range(3):
                    tap = 27 * ch + 9 * ox + 3 * oy + oz
                    for y in range(2):
                        grad[y, ((ox * 3 + oz) * 2 + ch) * 8 + 2 + y + oy, 64 + tap] = 1
                    for y in range(6):
                        ahead[y, tap, ((ox * 3 + oz) * 2 + ch) * 8 + y + oy] = 1
    return grad, ahead


def main_kernel(
    loss_scale,
    sc_hbm, vel_hbm, w_mix_hbm, spread_hbm, w_lift_hbm, ahead_hbm, b_lift_hbm, b_mix_hbm, w_out_hbm, b_out_hbm,
    unspread_hbm, pick_hbm,
    adv, out,
    sc, vel, w_mix, spread, w_lift, ahead, b_lift, b_mix, w_out, b_out, unspread, pick,
    load, lift_w, mix_w, back_w, out_w, outt_w, bias,
    net, tgt, halo, held, wide, seen, inc, gains,
    v3, lifted, slope1, mixed, slope2, cot, down, errors, total, buf,
    from_core, mine, from_plane, from_z,
    a_send, a_recv, b_send, b_recv, n_send, n_recv, c_send, c_recv,
    *sums,
):
    pairs = (
        (sc_hbm, sc), (vel_hbm, vel), (w_mix_hbm, w_mix), (spread_hbm, spread), (w_lift_hbm, w_lift),
        (ahead_hbm, ahead), (b_lift_hbm, b_lift), (b_mix_hbm, b_mix), (w_out_hbm, w_out), (b_out_hbm, b_out),
        (unspread_hbm, unspread), (pick_hbm, pick),
    )
    loads = [pltpu.make_async_copy(*pair, load.at[j]) for j, pair in enumerate(pairs)]
    for copy in loads:
        copy.start()
    ring = Ring()
    prepared = Prepared(
        w_lift, b_lift, w_mix, b_mix, w_out, b_out, ahead, spread, lift_w, mix_w, back_w, out_w, outt_w, bias
    )

    def prepare_mix():
        for copy in loads[2:4]:
            copy.wait()
        prepared.mix_form()
        for copy in loads[:2]:
            copy.wait()

    def prepare_lift():
        for copy in loads[4:10]:
            copy.wait()
        prepared.lift_form()

    sent = solver(
        ring, prepare_mix, prepare_lift, prepared.back_form,
        sc, vel, adv, net, tgt, halo, held, wide, seen, inc, gains,
        a_send, a_recv, b_send, b_recv, n_send, n_recv, c_send, c_recv,
    )
    for copy in loads[10:]:
        copy.wait()
    network(
        loss_scale, net, tgt, prepared, unspread, pick,
        v3, lifted, slope1, mixed, slope2, cot, down, errors, total, buf,
    )
    for copy in sent:
        copy.wait_send()
    all_sum(ring, buf, out, from_core, mine, from_plane, from_z, *sums)


def finish_kernel(adv_in, out, adv, mix, lift, liftbias, mixbias, out_grad, outbias):
    adv[...] = adv_in[...]
    for r in range(16):
        mix[pl.ds(4 * r, 4), pl.ds(0, 896)] = out[2 * r]
        mix[pl.ds(4 * r, 4), pl.ds(896, 832)] = out[2 * r + 1][:, :832]
    last = jnp.concatenate([out[2 * r + 1][:, 768:] for r in range(16)], axis=0)
    turned = last.T
    lift[...] = turned[64:118]
    liftbias[...] = turned[118:119]
    mixbias[...] = turned[119:120]
    out_grad[...] = turned[120:122]
    outbias[...] = turned[122:123, :2]


def train(loss_scale, scalars, velocity, w_lift, b_lift, w_mix, b_mix, w_out, b_out):
    dma = pltpu.SemaphoreType.DMA
    hbm = pl.BlockSpec(memory_space=pltpu.HBM)
    pick, ahead = picks()
    spread = np.zeros((64, 9, 3, 9, 64), np.float32)
    for m in range(9):
        for i in range(64):
            spread[i, m, 0, m, i] = 1
    spread = spread.reshape(1728, 576)
    unspread = np.zeros((576, 1792), np.float32)
    unspread[:, :1728] = spread.T
    chunk = (4, 896)

    def vmem(*shape, dtype=F32):
        return pltpu.VMEM(shape, dtype)

    adv, out = pl.pallas_call(
        functools.partial(main_kernel, loss_scale),
        out_shape=(jax.ShapeDtypeStruct((64, 128), F32), jax.ShapeDtypeStruct((32,) + chunk, F32)),
        in_specs=[hbm] * 12,
        out_specs=(VMEM, VMEM),
        scratch_shapes=[
            vmem(64, 128), vmem(192, 128), vmem(64, 1728, dtype=BF16), vmem(1728, 576, dtype=BF16),
            vmem(54, 64, dtype=BF16), vmem(6, 54, 144, dtype=BF16), vmem(1, 64), vmem(1, 64),
            vmem(2, 64, dtype=BF16), vmem(1, 2), vmem(576, 1792, dtype=BF16), vmem(2, 144, 128), dma((12,)),
            vmem(384, 144, dtype=BF16), vmem(192, 576, dtype=BF16), vmem(192, 576, dtype=BF16),
            vmem(16, 256, dtype=BF16), vmem(256, 16, dtype=BF16), vmem(2, 64, 128),
            vmem(38 * 16, 128), vmem(34 * 8, 128),
            vmem(2, 64, 128), vmem(2, 32, 128), vmem(2, 32, 128, dtype=BF16),
            vmem(5, 2, 2, 32, 128, dtype=BF16), vmem(2, 4, 32, 128), vmem(2, 32, 128),
            vmem(22, 48, 128, dtype=BF16), vmem(20, 384, 128, dtype=BF16), vmem(20, 128, 128),
            vmem(18, 256, 128, dtype=BF16), vmem(18, 256, 128), vmem(18, 256, 128, dtype=BF16),
            vmem(16, 128, 128, dtype=BF16), vmem(18, 16, 128, dtype=BF16), vmem(576, 192),
            vmem(32, *chunk), vmem(16, *chunk), vmem(16, *chunk), vmem(16, *chunk), vmem(8, *chunk),
            dma((2,)), dma((2,)), dma((2,)), dma((2,)),
            dma((9,)), dma((9,)), dma((5,)), dma((5,)),
            dma, dma, dma((16,)), dma((16,)), dma((8,)), dma((8,)),
            dma((16,)), dma((16,)), dma((16,)), dma((16,)),
        ],
        compiler_params=pltpu.CompilerParams(
            collective_id=0, has_side_effects=True, vmem_limit_bytes=VMEM_BYTES
        ),
        name="train",
    )(
        scalars, velocity, w_mix, jnp.asarray(spread, BF16), w_lift.T, jnp.asarray(ahead, BF16),
        b_lift[None], b_mix[None], w_out, b_out[None], jnp.asarray(unspread, BF16), jnp.asarray(pick),
    )
    shapes = ((64, 128), (64, 1728), (54, 64), (1, 64), (1, 64), (2, 64), (1, 2))
    return pl.pallas_call(
        finish_kernel,
        out_shape=tuple(jax.ShapeDtypeStruct(shape, F32) for shape in shapes),
        in_specs=[VMEM] * 2,
        out_specs=(VMEM,) * 7,
        compiler_params=pltpu.CompilerParams(vmem_limit_bytes=8 * 2**20),
        name="finish",
    )(adv, out)


def on_device(scalars, velocity, w_lift, b_lift, w_mix, b_mix, w_out, b_out):
    total_cells = scalars.size * lax.axis_size("gx") * lax.axis_size("gy")
    loss_scale = 2.0 / math.sqrt(total_cells)
    adv, mix, lift, liftbias, mixbias, out_grad, outbias = train(
        loss_scale, scalars.reshape(64, 128), velocity.reshape(192, 128),
        w_lift, b_lift, w_mix, b_mix, w_out, b_out,
    )
    return (
        adv.reshape(scalars.shape), lift.T, liftbias[0], mix, mixbias[0], out_grad, outbias[0],
    )


def solution(mesh):
    cells = P("grp", None, ("gx", "gy"), None)
    in_specs = (cells, P(None, None, ("gx", "gy"), None)) + (P(),) * 6
    out_specs = (cells,) + (P(),) * 6
    return jax.shard_map(
        on_device, mesh=mesh, in_specs=in_specs, out_specs=out_specs, check_vma=False
    )
```

time: 98.7 us -> 66.8 us (0.68)
  Pallas kernels: 79.4 us -> 64.2 us
  local copies, waits for them, and re-layouts: 16.4 us -> 1.77 us
  matrix products: 1.17 us -> 0 us
    pallas_call x3 -> x2, Pallas kernels: 79.4 us -> 64.2 us  [the longest x1 63.3 us: train(): pl.pallas_call(functools.partial(main_kernel, loss_scale), out_shape=(jax...]
    unnamed x21 -> x4, local copies, waits for them, and re-layouts: 6.18 us -> 1.77 us
    reshape x8 -> x0, local copies, waits for them, and re-layouts: 3.51 us -> none  [the longest x2 1.85 us: layouts(): mix = taps.transpose(3, 0, 2, 1).reshape(192, 576)]
    dynamic_update_slice x5 -> x0, local copies, waits for them, and re-layouts: 2.37 us -> none  [layouts(): out = lax.dynamic_update_slice(out, w_out, (2 * y, 64 * y))]
    rev x1 -> x0, local copies, waits for them, and re-layouts: 1.52 us -> none  [layouts(): back = taps[:, :, ::-1, ::-1].transpose(3, 1, 2, 0).reshape(192, 576)]
    slice x5 -> x0, local copies, waits for them, and re-layouts: 1.42 us -> none  [the longest x1 0.7 us: on_device(): small[:, 55]]
    dot_general x1 -> x0, matrix products: 1.17 us -> none  [layouts(): jnp.einsum('oj,yjc->yoc', w_lift, jnp.asarray(ahead, BF16))]
where the time goes in v3:
time: 66.8 us; the launch traced here: 66.6 us
  Pallas kernels  64.2 us (96%)
  local copies, waits for them, and re-layouts  1.77 us (3%)
    pallas_call x1, Pallas kernels, train(): pl.pallas_call(functools.partial(main_kernel, loss_scale), out_shape=(jax...  63.3 us
    unnamed x4, local copies, waits for them, and re-layouts  1.77 us

profile of v3, /device:TPU:1, one launch (start us, length us, event | category | flops | bytes accessed | tf_op | source)
XLA Modules:
  0.0 66.6 jit_solution(11588682167541124015)
XLA Ops:
  0.6 63.3 %train.1 = (f32[64,128]{1,0:T(8,128)}, f32[32,4,896]{2,1,0:T(4,128)}) custom-call(f32[64,128]{1,0:T(8,128)} %bitcast.12, f32[192,128]{1,0:T(8,128)} %bitcast.11, bf16[64,1728]{1,0:T(8,128)(2,1)} %w_mix_hbm.1, bf16[1728,576]{1,0:T(8,128)(2,1)} %constant.8.clone.spread_hbm, bf16[54,64]{1,0:T(8,128)(2,1)} %bitcast.13, ...), custom_call_target="tpu_custom_call" | custom-call | tf_op jit(solution)/shard_map/train/pallas_call | solution.py:630
  64.0 0.0 copy-start
  64.0 1.0 %copy-done = f32[32,4,896]{2,1,0:T(4,128)S(1)} copy-done((f32[32,4,896]{2,1,0:T(4,128)S(1)}, f32[32,4,896]{2,1,0:T(4,128)}, u32[]{:S(2)}) %copy-start) | copy-done | bytes 458776
  65.0 0.0 copy-start.1
  65.0 0.8 %copy-done.1 = f32[64,128]{1,0:T(8,128)S(1)} copy-done((f32[64,128]{1,0:T(8,128)S(1)}, f32[64,128]{1,0:T(8,128)}, u32[]{:S(2)}) %copy-start.1) | copy-done | bytes 32792
  65.7 0.8 %finish.1 = (f32[64,128]{1,0:T(8,128)}, f32[64,1728]{1,0:T(8,128)}, f32[54,64]{1,0:T(8,128)}, f32[1,64]{1,0:T(1,128)}, f32[1,64]{1,0:T(1,128)}, /*index=5*/f32[2,64]{1,0:T(2,128)}, f32[1,2]{1,0:T(1,128)}) custom-call(f32[64,128]{1,0:T(8,128)S(1)} %copy-done.1, f32[32,4,896]{2,1,0:T(4,128)S(1)} %copy-done), custom_call_target="tpu_custom_call" | custom-call | tf_op jit(solution)/shard_map/finish/pallas_call | solution.py:662
Async XLA Ops:
  64.0 1.0 %copy-start = (f32[32,4,896]{2,1,0:T(4,128)S(1)}, f32[32,4,896]{2,1,0:T(4,128)}, u32[]{:S(2)}) copy-start(f32[32,4,896]{2,1,0:T(4,128)} %get-tuple-element.17.out) | copy-start | bytes 1376260
  65.0 0.8 %copy-start.1 = (f32[64,128]{1,0:T(8,128)S(1)}, f32[64,128]{1,0:T(8,128)}, u32[]{:S(2)}) copy-start(f32[64,128]{1,0:T(8,128)} %get-tuple-element.16.adv_in) | copy-start | bytes 98308

commit v4 on v3

--- a/solution.py
+++ b/solution.py
@@ -56,9 +56,10 @@
         )
 
     first = [
-        send(sc, halo.at[0], a_send.at[0], a_recv.at[0], 1, 0),
-        send(sc, halo.at[1], a_send.at[1], a_recv.at[1], -1, 0),
+        send(sc, halo.at[0], a_send, a_recv, 1, 0),
+        send(sc, halo.at[1], a_send, a_recv, -1, 0),
     ]
+    first_all = send(halo, halo, a_send, a_recv, 1, 0)
     for copy in first:
         copy.start()
 
@@ -80,8 +81,7 @@
 
     prepare_lift()
     own = [sc[pl.ds(y, 32, stride=2), :] for y in range(2)]
-    for copy in first:
-        copy.wait_recv()
+    first_all.wait_recv()
     below = jnp.where(s == 0, 0.0, halo[0, pl.ds(1, 32, stride=2), :])
     above = jnp.where(s == 127, 0.0, halo[1, pl.ds(0, 32, stride=2), :])
     stepped = [step(own[0], below, own[1], 0), step(own[1], own[0], above, 1)]
@@ -90,80 +90,68 @@
         wide[y] = stepped[y].astype(BF16)
 
     second = [
-        send(held.at[1], gains.at[0], b_send.at[0], b_recv.at[0], 1, 0),
-        send(held.at[0], gains.at[1], b_send.at[1], b_recv.at[1], -1, 0),
+        send(held.at[1], gains.at[0], b_send, b_recv, 1, 0),
+        send(held.at[0], gains.at[1], b_send, b_recv, -1, 0),
     ]
+    second_all = send(gains, gains, b_send, b_recv, 1, 0)
     third = []
-    for index, (d, f) in enumerate(partners):
-        field = g
+    for d, f in partners:
+        slot = 2 * (2 - d) + g
         if abs(d) == 2:
             y = 1 if d > 0 else 0
-            src, dst = wide.at[y], seen.at[2 - d, field, y]
+            third.append(send(wide.at[y], seen.at[slot, y], n_send, n_recv, d, f))
         else:
-            src, dst = wide, seen.at[2 - d, field]
-        third.append(send(src, dst, n_send.at[index], n_recv.at[index], d, f))
-    arrivals = []
-    for index, (d, f) in enumerate(partners):
-        field = g if f == 0 else 1 - g
-        if abs(d) == 2:
-            y = 1 if d > 0 else 0
-            src, dst = wide.at[y], seen.at[2 - d, field, y]
-        else:
-            src, dst = wide, seen.at[2 - d, field]
-        arrivals.append(send(src, dst, n_send.at[index], n_recv.at[index], d, f))
+            third.append(send(wide, seen.at[slot], n_send, n_recv, d, f))
+    third_all = send(seen.at[pl.ds(0, 7)], seen.at[pl.ds(0, 7)], n_send, n_recv, 1, 0)
     for copy in second:
         copy.start()
     for copy in third:
         copy.start()
     for y in range(2):
-        seen[2, g, y] = wide[y]
+        seen[4 + g, y] = wide[y]
     net[pl.ds(0, 48), :] = jnp.zeros((48, 128), F32)
     net[pl.ds(35 * 16, 48), :] = jnp.zeros((48, 128), F32)
-    tgt[pl.ds(0, 8), :] = jnp.zeros((8, 128), F32)
-    tgt[pl.ds(33 * 8, 8), :] = jnp.zeros((8, 128), F32)
-
     prepare_back()
-    for copy in second:
-        copy.wait_recv()
-    below = jnp.where(s == 0, 0.0, gains[0])
-    above = jnp.where(s == 127, 0.0, gains[1])
-    advanced = [
-        step(stepped[0], below, stepped[1], 0),
-        step(stepped[1], stepped[0], above, 1),
-    ]
-    for y in range(2):
-        adv[pl.ds(y, 32, stride=2), :] = advanced[y]
-        inc[g, 1 + y] = advanced[y] - stepped[y]
-    fourth, landings = [], []
-    for index, (d, f) in enumerate([(0, 1), (1, 0), (1, 1), (-1, 0), (-1, 1)]):
-        def ends(field):
-            if d == 0:
-                return inc.at[g, pl.ds(1, 2)], inc.at[field, pl.ds(1, 2)]
-            if d == 1:
-                return inc.at[g, 2], inc.at[field, 0]
-            return inc.at[g, 1], inc.at[field, 3]
-        fourth.append(send(*ends(g), c_send.at[index], c_recv.at[index], d, f))
-        landings.append(
-            send(*ends(g if f == 0 else 1 - g), c_send.at[index], c_recv.at[index], d, f)
-        )
-    for copy in fourth:
-        copy.start()
-
-    for copy in arrivals:
-        copy.wait_recv()
+    third_all.wait_recv()
     for field in range(2):
         for yy in range(8):
             slab, y = (yy + 1) // 2, (yy + 1) % 2
             y_at = 2 * s - 3 + yy
             inside = (y_at >= 0) & (y_at < 256)
-            value = jnp.where(inside, seen[slab, field, y].astype(F32), 0.0)
+            value = jnp.where(inside, seen[2 * slab + field, y].astype(F32), 0.0)
             net[pl.ds(48 + field * 8 + yy, 32, stride=16), :] = value
-    for copy in landings:
-        copy.wait_recv()
-    for field in range(2):
-        for yy in range(4):
-            tgt[pl.ds(8 + yy * 2 + field, 32, stride=8), :] = inc[field, yy]
-    return first + second + third + fourth
+
+    def increments():
+        second_all.wait_recv()
+        below = jnp.where(s == 0, 0.0, gains[0])
+        above = jnp.where(s == 127, 0.0, gains[1])
+        advanced = [
+            step(stepped[0], below, stepped[1], 0),
+            step(stepped[1], stepped[0], above, 1),
+        ]
+        for y in range(2):
+            adv[pl.ds(y, 32, stride=2), :] = advanced[y]
+            inc[4 * g + 1 + y] = advanced[y] - stepped[y]
+        for d, f in [(0, 1), (1, 0), (1, 1), (-1, 0), (-1, 1)]:
+            if d == 0:
+                part = inc.at[pl.ds(4 * g + 1, 2)]
+                send(part, part, c_send, c_recv, d, f).start()
+            elif d == 1:
+                send(inc.at[4 * g + 2], inc.at[4 * g], c_send, c_recv, d, f).start()
+            else:
+                send(inc.at[4 * g + 1], inc.at[4 * g + 3], c_send, c_recv, d, f).start()
+
+    fourth_all = send(inc.at[pl.ds(0, 6)], inc.at[pl.ds(0, 6)], c_send, c_recv, 1, 0)
+
+    def targets():
+        fourth_all.wait_recv()
+        tgt[pl.ds(0, 8), :] = jnp.zeros((8, 128), F32)
+        tgt[pl.ds(33 * 8, 8), :] = jnp.zeros((8, 128), F32)
+        for field in range(2):
+            for yy in range(4):
+                tgt[pl.ds(8 + yy * 2 + field, 32, stride=8), :] = inc[4 * field + yy]
+
+    return increments, targets, (first_all, second_all, third_all, fourth_all)
 
 
 def gelu_parts(v):
@@ -211,7 +199,10 @@
             tiles = [flat[64 * m : 64 * m + 64, 64 * oz : 64 * oz + 64] for m in range(8, -1, -1)]
             self.back[pl.ds(64 * (2 - oz), 64), :] = jnp.concatenate(tiles, axis=1).astype(BF16)
 
-def network(loss_scale, net, tgt, prepared, unspread_ref, pick, v3, lifted, slope1, mixed, slope2, cot, down, errors, total, buf):
+def network(
+    loss_scale, increments, targets, summing, net, tgt, prepared, unspread_ref, pick,
+    v3, lifted, slope1, mixed, slope2, cot, down, errors, total, buf, small_buf,
+):
     g, s = place()
     x0 = g * 16
 
@@ -264,6 +255,7 @@
             wipe(last_y)
 
     clear(lifted, (0, 1), (18, 19), pl.ds(0, 128), pl.ds(256, 128))
+    increments()
 
     def summed_z(u):
         return roll_z(u[:64], 1) + u[64:128] + roll_z(u[128:], -1)
@@ -287,6 +279,8 @@
         return 0
 
     lax.fori_loop(0, 18, mix, 0, unroll=3)
+
+    targets()
 
     def compare(batch, _):
         first = 6 * batch
@@ -323,12 +317,29 @@
             axis=1,
         )
         total[...] += rows_dot(seen, theirs)
+        return mixbias + mine[:64] + mine[64:]
+
+    mixbias = lax.fori_loop(0, 16, mix_grad, jnp.zeros((64, 128), F32), unroll=4)
+
+    flat = total[...].T
+    high = flat.astype(BF16)
+    low = (flat - high.astype(F32)).astype(BF16)
+    placed = jnp.dot(jnp.concatenate([high, low], axis=0), unspread_ref[...], preferred_element_type=F32)
+    placed = placed[:192] + placed[192:]
+    full = placed[:64] + pltpu.roll(placed[64:128], 1, 1) + pltpu.roll(placed[128:], 2, 1)
+    for c in range(32):
+        at, half = 4 * (c // 2), 896 * (c % 2)
+        buf[c] = full[at : at + 4, half : half + 896]
+    summing.begin()
+
+    def backward(x, _):
         u = jnp.dot(prepared.back[...], around(cot, x, 0, 2), preferred_element_type=F32)
         back = jnp.concatenate([summed_z(u[:, :128]), summed_z(u[:, 128:])], axis=0)
         down[x] = (back * slope1[x + 2]).astype(BF16)
-        return mixbias + mine[:64] + mine[64:]
-
-    mixbias = lax.fori_loop(0, 16, mix_grad, jnp.zeros((64, 128), F32), unroll=4)
+        return 0
+
+    lax.fori_loop(0, 16, backward, 0, unroll=4)
+    summing.plane()
 
     liftbias = jnp.zeros((64, 128), F32)
     outbias = jnp.zeros((8, 128), F32)
@@ -350,13 +361,6 @@
             jnp.concatenate(errs, axis=1),
         )
 
-    flat = total[...].T
-    high = flat.astype(BF16)
-    low = (flat - high.astype(F32)).astype(BF16)
-    placed = jnp.dot(jnp.concatenate([high, low], axis=0), unspread_ref[...], preferred_element_type=F32)
-    placed = placed[:192] + placed[192:]
-    full = placed[:64] + pltpu.roll(placed[64:128], 1, 1) + pltpu.roll(placed[128:], 2, 1)
-
     small = jnp.zeros((64, 128), F32)
     for y in range(2):
         small += jnp.dot(
@@ -365,19 +369,20 @@
         )
     lane = lax.broadcasted_iota(jnp.int32, (64, 128), 1)
     row = lax.broadcasted_iota(jnp.int32, (64, 128), 0)
-    small = jnp.where(lane == 118, jnp.sum(liftbias, axis=1, keepdims=True), small)
-    small = jnp.where(lane == 119, jnp.sum(mixbias, axis=1, keepdims=True), small)
+    small = jnp.where(lane == 54, jnp.sum(liftbias, axis=1, keepdims=True), small)
+    small = jnp.where(lane == 55, jnp.sum(mixbias, axis=1, keepdims=True), small)
     for k in range(2):
         piece = out_total[:64, 2 + k : 3 + k] + out_total[64:, 4 + k : 5 + k]
-        small = jnp.where(lane == 120 + k, piece, small)
+        small = jnp.where(lane == 56 + k, piece, small)
     per_row = jnp.sum(outbias, axis=1, keepdims=True)
     pair = per_row[2:4] + per_row[4:6]
     for k in range(2):
-        small = jnp.where((lane == 122) & (row == k), pair[k : k + 1], small)
-    full = jnp.concatenate([full[:, :1664], full[:, 1664:] + small], axis=1)
-    for c in range(32):
-        at, half = 4 * (c // 2), 896 * (c % 2)
-        buf[c] = full[at : at + 4, half : half + 896]
+        small = jnp.where((lane == 58) & (row == k), pair[k : k + 1], small)
+    small = jnp.concatenate([small[:32, :64], small[32:, :64]], axis=1)
+    for c in range(16):
+        small_buf[c] = small[2 * c : 2 * c + 2]
+    summing.small_plane()
+
 
 class Ring:
     def __init__(self):
@@ -413,119 +418,101 @@
         lax.fori_loop(1, 8, greet_z, 0)
 
 
-def all_sum(ring, buf, out, from_core, mine, from_plane, from_z, s1, r1, s2, r2, s3, r3, s4, r4, s5, r5):
-    place, z, core, sibling = ring.place, ring.z, ring.core, ring.sibling
-    in_plane, in_z = ring.in_plane, ring.in_z
-    theirs = pl.multiple_of((1 - core) * 16, 16)
-    ours = pl.multiple_of(core * 16, 16)
-    swap = pltpu.make_async_remote_copy(
-        buf.at[pl.ds(theirs, 16)], from_core, s1, r1, device_id=sibling, device_id_type=MESH
-    )
-    swap.start()
-    swap.wait()
-
-    def add_core(j, _):
-        mine[j] = buf[ours + j] + from_core[j]
-        return 0
-
-    lax.fori_loop(0, 16, add_core, 0)
-
-    def to_plane(j):
-        other = (place + j) % 16
+class Summing:
+    def __init__(self, ring, buf, out, from_core, mine, from_plane, from_z, small, s_plane, s_z, s_out, s_core, sems):
+        self.__dict__.update(locals())
+        self.ours = pl.multiple_of(ring.core * 16, 16)
+        self.theirs = pl.multiple_of((1 - ring.core) * 16, 16)
+
+    def copy(self, src, dst, pair, device):
         return pltpu.make_async_remote_copy(
-            mine.at[other], from_plane.at[place], s2.at[other], r2.at[place],
-            device_id=in_plane(other), device_id_type=MESH,
-        )
-
-    def of_plane(j):
-        other = (place + j) % 16
-        return pltpu.make_async_remote_copy(
-            mine.at[other], from_plane.at[other], s2.at[other], r2.at[other],
-            device_id=in_plane(other), device_id_type=MESH,
-        )
-
-    lax.fori_loop(1, 16, lambda j, _: (to_plane(j).start(), 0)[1], 0)
-    from_plane[place] = mine[place]
-
-    def wait_plane(j, _):
-        of_plane(j).wait()
-        return 0
-
-    lax.fori_loop(1, 16, wait_plane, 0)
-    total = from_plane[0]
-    for j in range(1, 16):
-        total = total + from_plane[j]
-    from_z[z] = total
-
-    def to_z(j):
-        other = (z + j) % 8
-        return pltpu.make_async_remote_copy(
-            from_z.at[z], from_z.at[z], s3.at[other], r3.at[z], device_id=in_z(other), device_id_type=MESH
-        )
-
-    def of_z(j):
-        other = (z + j) % 8
-        return pltpu.make_async_remote_copy(
-            from_z.at[other], from_z.at[other], s3.at[other], r3.at[other], device_id=in_z(other), device_id_type=MESH
-        )
-
-    lax.fori_loop(1, 8, lambda j, _: (to_z(j).start(), 0)[1], 0)
-
-    def wait_z(j, _):
-        of_z(j).wait()
-        return 0
-
-    lax.fori_loop(1, 8, wait_z, 0)
-    total = from_z[0]
-    for j in range(1, 8):
-        total = total + from_z[j]
-    out[ours + place] = total
-
-    def gather(j):
-        other = (place + j) % 16
-        return pltpu.make_async_remote_copy(
-            out.at[ours + place], out.at[ours + place], s4.at[other], r4.at[place],
-            device_id=in_plane(other), device_id_type=MESH,
-        )
-
-    def gathered(j):
-        other = (place + j) % 16
-        return pltpu.make_async_remote_copy(
-            out.at[ours + other], out.at[ours + other], s4.at[other], r4.at[other],
-            device_id=in_plane(other), device_id_type=MESH,
-        )
-
-    def hand(j):
-        other = (place + j) % 16
-        return pltpu.make_async_remote_copy(
-            out.at[ours + other], out.at[ours + other], s5.at[other], r5.at[other],
-            device_id=sibling, device_id_type=MESH,
-        )
-
-    def handed(j):
-        other = (place + j) % 16
-        return pltpu.make_async_remote_copy(
-            out.at[theirs + other], out.at[theirs + other], s5.at[other], r5.at[other],
-            device_id=sibling, device_id_type=MESH,
-        )
-
-    lax.fori_loop(1, 16, lambda j, _: (gather(j).start(), 0)[1], 0)
-    hand(0).start()
-
-    def pass_on(j, _):
-        gathered(j).wait_recv()
-        hand(j).start()
-        return 0
-
-    lax.fori_loop(1, 16, pass_on, 0)
-
-    def finish(j, _):
-        handed(j).wait_recv()
-        hand(j).wait_send()
-        return 0
-
-    lax.fori_loop(0, 16, finish, 0)
-    lax.fori_loop(1, 16, lambda j, _: (gather(j).wait_send(), 0)[1], 0)
+            src, dst, self.sems.at[2 * pair], self.sems.at[2 * pair + 1], device_id=device, device_id_type=MESH
+        )
+
+    def begin(self):
+        self.swap = self.copy(self.buf.at[pl.ds(self.theirs, 16)], self.from_core, 0, self.ring.sibling)
+        self.swap.start()
+
+    def spread_plane(self, source, target, pair):
+        ring = self.ring
+
+        def start(j, _):
+            other = lax.rem(ring.place + j, 16)
+            self.copy(source(other), target, pair, ring.in_plane(other)).start()
+            return 0
+
+        lax.fori_loop(1, 16, start, 0)
+
+    def spread_z(self, ref, pair):
+        ring = self.ring
+        own = ref.at[ring.z]
+
+        def start(j, _):
+            self.copy(own, own, pair, ring.in_z(lax.rem(ring.z + j, 8))).start()
+            return 0
+
+        lax.fori_loop(1, 8, start, 0)
+
+    def finish(self, ref, first, count, pair):
+        part = ref.at[pl.ds(first, count)]
+        self.copy(part, part, pair, self.ring.sibling).wait()
+
+    def plane(self):
+        self.swap.wait()
+        buf, mine, ours = self.buf, self.mine, self.ours
+
+        def add_core(j, _):
+            mine[j] = buf[ours + j] + self.from_core[j]
+            return 0
+
+        lax.fori_loop(0, 16, add_core, 0, unroll=4)
+        place = self.ring.place
+        self.spread_plane(lambda other: mine.at[other], self.from_plane.at[place], 1)
+        self.from_plane[place] = mine[place]
+
+    def small_plane(self):
+        place = self.ring.place
+        self.spread_plane(lambda other: self.small.at[other], self.s_plane.at[place], 2)
+        self.s_plane[place] = self.small[place]
+
+    def rest(self):
+        place, z = self.ring.place, self.ring.z
+
+        def total(ref, count):
+            value = ref[0]
+            for j in range(1, count):
+                value = value + ref[j]
+            return value
+
+        self.finish(self.from_plane, 0, 15, 1)
+        self.from_z[z] = total(self.from_plane, 16)
+        self.spread_z(self.from_z, 3)
+        self.finish(self.s_plane, 0, 15, 2)
+        self.s_z[z] = total(self.s_plane, 16)
+        self.spread_z(self.s_z, 4)
+
+        self.finish(self.from_z, 0, 7, 3)
+        own = self.out.at[self.ours + place]
+        self.out[self.ours + place] = total(self.from_z, 8)
+        self.spread_plane(lambda other: own, own, 5)
+        self.finish(self.s_z, 0, 7, 4)
+        small = self.s_out.at[place]
+        self.s_out[place] = total(self.s_z, 8)
+        self.spread_plane(lambda other: small, small, 6)
+
+        self.finish(self.out, 0, 15, 5)
+        half = self.out.at[pl.ds(self.ours, 16)]
+        hand = self.copy(half, half, 7, self.ring.sibling)
+        hand.start()
+        self.finish(self.s_out, 0, 15, 6)
+        swap = self.copy(self.s_out, self.s_core, 8, self.ring.sibling)
+        swap.start()
+        swap.wait()
+        both = self.s_out[...] + self.s_core[...]
+        for c in range(16):
+            at = 16 + c // 2
+            self.out[32 + at // 7, pl.ds(2 * (c % 2), 2), pl.ds(128 * (at % 7), 128)] = both[c]
+        hand.wait()
 
 
 def picks():
@@ -537,7 +524,7 @@
                 for oy in range(3):
                     tap = 27 * ch + 9 * ox + 3 * oy + oz
                     for y in range(2):
-                        grad[y, ((ox * 3 + oz) * 2 + ch) * 8 + 2 + y + oy, 64 + tap] = 1
+                        grad[y, ((ox * 3 + oz) * 2 + ch) * 8 + 2 + y + oy, tap] = 1
                     for y in range(6):
                         ahead[y, tap, ((ox * 3 + oz) * 2 + ch) * 8 + y + oy] = 1
     return grad, ahead
@@ -547,14 +534,13 @@
     loss_scale,
     sc_hbm, vel_hbm, w_mix_hbm, spread_hbm, w_lift_hbm, ahead_hbm, b_lift_hbm, b_mix_hbm, w_out_hbm, b_out_hbm,
     unspread_hbm, pick_hbm,
-    adv, out,
-    sc, vel, w_mix, spread, w_lift, ahead, b_lift, b_mix, w_out, b_out, unspread, pick,
+    out,
+    adv, sc, vel, w_mix, spread, w_lift, ahead, b_lift, b_mix, w_out, b_out, unspread, pick,
     load, lift_w, mix_w, back_w, out_w, outt_w, bias,
     net, tgt, halo, held, wide, seen, inc, gains,
     v3, lifted, slope1, mixed, slope2, cot, down, errors, total, buf,
-    from_core, mine, from_plane, from_z,
-    a_send, a_recv, b_send, b_recv, n_send, n_recv, c_send, c_recv,
-    *sums,
+    from_core, mine, from_plane, from_z, small, s_plane, s_z, s_out, s_core,
+    a_send, a_recv, b_send, b_recv, n_send, n_recv, c_send, c_recv, sums,
 ):
     pairs = (
         (sc_hbm, sc), (vel_hbm, vel), (w_mix_hbm, w_mix), (spread_hbm, spread), (w_lift_hbm, w_lift),
@@ -581,34 +567,44 @@
             copy.wait()
         prepared.lift_form()
 
-    sent = solver(
+    increments, targets, sent = solver(
         ring, prepare_mix, prepare_lift, prepared.back_form,
         sc, vel, adv, net, tgt, halo, held, wide, seen, inc, gains,
         a_send, a_recv, b_send, b_recv, n_send, n_recv, c_send, c_recv,
     )
     for copy in loads[10:]:
         copy.wait()
+    summing = Summing(
+        ring, buf, out, from_core, mine, from_plane, from_z, small, s_plane, s_z, s_out, s_core, sums
+    )
     network(
-        loss_scale, net, tgt, prepared, unspread, pick,
-        v3, lifted, slope1, mixed, slope2, cot, down, errors, total, buf,
+        loss_scale, increments, targets, summing, net, tgt, prepared, unspread, pick,
+        v3, lifted, slope1, mixed, slope2, cot, down, errors, total, buf, small,
     )
     for copy in sent:
         copy.wait_send()
-    all_sum(ring, buf, out, from_core, mine, from_plane, from_z, *sums)
-
-
-def finish_kernel(adv_in, out, adv, mix, lift, liftbias, mixbias, out_grad, outbias):
-    adv[...] = adv_in[...]
+    for block in range(16):
+        out[32 + block // 7, :, pl.ds(128 * (block % 7), 128)] = adv[pl.ds(4 * block, 4), :]
+    summing.rest()
+
+
+def finish_kernel(out, adv, mix, lift, liftbias, mixbias, out_grad, outbias):
+    def block(at):
+        return out[32 + at // 7, :, pl.ds(128 * (at % 7), 128)]
+
+    for at in range(16):
+        adv[pl.ds(4 * at, 4), :] = block(at)
     for r in range(16):
         mix[pl.ds(4 * r, 4), pl.ds(0, 896)] = out[2 * r]
         mix[pl.ds(4 * r, 4), pl.ds(896, 832)] = out[2 * r + 1][:, :832]
-    last = jnp.concatenate([out[2 * r + 1][:, 768:] for r in range(16)], axis=0)
-    turned = last.T
-    lift[...] = turned[64:118]
-    liftbias[...] = turned[118:119]
-    mixbias[...] = turned[119:120]
-    out_grad[...] = turned[120:122]
-    outbias[...] = turned[122:123, :2]
+    small = jnp.concatenate([block(16 + at) for at in range(8)], axis=0)
+    turned = small.T
+    turned = jnp.concatenate([turned[:64], turned[64:]], axis=1)
+    lift[...] = turned[:54]
+    liftbias[...] = turned[54:55]
+    mixbias[...] = turned[55:56]
+    out_grad[...] = turned[56:58]
+    outbias[...] = turned[58:59, :2]
 
 
 def train(loss_scale, scalars, velocity, w_lift, b_lift, w_mix, b_mix, w_out, b_out):
@@ -627,12 +623,13 @@
     def vmem(*shape, dtype=F32):
         return pltpu.VMEM(shape, dtype)
 
-    adv, out = pl.pallas_call(
+    out = pl.pallas_call(
         functools.partial(main_kernel, loss_scale),
-        out_shape=(jax.ShapeDtypeStruct((64, 128), F32), jax.ShapeDtypeStruct((32,) + chunk, F32)),
+        out_shape=jax.ShapeDtypeStruct((36,) + chunk, F32),
         in_specs=[hbm] * 12,
-        out_specs=(VMEM, VMEM),
+        out_specs=VMEM,
         scratch_shapes=[
+            vmem(64, 128),
             vmem(64, 128), vmem(192, 128), vmem(64, 1728, dtype=BF16), vmem(1728, 576, dtype=BF16),
             vmem(54, 64, dtype=BF16), vmem(6, 54, 144, dtype=BF16), vmem(1, 64), vmem(1, 64),
             vmem(2, 64, dtype=BF16), vmem(1, 2), vmem(576, 1792, dtype=BF16), vmem(2, 144, 128), dma((12,)),
@@ -640,15 +637,13 @@
             vmem(16, 256, dtype=BF16), vmem(256, 16, dtype=BF16), vmem(2, 64, 128),
             vmem(38 * 16, 128), vmem(34 * 8, 128),
             vmem(2, 64, 128), vmem(2, 32, 128), vmem(2, 32, 128, dtype=BF16),
-            vmem(5, 2, 2, 32, 128, dtype=BF16), vmem(2, 4, 32, 128), vmem(2, 32, 128),
+            vmem(10, 2, 32, 128, dtype=BF16), vmem(8, 32, 128), vmem(2, 32, 128),
             vmem(22, 48, 128, dtype=BF16), vmem(20, 384, 128, dtype=BF16), vmem(20, 128, 128),
             vmem(18, 256, 128, dtype=BF16), vmem(18, 256, 128), vmem(18, 256, 128, dtype=BF16),
             vmem(16, 128, 128, dtype=BF16), vmem(18, 16, 128, dtype=BF16), vmem(576, 192),
             vmem(32, *chunk), vmem(16, *chunk), vmem(16, *chunk), vmem(16, *chunk), vmem(8, *chunk),
-            dma((2,)), dma((2,)), dma((2,)), dma((2,)),
-            dma((9,)), dma((9,)), dma((5,)), dma((5,)),
-            dma, dma, dma((16,)), dma((16,)), dma((8,)), dma((8,)),
-            dma((16,)), dma((16,)), dma((16,)), dma((16,)),
+            vmem(16, 2, 128), vmem(16, 2, 128), vmem(8, 2, 128), vmem(16, 2, 128), vmem(16, 2, 128),
+            dma, dma, dma, dma, dma, dma, dma, dma, dma((18,)),
         ],
         compiler_params=pltpu.CompilerParams(
             collective_id=0, has_side_effects=True, vmem_limit_bytes=VMEM_BYTES
@@ -662,11 +657,11 @@
     return pl.pallas_call(
         finish_kernel,
         out_shape=tuple(jax.ShapeDtypeStruct(shape, F32) for shape in shapes),
-        in_specs=[VMEM] * 2,
+        in_specs=[VMEM],
         out_specs=(VMEM,) * 7,
         compiler_params=pltpu.CompilerParams(vmem_limit_bytes=8 * 2**20),
         name="finish",
-    )(adv, out)
+    )(out)
 
 
 def on_device(scalars, velocity, w_lift, b_lift, w_mix, b_mix, w_out, b_out):

time: 66.8 us -> 60.2 us (0.901)
  Pallas kernels: 64.2 us -> 58.3 us
  local copies, waits for them, and re-layouts: 1.77 us -> 1.03 us
    pallas_call x1, Pallas kernels: 63.3 us -> 57.5 us  [train(): pl.pallas_call(functools.partial(main_kernel, loss_scale), out_shape=jax....]
    unnamed x4 -> x2, local copies, waits for them, and re-layouts: 1.77 us -> 1.03 us
where the time goes in v4:
time: 60.2 us; the launch traced here: 60 us
  Pallas kernels  58.3 us (97%)
  local copies, waits for them, and re-layouts  1.03 us (2%)
  between operations  0.65 us (1%)
    pallas_call x1, Pallas kernels, train(): pl.pallas_call(functools.partial(main_kernel, loss_scale), out_shape=jax....  57.5 us

profile of v4, /device:TPU:1, one launch (start us, length us, event | category | flops | bytes accessed | tf_op | source)
XLA Modules:
  0.0 60.0 jit_solution(12928948887833536791)
XLA Ops:
  0.6 57.5 %train.1.out = f32[36,4,896]{2,1,0:T(4,128)} custom-call(f32[64,128]{1,0:T(8,128)} %bitcast.12, f32[192,128]{1,0:T(8,128)} %bitcast.11, bf16[64,1728]{1,0:T(8,128)(2,1)} %w_mix_hbm.1, bf16[1728,576]{1,0:T(8,128)(2,1)} %constant.8.clone.spread_hbm, bf16[54,64]{1,0:T(8,128)(2,1)} %bitcast.13, bf16[6,54,144]{2,1,0:T(8,128)(2,1)} %constant.9.clone.ahead_hbm, ...), custom_call_target="tpu_custom_call" | custom-call | tf_op jit(solution)/shard_map/train/pallas_call | solution.py:626
  58.1 0.0 copy-start
  58.1 1.0 %copy-done = f32[36,4,896]{2,1,0:T(4,128)S(1)} copy-done((f32[36,4,896]{2,1,0:T(4,128)S(1)}, f32[36,4,896]{2,1,0:T(4,128)}, u32[]{:S(2)}) %copy-start) | copy-done | bytes 516120
  59.1 0.9 %finish.1 = (f32[64,128]{1,0:T(8,128)}, f32[64,1728]{1,0:T(8,128)}, f32[54,64]{1,0:T(8,128)}, f32[1,64]{1,0:T(1,128)}, f32[1,64]{1,0:T(1,128)}, /*index=5*/f32[2,64]{1,0:T(2,128)}, f32[1,2]{1,0:T(1,128)}) custom-call(f32[36,4,896]{2,1,0:T(4,128)S(1)} %copy-done), custom_call_target="tpu_custom_call" | custom-call | tf_op jit(solution)/shard_map/finish/pallas_call | solution.py:657
Async XLA Ops:
  58.1 1.0 %copy-start = (f32[36,4,896]{2,1,0:T(4,128)S(1)}, f32[36,4,896]{2,1,0:T(4,128)}, u32[]{:S(2)}) copy-start(f32[36,4,896]{2,1,0:T(4,128)} %train.1.out) | copy-start | bytes 1548292

commit v5 on v4

--- a/solution.py
+++ b/solution.py
@@ -28,7 +28,7 @@
 
 def solver(
     ring, prepare_mix, prepare_lift, prepare_back,
-    sc, vel, adv, net, tgt,
+    sc_hbm, sc, vel, adv, net, tgt,
     halo, held, wide, seen, inc, gains,
     a_send, a_recv, b_send, b_recv, n_send, n_recv, c_send, c_recv,
 ):
@@ -47,7 +47,6 @@
     for d, f in partners:
         pl.semaphore_signal(barrier, inc=1, device_id=partner(d, f), device_id_type=MESH)
     ring.greet(barrier)
-    prepare_mix()
     pl.semaphore_wait(barrier, len(partners) + 23)
 
     def send(src, dst, ssem, rsem, d, f):
@@ -56,13 +55,14 @@
         )
 
     first = [
-        send(sc, halo.at[0], a_send, a_recv, 1, 0),
-        send(sc, halo.at[1], a_send, a_recv, -1, 0),
+        send(sc_hbm, halo.at[0], a_send, a_recv, 1, 0),
+        send(sc_hbm, halo.at[1], a_send, a_recv, -1, 0),
     ]
     first_all = send(halo, halo, a_send, a_recv, 1, 0)
     for copy in first:
         copy.start()
 
+    prepare_mix()
     speed = [[vel[pl.ds(64 * d + y, 32, stride=2), :] for y in range(2)] for d in range(3)]
     row = lax.broadcasted_iota(jnp.int32, (32, 128), 0)
 
@@ -79,7 +79,6 @@
         )
         return centre + diffusivity * laplace - 0.5 * advect
 
-    prepare_lift()
     own = [sc[pl.ds(y, 32, stride=2), :] for y in range(2)]
     first_all.wait_recv()
     below = jnp.where(s == 0, 0.0, halo[0, pl.ds(1, 32, stride=2), :])
@@ -111,7 +110,30 @@
         seen[4 + g, y] = wide[y]
     net[pl.ds(0, 48), :] = jnp.zeros((48, 128), F32)
     net[pl.ds(35 * 16, 48), :] = jnp.zeros((48, 128), F32)
+    prepare_lift()
     prepare_back()
+    second_all.wait_recv()
+    below = jnp.where(s == 0, 0.0, gains[0])
+    above = jnp.where(s == 127, 0.0, gains[1])
+    advanced = [
+        step(stepped[0], below, stepped[1], 0),
+        step(stepped[1], stepped[0], above, 1),
+    ]
+    for y in range(2):
+        adv[pl.ds(y, 32, stride=2), :] = advanced[y]
+        inc[4 * g + 1 + y] = advanced[y] - stepped[y]
+    for d, f in [(0, 1), (1, 0), (1, 1), (-1, 0), (-1, 1)]:
+        if d == 0:
+            part = inc.at[pl.ds(4 * g + 1, 2)]
+            send(part, part, c_send, c_recv, d, f).start()
+        elif d == 1:
+            send(inc.at[4 * g + 2], inc.at[4 * g], c_send, c_recv, d, f).start()
+        else:
+            send(inc.at[4 * g + 1], inc.at[4 * g + 3], c_send, c_recv, d, f).start()
+
+    fourth_all = send(inc.at[pl.ds(0, 6)], inc.at[pl.ds(0, 6)], c_send, c_recv, 1, 0)
+
+
     third_all.wait_recv()
     for field in range(2):
         for yy in range(8):
@@ -121,28 +143,6 @@
             value = jnp.where(inside, seen[2 * slab + field, y].astype(F32), 0.0)
             net[pl.ds(48 + field * 8 + yy, 32, stride=16), :] = value
 
-    def increments():
-        second_all.wait_recv()
-        below = jnp.where(s == 0, 0.0, gains[0])
-        above = jnp.where(s == 127, 0.0, gains[1])
-        advanced = [
-            step(stepped[0], below, stepped[1], 0),
-            step(stepped[1], stepped[0], above, 1),
-        ]
-        for y in range(2):
-            adv[pl.ds(y, 32, stride=2), :] = advanced[y]
-            inc[4 * g + 1 + y] = advanced[y] - stepped[y]
-        for d, f in [(0, 1), (1, 0), (1, 1), (-1, 0), (-1, 1)]:
-            if d == 0:
-                part = inc.at[pl.ds(4 * g + 1, 2)]
-                send(part, part, c_send, c_recv, d, f).start()
-            elif d == 1:
-                send(inc.at[4 * g + 2], inc.at[4 * g], c_send, c_recv, d, f).start()
-            else:
-                send(inc.at[4 * g + 1], inc.at[4 * g + 3], c_send, c_recv, d, f).start()
-
-    fourth_all = send(inc.at[pl.ds(0, 6)], inc.at[pl.ds(0, 6)], c_send, c_recv, 1, 0)
-
     def targets():
         fourth_all.wait_recv()
         tgt[pl.ds(0, 8), :] = jnp.zeros((8, 128), F32)
@@ -151,7 +151,7 @@
             for yy in range(4):
                 tgt[pl.ds(8 + yy * 2 + field, 32, stride=8), :] = inc[4 * field + yy]
 
-    return increments, targets, (first_all, second_all, third_all, fourth_all)
+    return targets, (first_all, second_all, third_all, fourth_all)
 
 
 def gelu_parts(v):
@@ -200,8 +200,8 @@
             self.back[pl.ds(64 * (2 - oz), 64), :] = jnp.concatenate(tiles, axis=1).astype(BF16)
 
 def network(
-    loss_scale, increments, targets, summing, net, tgt, prepared, unspread_ref, pick,
-    v3, lifted, slope1, mixed, slope2, cot, down, errors, total, buf, small_buf,
+    loss_scale, targets, summing, net, tgt, prepared, pick,
+    v3, lifted, slope1, mixed, slope2, cot, down, errors, total, small_buf,
 ):
     g, s = place()
     x0 = g * 16
@@ -255,7 +255,6 @@
             wipe(last_y)
 
     clear(lifted, (0, 1), (18, 19), pl.ds(0, 128), pl.ds(256, 128))
-    increments()
 
     def summed_z(u):
         return roll_z(u[:64], 1) + u[64:128] + roll_z(u[128:], -1)
@@ -299,7 +298,7 @@
             errors[first + j] = error[:, 128 * j : 128 * j + 128]
         return 0
 
-    lax.fori_loop(0, 3, compare, 0)
+    lax.fori_loop(0, 3, compare, 0, unroll=3)
     clear(cot, (0,), (17,), pl.ds(0, 64), pl.ds(192, 64))
     total[...] = jnp.zeros_like(total)
 
@@ -311,25 +310,23 @@
         seen = around(lifted, x + 1, 1, 2)
         theirs = jnp.concatenate(
             [
-                jnp.concatenate([part[64 * y : 64 * y + 64] for part in (before, here, after)], axis=0)
+                jnp.concatenate(
+                    [
+                        part[64 * y + 32 * half : 64 * y + 32 * half + 32]
+                        for half in range(2)
+                        for part in (before, here, after)
+                    ],
+                    axis=0,
+                )
                 for y in range(2)
             ],
             axis=1,
         )
-        total[...] += rows_dot(seen, theirs)
+        total[:, pl.ds(0, 576)] += rows_dot(theirs, seen)
         return mixbias + mine[:64] + mine[64:]
 
     mixbias = lax.fori_loop(0, 16, mix_grad, jnp.zeros((64, 128), F32), unroll=4)
 
-    flat = total[...].T
-    high = flat.astype(BF16)
-    low = (flat - high.astype(F32)).astype(BF16)
-    placed = jnp.dot(jnp.concatenate([high, low], axis=0), unspread_ref[...], preferred_element_type=F32)
-    placed = placed[:192] + placed[192:]
-    full = placed[:64] + pltpu.roll(placed[64:128], 1, 1) + pltpu.roll(placed[128:], 2, 1)
-    for c in range(32):
-        at, half = 4 * (c // 2), 896 * (c % 2)
-        buf[c] = full[at : at + 4, half : half + 896]
     summing.begin()
 
     def backward(x, _):
@@ -338,8 +335,9 @@
         down[x] = (back * slope1[x + 2]).astype(BF16)
         return 0
 
-    lax.fori_loop(0, 16, backward, 0, unroll=4)
+    lax.fori_loop(0, 8, backward, 0, unroll=4)
     summing.plane()
+    lax.fori_loop(8, 16, backward, 0, unroll=4)
 
     liftbias = jnp.zeros((64, 128), F32)
     outbias = jnp.zeros((8, 128), F32)
@@ -419,10 +417,9 @@
 
 
 class Summing:
-    def __init__(self, ring, buf, out, from_core, mine, from_plane, from_z, small, s_plane, s_z, s_out, s_core, sems):
+    def __init__(self, ring, total, unspread, out, from_core, mine, from_plane, from_z, small, s_plane, s_z, s_out, s_core, sems):
         self.__dict__.update(locals())
         self.ours = pl.multiple_of(ring.core * 16, 16)
-        self.theirs = pl.multiple_of((1 - ring.core) * 16, 16)
 
     def copy(self, src, dst, pair, device):
         return pltpu.make_async_remote_copy(
@@ -430,7 +427,9 @@
         )
 
     def begin(self):
-        self.swap = self.copy(self.buf.at[pl.ds(self.theirs, 16)], self.from_core, 0, self.ring.sibling)
+        self.swap = self.copy(
+            self.total.at[pl.ds(pl.multiple_of((1 - self.ring.core) * 96, 96), 96)], self.from_core, 0, self.ring.sibling
+        )
         self.swap.start()
 
     def spread_plane(self, source, target, pair):
@@ -459,13 +458,19 @@
 
     def plane(self):
         self.swap.wait()
-        buf, mine, ours = self.buf, self.mine, self.ours
-
-        def add_core(j, _):
-            mine[j] = buf[ours + j] + self.from_core[j]
-            return 0
-
-        lax.fori_loop(0, 16, add_core, 0, unroll=4)
+        mine = self.mine
+        own = self.total[pl.ds(pl.multiple_of(self.ring.core * 96, 96), 96), pl.ds(0, 576)]
+        flat = own + self.from_core[:, pl.ds(0, 576)]
+        high = flat.astype(BF16)
+        low = (flat - high.astype(F32)).astype(BF16)
+        placed = jnp.dot(
+            jnp.concatenate([high, low], axis=0), self.unspread[...], preferred_element_type=F32
+        )
+        placed = placed[:96] + placed[96:]
+        full = placed[:32] + pltpu.roll(placed[32:64], 1, 1) + pltpu.roll(placed[64:], 2, 1)
+        for c in range(16):
+            at, half = 4 * (c // 2), 896 * (c % 2)
+            mine[c] = full[at : at + 4, half : half + 896]
         place = self.ring.place
         self.spread_plane(lambda other: mine.at[other], self.from_plane.at[place], 1)
         self.from_plane[place] = mine[place]
@@ -538,7 +543,7 @@
     adv, sc, vel, w_mix, spread, w_lift, ahead, b_lift, b_mix, w_out, b_out, unspread, pick,
     load, lift_w, mix_w, back_w, out_w, outt_w, bias,
     net, tgt, halo, held, wide, seen, inc, gains,
-    v3, lifted, slope1, mixed, slope2, cot, down, errors, total, buf,
+    v3, lifted, slope1, mixed, slope2, cot, down, errors, total,
     from_core, mine, from_plane, from_z, small, s_plane, s_z, s_out, s_core,
     a_send, a_recv, b_send, b_recv, n_send, n_recv, c_send, c_recv, sums,
 ):
@@ -567,19 +572,19 @@
             copy.wait()
         prepared.lift_form()
 
-    increments, targets, sent = solver(
+    targets, sent = solver(
         ring, prepare_mix, prepare_lift, prepared.back_form,
-        sc, vel, adv, net, tgt, halo, held, wide, seen, inc, gains,
+        sc_hbm, sc, vel, adv, net, tgt, halo, held, wide, seen, inc, gains,
         a_send, a_recv, b_send, b_recv, n_send, n_recv, c_send, c_recv,
     )
     for copy in loads[10:]:
         copy.wait()
     summing = Summing(
-        ring, buf, out, from_core, mine, from_plane, from_z, small, s_plane, s_z, s_out, s_core, sums
+        ring, total, unspread, out, from_core, mine, from_plane, from_z, small, s_plane, s_z, s_out, s_core, sums
     )
     network(
-        loss_scale, increments, targets, summing, net, tgt, prepared, unspread, pick,
-        v3, lifted, slope1, mixed, slope2, cot, down, errors, total, buf, small,
+        loss_scale, targets, summing, net, tgt, prepared, pick,
+        v3, lifted, slope1, mixed, slope2, cot, down, errors, total, small,
     )
     for copy in sent:
         copy.wait_send()
@@ -640,8 +645,8 @@
             vmem(10, 2, 32, 128, dtype=BF16), vmem(8, 32, 128), vmem(2, 32, 128),
             vmem(22, 48, 128, dtype=BF16), vmem(20, 384, 128, dtype=BF16), vmem(20, 128, 128),
             vmem(18, 256, 128, dtype=BF16), vmem(18, 256, 128), vmem(18, 256, 128, dtype=BF16),
-            vmem(16, 128, 128, dtype=BF16), vmem(18, 16, 128, dtype=BF16), vmem(576, 192),
-            vmem(32, *chunk), vmem(16, *chunk), vmem(16, *chunk), vmem(16, *chunk), vmem(8, *chunk),
+            vmem(16, 128, 128, dtype=BF16), vmem(18, 16, 128, dtype=BF16), vmem(192, 640),
+            vmem(96, 640), vmem(16, *chunk), vmem(16, *chunk), vmem(8, *chunk),
             vmem(16, 2, 128), vmem(16, 2, 128), vmem(8, 2, 128), vmem(16, 2, 128), vmem(16, 2, 128),
             dma, dma, dma, dma, dma, dma, dma, dma, dma((18,)),
         ],

time: 60.2 us -> 57.9 us (0.962)
  Pallas kernels: 58.3 us -> 56.1 us
    pallas_call x1, Pallas kernels: 57.5 us -> 55.2 us  [train(): pl.pallas_call(functools.partial(main_kernel, loss_scale), out_shape=jax....]
where the time goes in v5:
time: 57.9 us; the launch traced here: 57.8 us
  Pallas kernels  56.1 us (97%)
  local copies, waits for them, and re-layouts  1.03 us (2%)
  between operations  0.65 us (1%)
    pallas_call x1, Pallas kernels, train(): pl.pallas_call(functools.partial(main_kernel, loss_scale), out_shape=jax....  55.2 us

profile of v5, /device:TPU:1, one launch (start us, length us, event | category | flops | bytes accessed | tf_op | source)
XLA Modules:
  0.0 57.8 jit_solution(13059083081765457781)
XLA Ops:
  0.6 55.2 %train.1.out = f32[36,4,896]{2,1,0:T(4,128)} custom-call(f32[64,128]{1,0:T(8,128)} %bitcast.12, f32[192,128]{1,0:T(8,128)} %bitcast.11, bf16[64,1728]{1,0:T(8,128)(2,1)} %w_mix_hbm.1, bf16[1728,576]{1,0:T(8,128)(2,1)} %constant.8.clone.spread_hbm, bf16[54,64]{1,0:T(8,128)(2,1)} %bitcast.13, bf16[6,54,144]{2,1,0:T(8,128)(2,1)} %constant.9.clone.ahead_hbm, ...), custom_call_target="tpu_custom_call" | custom-call | tf_op jit(solution)/shard_map/train/pallas_call | solution.py:631
  55.9 0.0 copy-start
  55.9 1.0 %copy-done = f32[36,4,896]{2,1,0:T(4,128)S(1)} copy-done((f32[36,4,896]{2,1,0:T(4,128)S(1)}, f32[36,4,896]{2,1,0:T(4,128)}, u32[]{:S(2)}) %copy-start) | copy-done | bytes 516120
  56.9 0.9 %finish.1 = (f32[64,128]{1,0:T(8,128)}, f32[64,1728]{1,0:T(8,128)}, f32[54,64]{1,0:T(8,128)}, f32[1,64]{1,0:T(1,128)}, f32[1,64]{1,0:T(1,128)}, /*index=5*/f32[2,64]{1,0:T(2,128)}, f32[1,2]{1,0:T(1,128)}) custom-call(f32[36,4,896]{2,1,0:T(4,128)S(1)} %copy-done), custom_call_target="tpu_custom_call" | custom-call | tf_op jit(solution)/shard_map/finish/pallas_call | solution.py:662
Async XLA Ops:
  55.9 1.0 %copy-start = (f32[36,4,896]{2,1,0:T(4,128)S(1)}, f32[36,4,896]{2,1,0:T(4,128)}, u32[]{:S(2)}) copy-start(f32[36,4,896]{2,1,0:T(4,128)} %train.1.out) | copy-start | bytes 1548292

commit v6 on v5

--- a/solution.py
+++ b/solution.py
@@ -39,14 +39,14 @@
         other = lax.rem(s + step + 128, 128)
         return (field, other // 4, lax.rem(other, 4))
 
-    partners = [(d, f) for d in (-2, -1, 0, 1, 2) for f in (0, 1) if (d, f) != (0, 0)]
+    partners = [(d, f) for d in (-2, 2, -1, 1, 0) for f in (1, 0) if (d, f) != (0, 0)]
     def partner(d, f):
         return device(d, g if f == 0 else 1 - g)
 
     barrier = pltpu.get_barrier_semaphore()
+    ring.greet(barrier)
     for d, f in partners:
         pl.semaphore_signal(barrier, inc=1, device_id=partner(d, f), device_id_type=MESH)
-    ring.greet(barrier)
     pl.semaphore_wait(barrier, len(partners) + 23)
 
     def send(src, dst, ssem, rsem, d, f):
@@ -277,7 +277,7 @@
             slope2[x, pl.ds(64 * y, 64), :] = slope
         return 0
 
-    lax.fori_loop(0, 18, mix, 0, unroll=3)
+    lax.fori_loop(0, 18, mix, 0, unroll=6)
 
     targets()
 
@@ -325,7 +325,7 @@
         total[:, pl.ds(0, 576)] += rows_dot(theirs, seen)
         return mixbias + mine[:64] + mine[64:]
 
-    mixbias = lax.fori_loop(0, 16, mix_grad, jnp.zeros((64, 128), F32), unroll=4)
+    mixbias = lax.fori_loop(0, 16, mix_grad, jnp.zeros((64, 128), F32), unroll=8)
 
     summing.begin()
 
@@ -387,33 +387,28 @@
         y_lo = lax.axis_index("grp")
         gx = lax.axis_index("gx")
         gy = lax.axis_index("gy")
-        self.z, self.x = gx // 4, gx % 4
-        self.y_hi, self.core = gy // 2, gy % 2
-        self.y_lo, self.gx, self.gy = y_lo, gx, gy
-        self.place = self.x * 4 + self.y_hi * 2 + y_lo
-        self.sibling = (y_lo, gx, self.y_hi * 2 + 1 - self.core)
-
-    def in_plane(self, other):
-        return (other % 2, self.z * 4 + other // 4, ((other // 2) % 2) * 2 + self.core)
-
-    def in_z(self, other):
-        return (self.y_lo, other * 4 + self.x, self.gy)
+        self.z, x = lax.div(gx, 4), lax.rem(gx, 4)
+        y_hi, core = lax.div(gy, 2), lax.rem(gy, 2)
+        self.core, self.place = core, x * 4 + y_hi * 2 + y_lo
+        self.sibling = (y_lo, gx, y_hi * 2 + 1 - core)
+
+        def along(at, size):
+            steps = [jnp.where(at + j >= size, at + j - size, at + j) for j in range(1, size)]
+            return [(0, at)] + [(min(j, size - j), step) for j, step in enumerate(steps, 1)]
+
+        plane = []
+        for far_x, to_x in along(x, 4):
+            for far_y, to_y in along(y_hi * 2 + y_lo, 4):
+                to = (lax.rem(to_y, 2), self.z * 4 + to_x, lax.div(to_y, 2) * 2 + core)
+                plane.append((far_x + far_y, to_x * 4 + to_y, to))
+        rows = [(far, to_z, (y_lo, to_z * 4 + x, gy)) for far, to_z in along(self.z, 8)]
+        self.plane = sorted(plane, key=lambda entry: -entry[0])[:-1]
+        self.rows = sorted(rows, key=lambda entry: -entry[0])[:-1]
 
     def greet(self, barrier):
+        for _, _, to in self.rows + self.plane:
+            pl.semaphore_signal(barrier, inc=1, device_id=to, device_id_type=MESH)
         pl.semaphore_signal(barrier, inc=1, device_id=self.sibling, device_id_type=MESH)
-
-        def greet_plane(j, _):
-            other = self.in_plane((self.place + j) % 16)
-            pl.semaphore_signal(barrier, inc=1, device_id=other, device_id_type=MESH)
-            return 0
-
-        def greet_z(j, _):
-            other = self.in_z((self.z + j) % 8)
-            pl.semaphore_signal(barrier, inc=1, device_id=other, device_id_type=MESH)
-            return 0
-
-        lax.fori_loop(1, 16, greet_plane, 0)
-        lax.fori_loop(1, 8, greet_z, 0)
 
 
 class Summing:
@@ -433,24 +428,13 @@
         self.swap.start()
 
     def spread_plane(self, source, target, pair):
-        ring = self.ring
-
-        def start(j, _):
-            other = lax.rem(ring.place + j, 16)
-            self.copy(source(other), target, pair, ring.in_plane(other)).start()
-            return 0
-
-        lax.fori_loop(1, 16, start, 0)
+        for _, other, to in self.ring.plane:
+            self.copy(source(other), target, pair, to).start()
 
     def spread_z(self, ref, pair):
-        ring = self.ring
-        own = ref.at[ring.z]
-
-        def start(j, _):
-            self.copy(own, own, pair, ring.in_z(lax.rem(ring.z + j, 8))).start()
-            return 0
-
-        lax.fori_loop(1, 8, start, 0)
+        own = ref.at[self.ring.z]
+        for _, _, to in self.ring.rows:
+            self.copy(own, own, pair, to).start()
 
     def finish(self, ref, first, count, pair):
         part = ref.at[pl.ds(first, count)]

time: 57.9 us -> 54.7 us (0.945)
  Pallas kernels: 56.1 us -> 52.9 us
    pallas_call x1, Pallas kernels: 55.2 us -> 52 us  [train(): pl.pallas_call(functools.partial(main_kernel, loss_scale), out_shape=jax....]
where the time goes in v6:
time: 54.7 us; the launch traced here: 54.6 us
  Pallas kernels  52.9 us (97%)
  local copies, waits for them, and re-layouts  1.03 us (2%)
  between operations  0.65 us (1%)
    pallas_call x1, Pallas kernels, train(): pl.pallas_call(functools.partial(main_kernel, loss_scale), out_shape=jax....  52 us

profile of v6, /device:TPU:1, one launch (start us, length us, event | category | flops | bytes accessed | tf_op | source)
XLA Modules:
  0.0 54.6 jit_solution(15295014656384976970)
XLA Ops:
  0.6 52.0 %train.1.out = f32[36,4,896]{2,1,0:T(4,128)} custom-call(f32[64,128]{1,0:T(8,128)} %bitcast.12, f32[192,128]{1,0:T(8,128)} %bitcast.11, bf16[64,1728]{1,0:T(8,128)(2,1)} %w_mix_hbm.1, bf16[1728,576]{1,0:T(8,128)(2,1)} %constant.8.clone.spread_hbm, bf16[54,64]{1,0:T(8,128)(2,1)} %bitcast.13, bf16[6,54,144]{2,1,0:T(8,128)(2,1)} %constant.9.clone.ahead_hbm, ...), custom_call_target="tpu_custom_call" | custom-call | tf_op jit(solution)/shard_map/train/pallas_call | solution.py:615
  52.6 0.0 copy-start
  52.6 1.0 %copy-done = f32[36,4,896]{2,1,0:T(4,128)S(1)} copy-done((f32[36,4,896]{2,1,0:T(4,128)S(1)}, f32[36,4,896]{2,1,0:T(4,128)}, u32[]{:S(2)}) %copy-start) | copy-done | bytes 516120
  53.7 0.9 %finish.1 = (f32[64,128]{1,0:T(8,128)}, f32[64,1728]{1,0:T(8,128)}, f32[54,64]{1,0:T(8,128)}, f32[1,64]{1,0:T(1,128)}, f32[1,64]{1,0:T(1,128)}, /*index=5*/f32[2,64]{1,0:T(2,128)}, f32[1,2]{1,0:T(1,128)}) custom-call(f32[36,4,896]{2,1,0:T(4,128)S(1)} %copy-done), custom_call_target="tpu_custom_call" | custom-call | tf_op jit(solution)/shard_map/finish/pallas_call | solution.py:646
Async XLA Ops:
  52.6 1.0 %copy-start = (f32[36,4,896]{2,1,0:T(4,128)S(1)}, f32[36,4,896]{2,1,0:T(4,128)}, u32[]{:S(2)}) copy-start(f32[36,4,896]{2,1,0:T(4,128)} %train.1.out) | copy-start | bytes 1548292

commit v7 on v6

--- a/solution.py
+++ b/solution.py
@@ -149,7 +149,7 @@
         tgt[pl.ds(33 * 8, 8), :] = jnp.zeros((8, 128), F32)
         for field in range(2):
             for yy in range(4):
-                tgt[pl.ds(8 + yy * 2 + field, 32, stride=8), :] = inc[4 * field + yy]
+                tgt[pl.ds(8 + (yy + 3) % 4 * 2 + field, 32, stride=8), :] = inc[4 * field + yy]
 
     return targets, (first_all, second_all, third_all, fourth_all)
 
@@ -269,37 +269,54 @@
             axis=1,
         )
 
-    def mix(x, _):
-        u = jnp.dot(prepared.mix[...], around(lifted, x, 0, 4), preferred_element_type=F32)
-        for y in range(4):
-            value, slope = gelu_parts(summed_z(u[:, 128 * y : 128 * y + 128]) + prepared.bias[1])
+    def mix(x, ys):
+        seen = jnp.concatenate([around(lifted, x, y, 1) for y in ys], axis=1)
+        u = jnp.dot(prepared.mix[...], seen, preferred_element_type=F32)
+        for j, y in enumerate(ys):
+            value, slope = gelu_parts(summed_z(u[:, 128 * j : 128 * j + 128]) + prepared.bias[1])
             mixed[x, pl.ds(64 * y, 64), :] = value.astype(BF16)
             slope2[x, pl.ds(64 * y, 64), :] = slope
+
+    def mix_own(x, _):
+        mix(x, (1, 2))
         return 0
 
-    lax.fori_loop(0, 18, mix, 0, unroll=6)
-
+    def mix_rim(x, _):
+        mix(x, (3, 0))
+        return 0
+
+    def compare(xs, ys):
+        width = 128 * len(xs)
+        part = 0 if ys == (1, 2) else 128
+        seen = jnp.concatenate(
+            [
+                jnp.concatenate([mixed[x, pl.ds(64 * y, 64), :] for y in ys], axis=0)
+                for x in xs
+            ],
+            axis=1,
+        )
+        row = lax.broadcasted_iota(jnp.int32, (16, width), 0)
+        bias = jnp.where(row % 2 == 0, prepared.b_out[:, 0:1], prepared.b_out[:, 1:2])
+        predicted = jnp.dot(prepared.out[:, part : part + 128], seen, preferred_element_type=F32) + bias
+        goal = jnp.concatenate(
+            [tgt[pl.ds(pl.multiple_of((x0 + x) * 8, 8), 8), :] for x in xs], axis=1
+        )
+        goal = jnp.concatenate([goal, jnp.zeros((8, width), F32)], axis=0)
+        error = (loss_scale * (predicted - goal)).astype(BF16)
+        back = jnp.dot(prepared.outt[part : part + 128, :], error, preferred_element_type=F32)
+        for j, x in enumerate(xs):
+            for row_at, y in enumerate(ys):
+                piece = back[64 * row_at : 64 * row_at + 64, 128 * j : 128 * j + 128]
+                cot[x, pl.ds(64 * y, 64), :] = (piece * slope2[x, pl.ds(64 * y, 64), :]).astype(BF16)
+        return error
+
+    lax.fori_loop(1, 17, mix_own, 0, unroll=8)
     targets()
-
-    def compare(batch, _):
-        first = 6 * batch
-        seen = jnp.concatenate([mixed[first + j] for j in range(6)], axis=1)
-        row = lax.broadcasted_iota(jnp.int32, (16, 768), 0)
-        bias = jnp.where(row % 2 == 0, prepared.b_out[:, 0:1], prepared.b_out[:, 1:2])
-        predicted = jnp.dot(prepared.out[...], seen, preferred_element_type=F32) + bias
-        goal = jnp.concatenate(
-            [tgt[pl.ds(pl.multiple_of((x0 + first + j) * 8, 8), 8), :] for j in range(6)], axis=1
-        )
-        goal = jnp.concatenate([goal, jnp.zeros((8, 768), F32)], axis=0)
-        error = (loss_scale * (predicted - goal)).astype(BF16)
-        back = jnp.dot(prepared.outt[...], error, preferred_element_type=F32)
-        for j in range(6):
-            cot[first + j] = (back[:, 128 * j : 128 * j + 128] * slope2[first + j]).astype(BF16)
-            errors[first + j] = error[:, 128 * j : 128 * j + 128]
-        return 0
-
-    lax.fori_loop(0, 3, compare, 0, unroll=3)
-    clear(cot, (0,), (17,), pl.ds(0, 64), pl.ds(192, 64))
+    for batch in range(2):
+        xs = range(1 + 8 * batch, 9 + 8 * batch)
+        error = compare(xs, (1, 2))
+        for j, x in enumerate(xs):
+            errors[x] = error[:, 128 * j : 128 * j + 128]
     total[...] = jnp.zeros_like(total)
 
     def mix_grad(x, mixbias):
@@ -328,6 +345,15 @@
     mixbias = lax.fori_loop(0, 16, mix_grad, jnp.zeros((64, 128), F32), unroll=8)
 
     summing.begin()
+    lax.fori_loop(1, 9, mix_rim, 0, unroll=8)
+    summing.plane()
+    lax.fori_loop(9, 17, mix_rim, 0, unroll=8)
+    for x in (0, 17):
+        mix(x, (1, 2, 3, 0))
+    compare((0, 17), (1, 2))
+    compare(range(0, 9), (3, 0))
+    compare(range(9, 18), (3, 0))
+    clear(cot, (0,), (17,), pl.ds(0, 64), pl.ds(192, 64))
 
     def backward(x, _):
         u = jnp.dot(prepared.back[...], around(cot, x, 0, 2), preferred_element_type=F32)
@@ -335,9 +361,8 @@
         down[x] = (back * slope1[x + 2]).astype(BF16)
         return 0
 
-    lax.fori_loop(0, 8, backward, 0, unroll=4)
-    summing.plane()
-    lax.fori_loop(8, 16, backward, 0, unroll=4)
+    lax.fori_loop(0, 16, backward, 0, unroll=8)
+    summing.along_z()
 
     liftbias = jnp.zeros((64, 128), F32)
     outbias = jnp.zeros((8, 128), F32)
@@ -370,15 +395,15 @@
     small = jnp.where(lane == 54, jnp.sum(liftbias, axis=1, keepdims=True), small)
     small = jnp.where(lane == 55, jnp.sum(mixbias, axis=1, keepdims=True), small)
     for k in range(2):
-        piece = out_total[:64, 2 + k : 3 + k] + out_total[64:, 4 + k : 5 + k]
+        piece = out_total[:64, k : k + 1] + out_total[64:, 2 + k : 3 + k]
         small = jnp.where(lane == 56 + k, piece, small)
     per_row = jnp.sum(outbias, axis=1, keepdims=True)
-    pair = per_row[2:4] + per_row[4:6]
+    pair = per_row[0:2] + per_row[2:4]
     for k in range(2):
         small = jnp.where((lane == 58) & (row == k), pair[k : k + 1], small)
     small = jnp.concatenate([small[:32, :64], small[32:, :64]], axis=1)
-    for c in range(16):
-        small_buf[c] = small[2 * c : 2 * c + 2]
+    for half in range(2):
+        small_buf[half] = small[16 * half : 16 * half + 16]
     summing.small_plane()
 
 
@@ -412,7 +437,7 @@
 
 
 class Summing:
-    def __init__(self, ring, total, unspread, out, from_core, mine, from_plane, from_z, small, s_plane, s_z, s_out, s_core, sems):
+    def __init__(self, ring, total, unspread, out, from_core, mine, from_plane, from_z, small, s_mine, s_plane, s_z, s_out, s_core, sems):
         self.__dict__.update(locals())
         self.ours = pl.multiple_of(ring.core * 16, 16)
 
@@ -460,47 +485,50 @@
         self.from_plane[place] = mine[place]
 
     def small_plane(self):
-        place = self.ring.place
-        self.spread_plane(lambda other: self.small.at[other], self.s_plane.at[place], 2)
-        self.s_plane[place] = self.small[place]
+        place, core = self.ring.place, self.ring.core
+        swap = self.copy(self.small.at[1 - core], self.s_core, 8, self.ring.sibling)
+        swap.start()
+        swap.wait()
+        self.s_mine[...] = self.small[core] + self.s_core[...]
+        self.spread_plane(lambda other: self.s_mine, self.s_plane.at[place], 2)
+        self.s_plane[place] = self.s_mine[...]
+
+    def added(self, ref, count):
+        value = ref[0]
+        for j in range(1, count):
+            value = value + ref[j]
+        return value
+
+    def along_z(self):
+        self.finish(self.from_plane, 0, 15, 1)
+        self.from_z[self.ring.z] = self.added(self.from_plane, 16)
+        self.spread_z(self.from_z, 3)
 
     def rest(self):
         place, z = self.ring.place, self.ring.z
-
-        def total(ref, count):
-            value = ref[0]
-            for j in range(1, count):
-                value = value + ref[j]
-            return value
-
-        self.finish(self.from_plane, 0, 15, 1)
-        self.from_z[z] = total(self.from_plane, 16)
-        self.spread_z(self.from_z, 3)
-        self.finish(self.s_plane, 0, 15, 2)
-        self.s_z[z] = total(self.s_plane, 16)
-        self.spread_z(self.s_z, 4)
-
         self.finish(self.from_z, 0, 7, 3)
         own = self.out.at[self.ours + place]
-        self.out[self.ours + place] = total(self.from_z, 8)
+        self.out[self.ours + place] = self.added(self.from_z, 8)
         self.spread_plane(lambda other: own, own, 5)
-        self.finish(self.s_z, 0, 7, 4)
-        small = self.s_out.at[place]
-        self.s_out[place] = total(self.s_z, 8)
-        self.spread_plane(lambda other: small, small, 6)
+        self.finish(self.s_plane, 0, 15, 2)
+        self.s_z[z] = self.added(self.s_plane, 16)
+        self.spread_z(self.s_z, 4)
 
         self.finish(self.out, 0, 15, 5)
         half = self.out.at[pl.ds(self.ours, 16)]
         hand = self.copy(half, half, 7, self.ring.sibling)
         hand.start()
-        self.finish(self.s_out, 0, 15, 6)
-        swap = self.copy(self.s_out, self.s_core, 8, self.ring.sibling)
-        swap.start()
-        swap.wait()
-        both = self.s_out[...] + self.s_core[...]
-        for c in range(16):
-            at = 16 + c // 2
-            self.out[32 + at // 7, pl.ds(2 * (c % 2), 2), pl.ds(128 * (at % 7), 128)] = both[c]
+        self.finish(self.s_z, 0, 7, 4)
+        core = self.ring.core
+        self.s_out[core] = self.added(self.s_z, 8)
+        part = self.s_out.at[core]
+        give = self.copy(part, part, 6, self.ring.sibling)
+        give.start()
+        give.wait()
+        for block in range(8):
+            at = 16 + block
+            rows = self.s_out[block // 4, pl.ds(4 * (block % 4), 4), :]
+            self.out[32 + at // 7, :, pl.ds(128 * (at % 7), 128)] = rows
         hand.wait()
 
 
@@ -528,7 +556,7 @@
     load, lift_w, mix_w, back_w, out_w, outt_w, bias,
     net, tgt, halo, held, wide, seen, inc, gains,
     v3, lifted, slope1, mixed, slope2, cot, down, errors, total,
-    from_core, mine, from_plane, from_z, small, s_plane, s_z, s_out, s_core,
+    from_core, mine, from_plane, from_z, small, s_mine, s_plane, s_z, s_out, s_core,
     a_send, a_recv, b_send, b_recv, n_send, n_recv, c_send, c_recv, sums,
 ):
     pairs = (
@@ -564,7 +592,7 @@
     for copy in loads[10:]:
         copy.wait()
     summing = Summing(
-        ring, total, unspread, out, from_core, mine, from_plane, from_z, small, s_plane, s_z, s_out, s_core, sums
+        ring, total, unspread, out, from_core, mine, from_plane, from_z, small, s_mine, s_plane, s_z, s_out, s_core, sums
     )
     network(
         loss_scale, targets, summing, net, tgt, prepared, pick,
@@ -631,7 +659,7 @@
             vmem(18, 256, 128, dtype=BF16), vmem(18, 256, 128), vmem(18, 256, 128, dtype=BF16),
             vmem(16, 128, 128, dtype=BF16), vmem(18, 16, 128, dtype=BF16), vmem(192, 640),
             vmem(96, 640), vmem(16, *chunk), vmem(16, *chunk), vmem(8, *chunk),
-            vmem(16, 2, 128), vmem(16, 2, 128), vmem(8, 2, 128), vmem(16, 2, 128), vmem(16, 2, 128),
+            vmem(2, 16, 128), vmem(16, 128), vmem(16, 16, 128), vmem(8, 16, 128), vmem(2, 16, 128), vmem(16, 128),
             dma, dma, dma, dma, dma, dma, dma, dma, dma((18,)),
         ],
         compiler_params=pltpu.CompilerParams(

time: 54.7 us -> 53.6 us (0.980)
  Pallas kernels: 52.9 us -> 51.8 us
    pallas_call x1, Pallas kernels: 52 us -> 50.9 us  [train(): pl.pallas_call(functools.partial(main_kernel, loss_scale), out_shape=jax....]
where the time goes in v7:
time: 53.6 us; the launch traced here: 53.4 us
  Pallas kernels  51.8 us (97%)
  local copies, waits for them, and re-layouts  1.03 us (2%)
  between operations  0.65 us (1%)
    pallas_call x1, Pallas kernels, train(): pl.pallas_call(functools.partial(main_kernel, loss_scale), out_shape=jax....  50.9 us

profile of v7, /device:TPU:1, one launch (start us, length us, event | category | flops | bytes accessed | tf_op | source)
XLA Modules:
  0.0 53.4 jit_solution(3571007952030772945)
XLA Ops:
  0.6 50.9 %train.1.out = f32[36,4,896]{2,1,0:T(4,128)} custom-call(f32[64,128]{1,0:T(8,128)} %bitcast.12, f32[192,128]{1,0:T(8,128)} %bitcast.11, bf16[64,1728]{1,0:T(8,128)(2,1)} %w_mix_hbm.1, bf16[1728,576]{1,0:T(8,128)(2,1)} %constant.8.clone.spread_hbm, bf16[54,64]{1,0:T(8,128)(2,1)} %bitcast.13, bf16[6,54,144]{2,1,0:T(8,128)(2,1)} %constant.9.clone.ahead_hbm, ...), custom_call_target="tpu_custom_call" | custom-call | tf_op jit(solution)/shard_map/train/pallas_call | solution.py:643
  51.5 0.0 copy-start
  51.5 1.0 %copy-done = f32[36,4,896]{2,1,0:T(4,128)S(1)} copy-done((f32[36,4,896]{2,1,0:T(4,128)S(1)}, f32[36,4,896]{2,1,0:T(4,128)}, u32[]{:S(2)}) %copy-start) | copy-done | bytes 516120
  52.5 0.9 %finish.1 = (f32[64,128]{1,0:T(8,128)}, f32[64,1728]{1,0:T(8,128)}, f32[54,64]{1,0:T(8,128)}, f32[1,64]{1,0:T(1,128)}, f32[1,64]{1,0:T(1,128)}, /*index=5*/f32[2,64]{1,0:T(2,128)}, f32[1,2]{1,0:T(1,128)}) custom-call(f32[36,4,896]{2,1,0:T(4,128)S(1)} %copy-done), custom_call_target="tpu_custom_call" | custom-call | tf_op jit(solution)/shard_map/finish/pallas_call | solution.py:674
Async XLA Ops:
  51.5 1.0 %copy-start = (f32[36,4,896]{2,1,0:T(4,128)S(1)}, f32[36,4,896]{2,1,0:T(4,128)}, u32[]{:S(2)}) copy-start(f32[36,4,896]{2,1,0:T(4,128)} %train.1.out) | copy-start | bytes 1548292

commit v8 on v7

--- a/solution.py
+++ b/solution.py
@@ -401,9 +401,7 @@
     pair = per_row[0:2] + per_row[2:4]
     for k in range(2):
         small = jnp.where((lane == 58) & (row == k), pair[k : k + 1], small)
-    small = jnp.concatenate([small[:32, :64], small[32:, :64]], axis=1)
-    for half in range(2):
-        small_buf[half] = small[16 * half : 16 * half + 16]
+    small_buf[...] = jnp.concatenate([small[:32, :64], small[32:, :64]], axis=1)
     summing.small_plane()
 
 
@@ -437,7 +435,7 @@
 
 
 class Summing:
-    def __init__(self, ring, total, unspread, out, from_core, mine, from_plane, from_z, small, s_mine, s_plane, s_z, s_out, s_core, sems):
+    def __init__(self, ring, total, unspread, out, from_core, mine, from_plane, from_z, small, s_mine, s_plane, s_z, s_core, sems):
         self.__dict__.update(locals())
         self.ours = pl.multiple_of(ring.core * 16, 16)
 
@@ -485,11 +483,11 @@
         self.from_plane[place] = mine[place]
 
     def small_plane(self):
-        place, core = self.ring.place, self.ring.core
-        swap = self.copy(self.small.at[1 - core], self.s_core, 8, self.ring.sibling)
+        place = self.ring.place
+        swap = self.copy(self.small, self.s_core, 8, self.ring.sibling)
         swap.start()
         swap.wait()
-        self.s_mine[...] = self.small[core] + self.s_core[...]
+        self.s_mine[...] = self.small[...] + self.s_core[...]
         self.spread_plane(lambda other: self.s_mine, self.s_plane.at[place], 2)
         self.s_plane[place] = self.s_mine[...]
 
@@ -519,16 +517,10 @@
         hand = self.copy(half, half, 7, self.ring.sibling)
         hand.start()
         self.finish(self.s_z, 0, 7, 4)
-        core = self.ring.core
-        self.s_out[core] = self.added(self.s_z, 8)
-        part = self.s_out.at[core]
-        give = self.copy(part, part, 6, self.ring.sibling)
-        give.start()
-        give.wait()
+        both = self.added(self.s_z, 8)
         for block in range(8):
             at = 16 + block
-            rows = self.s_out[block // 4, pl.ds(4 * (block % 4), 4), :]
-            self.out[32 + at // 7, :, pl.ds(128 * (at % 7), 128)] = rows
+            self.out[32 + at // 7, :, pl.ds(128 * (at % 7), 128)] = both[4 * block : 4 * block + 4]
         hand.wait()
 
 
@@ -556,7 +548,7 @@
     load, lift_w, mix_w, back_w, out_w, outt_w, bias,
     net, tgt, halo, held, wide, seen, inc, gains,
     v3, lifted, slope1, mixed, slope2, cot, down, errors, total,
-    from_core, mine, from_plane, from_z, small, s_mine, s_plane, s_z, s_out, s_core,
+    from_core, mine, from_plane, from_z, small, s_mine, s_plane, s_z, s_core,
     a_send, a_recv, b_send, b_recv, n_send, n_recv, c_send, c_recv, sums,
 ):
     pairs = (
@@ -592,7 +584,7 @@
     for copy in loads[10:]:
         copy.wait()
     summing = Summing(
-        ring, total, unspread, out, from_core, mine, from_plane, from_z, small, s_mine, s_plane, s_z, s_out, s_core, sums
+        ring, total, unspread, out, from_core, mine, from_plane, from_z, small, s_mine, s_plane, s_z, s_core, sums
     )
     network(
         loss_scale, targets, summing, net, tgt, prepared, pick,
@@ -659,7 +651,7 @@
             vmem(18, 256, 128, dtype=BF16), vmem(18, 256, 128), vmem(18, 256, 128, dtype=BF16),
             vmem(16, 128, 128, dtype=BF16), vmem(18, 16, 128, dtype=BF16), vmem(192, 640),
             vmem(96, 640), vmem(16, *chunk), vmem(16, *chunk), vmem(8, *chunk),
-            vmem(2, 16, 128), vmem(16, 128), vmem(16, 16, 128), vmem(8, 16, 128), vmem(2, 16, 128), vmem(16, 128),
+            vmem(32, 128), vmem(32, 128), vmem(16, 32, 128), vmem(8, 32, 128), vmem(32, 128),
             dma, dma, dma, dma, dma, dma, dma, dma, dma((18,)),
         ],
         compiler_params=pltpu.CompilerParams(

time: 53.6 us -> 53.4 us (level)
  no operation moved by 1% of the time
where the time goes in v8:
time: 53.4 us; the launch traced here: 53.1 us
  Pallas kernels  51.4 us (96%)
  local copies, waits for them, and re-layouts  1.03 us (2%)
  between operations  0.65 us (1%)
    pallas_call x1, Pallas kernels, train(): pl.pallas_call(functools.partial(main_kernel, loss_scale), out_shape=jax....  50.5 us

profile of v8, /device:TPU:1, one launch (start us, length us, event | category | flops | bytes accessed | tf_op | source)
XLA Modules:
  0.0 53.1 jit_solution(9362126540268845090)
XLA Ops:
  0.6 50.5 %train.1.out = f32[36,4,896]{2,1,0:T(4,128)} custom-call(f32[64,128]{1,0:T(8,128)} %bitcast.12, f32[192,128]{1,0:T(8,128)} %bitcast.11, bf16[64,1728]{1,0:T(8,128)(2,1)} %w_mix_hbm.1, bf16[1728,576]{1,0:T(8,128)(2,1)} %constant.8.clone.spread_hbm, bf16[54,64]{1,0:T(8,128)(2,1)} %bitcast.13, bf16[6,54,144]{2,1,0:T(8,128)(2,1)} %constant.9.clone.ahead_hbm, ...), custom_call_target="tpu_custom_call" | custom-call | tf_op jit(solution)/shard_map/train/pallas_call | solution.py:635
  51.1 0.0 copy-start
  51.1 1.0 %copy-done = f32[36,4,896]{2,1,0:T(4,128)S(1)} copy-done((f32[36,4,896]{2,1,0:T(4,128)S(1)}, f32[36,4,896]{2,1,0:T(4,128)}, u32[]{:S(2)}) %copy-start) | copy-done | bytes 516120
  52.2 0.9 %finish.1 = (f32[64,128]{1,0:T(8,128)}, f32[64,1728]{1,0:T(8,128)}, f32[54,64]{1,0:T(8,128)}, f32[1,64]{1,0:T(1,128)}, f32[1,64]{1,0:T(1,128)}, /*index=5*/f32[2,64]{1,0:T(2,128)}, f32[1,2]{1,0:T(1,128)}) custom-call(f32[36,4,896]{2,1,0:T(4,128)S(1)} %copy-done), custom_call_target="tpu_custom_call" | custom-call | tf_op jit(solution)/shard_map/finish/pallas_call | solution.py:666
Async XLA Ops:
  51.1 1.0 %copy-start = (f32[36,4,896]{2,1,0:T(4,128)S(1)}, f32[36,4,896]{2,1,0:T(4,128)}, u32[]{:S(2)}) copy-start(f32[36,4,896]{2,1,0:T(4,128)} %train.1.out) | copy-start | bytes 1548292
